TPU v7x, 512 devices: a whole 4x8x8 slice. The times are simulated.
512 devices in a mesh: gx: 16 (over y, core), gy: 32 (over z, x).
Axes of the slice: x: 4, y: 8, z: 8, core: 2. Of those that a mesh axis runs over, the one named last changes fastest.
Arguments:
- fine_nodes: bfloat16 [262144, 512], P(('gx', 'gy')), may hold values from -6 to 6
- fine_edges: bfloat16 [524288, 512], P(('gx', 'gy')), may hold values from -6 to 6
- edge_src: int32 [524288], P(('gx', 'gy')), may hold values from 0 to 767
- edge_dst: int32 [524288], P(('gx', 'gy')), may hold values from 0 to 511
- send_rows: int32 [512, 8, 32], P(('gx', 'gy')), may hold values from 0 to 512, as said below
- parents: int32 [262144], P(('gx', 'gy')), may hold values from 0 to 255
- coarse_src: int32 [32768], P('gy'), may hold values from 0 to 767
- coarse_dst: int32 [32768], P('gy'), may hold values from 0 to 255
- w_edge_in: bfloat16 [1536, 512], replicated, may hold values from -0.15625 to 0.15625
- w_edge_out: bfloat16 [512, 512], replicated, may hold values from -0.25 to 0.25
- edge_gain: float32 [512], replicated, may hold values from 0.1 to 1.9
- w_node_in: bfloat16 [1024, 512], replicated, may hold values from -0.1875 to 0.1875
- w_node_out: bfloat16 [512, 512], replicated, may hold values from -0.25 to 0.25
- node_gain: float32 [512], replicated, may hold values from 0.1 to 1.9
- w_cedge_in: bfloat16 [1024, 512], replicated, may hold values from -0.1875 to 0.1875
- w_cedge_out: bfloat16 [512, 512], replicated, may hold values from -0.25 to 0.25
- w_cnode_in: bfloat16 [1024, 512], replicated, may hold values from -0.1875 to 0.1875
- w_cnode_out: bfloat16 [512, 512], replicated, may hold values from -0.25 to 0.25
- coarse_gain: float32 [512], replicated, may hold values from 0.1 to 1.9
- w_up_in: bfloat16 [1024, 512], replicated, may hold values from -0.1875 to 0.1875
- w_up_out: bfloat16 [512, 512], replicated, may hold values from -0.25 to 0.25
- up_gain: float32 [512], replicated, may hold values from 0.1 to 1.9
Outputs:
- fine_out: bfloat16 [262144, 512], P(('gx', 'gy'))
- edges_out: bfloat16 [524288, 512], P(('gx', 'gy'))
Inputs may be any that keep to these rules, and one draw needn't show every extreme that they name: `send_rows`: entries below 512 are local rows of the sending partition; 512 marks an empty slot; in each list the live entries come first, at least one is live, and some list is full.
All inputs are finite; a program needn't handle non-finite values.
Results may differ from a plain program's by a relative error of at most 0.015.
Values may be sent and summed in bfloat16 or wider, within the bound.
No kernel may reach another device: no remote copies, remote signals or barrier semaphores. Data moves between devices by JAX's collectives and lax.ppermute only.
A program may use at most 64 MiB of HBM per device.

v0:
```python
import jax
import jax.numpy as jnp
from jax import lax
from jax.sharding import PartitionSpec as P

COARSE = 256


OFFSETS = ((-1, -1), (-1, 0), (-1, 1), (0, -1), (0, 1), (1, -1), (1, 0), (1, 1))


def extended_2(array, sides, width):
    for axis, dim in sides:
        peers, length = (lax.axis_size(axis), array.shape[dim])
        up = [(i, (i + 1) % peers) for i in range(peers - 1)]
        down = [(j, i) for i, j in up]
        last = lax.slice_in_dim(array, length - width, length, axis=dim)
        first = lax.slice_in_dim(array, 0, width, axis=dim)
        before = lax.ppermute(last, axis, up)
        after = lax.ppermute(first, axis, down)
        array = jnp.concatenate([before, array, after], axis=dim)
    return array


def layer_norm(values):
    mean = jnp.mean(values, axis=-1, keepdims=True)
    centred = values - mean
    spread = jnp.mean(centred * centred, axis=-1, keepdims=True)
    return centred * lax.rsqrt(spread + 1e-05)


def mlp_tail(pre, w_out, gain):
    act = jax.nn.silu(pre).astype(jnp.bfloat16)
    return layer_norm(jnp.dot(act, w_out, preferred_element_type=jnp.float32)) * gain


def frame_column(side_src):
    return extended_2(side_src, (("gy", 0),), side_src.shape[0])


def coarse_messages(extended, side_dst, src_idx, dst_idx, w_cedge_out):
    act = jax.nn.silu(
        extended[src_idx].astype(jnp.float32) + side_dst[dst_idx].astype(jnp.float32)
    ).astype(jnp.bfloat16)
    msg = layer_norm(jnp.dot(act, w_cedge_out, preferred_element_type=jnp.float32))
    return jax.ops.segment_sum(msg, dst_idx, num_segments=side_dst.shape[0])


def coarse_update(coarse_zero, coarse_sum, w_cnode_in, w_cnode_out, coarse_gain):
    width = coarse_zero.shape[1]
    cpre = jnp.dot(coarse_zero, w_cnode_in[:width], preferred_element_type=jnp.float32)
    cpre = cpre + jnp.dot(coarse_sum, w_cnode_in[width:], preferred_element_type=jnp.float32)
    return (coarse_zero.astype(jnp.float32) + mlp_tail(cpre, w_cnode_out, coarse_gain)).astype(
        jnp.bfloat16
    )


def per_device(
    fine_nodes,
    fine_edges,
    edge_src,
    edge_dst,
    send_rows,
    parents,
    coarse_src,
    coarse_dst,
    w_edge_in,
    w_edge_out,
    edge_gain,
    w_node_in,
    w_node_out,
    node_gain,
    w_cedge_in,
    w_cedge_out,
    w_cnode_in,
    w_cnode_out,
    coarse_gain,
    w_up_in,
    w_up_out,
    up_gain,
):
    width = fine_nodes.shape[1]
    rows = fine_nodes.shape[0]
    src_proj = jnp.dot(
        fine_nodes, w_edge_in[width : 2 * width], preferred_element_type=jnp.float32
    ).astype(jnp.bfloat16)
    dst_proj = jnp.dot(
        fine_nodes, w_edge_in[2 * width :], preferred_element_type=jnp.float32
    ).astype(jnp.bfloat16)
    padded = jnp.concatenate([src_proj, jnp.zeros((1, width), jnp.bfloat16)], 0)
    lists = send_rows[0]
    outgoing = padded[lists]
    slots = lists.shape[1]
    count_x = lax.axis_size("gx")
    place_x = lax.axis_index("gx")
    blank = jnp.zeros((1, slots, width), jnp.bfloat16)
    grid = jnp.concatenate([outgoing[:4], blank, outgoing[4:]], 0).reshape(3, 3, slots, width)
    framed = extended_2(grid, (("gx", 0), ("gy", 1)), 1)
    received = jnp.stack([framed[2 - 2 * step_x, 2 - 2 * step_y] for step_x, step_y in OFFSETS])
    table = jnp.concatenate([src_proj, received.reshape(-1, width)], 0)
    pre = jnp.dot(fine_edges, w_edge_in[:width], preferred_element_type=jnp.float32)
    pre = pre + table[edge_src].astype(jnp.float32) + dst_proj[edge_dst].astype(jnp.float32)
    message = mlp_tail(pre, w_edge_out, edge_gain)
    edges_out = (fine_edges.astype(jnp.float32) + message).astype(jnp.bfloat16)
    summed = jax.ops.segment_sum(message, edge_dst, num_segments=rows).astype(jnp.bfloat16)
    node_pre = jnp.dot(fine_nodes, w_node_in[:width], preferred_element_type=jnp.float32)
    node_pre = node_pre + jnp.dot(summed, w_node_in[width:], preferred_element_type=jnp.float32)
    level_one = (fine_nodes.astype(jnp.float32) + mlp_tail(node_pre, w_node_out, node_gain)).astype(
        jnp.bfloat16
    )
    labels = jnp.arange(COARSE, dtype=jnp.int32)
    onehot = (parents[:, None] == labels[None, :]).astype(jnp.bfloat16)
    partial_value = jnp.dot(onehot.T, level_one, preferred_element_type=jnp.float32)
    share = lax.psum_scatter(
        partial_value.astype(jnp.bfloat16), "gx", scatter_dimension=0, tiled=True
    ).astype(jnp.float32)
    zero_share = layer_norm(share).astype(jnp.bfloat16)
    src_share = jnp.dot(zero_share, w_cedge_in[:width], preferred_element_type=jnp.float32).astype(
        jnp.bfloat16
    )
    dst_share = jnp.dot(zero_share, w_cedge_in[width:], preferred_element_type=jnp.float32).astype(
        jnp.bfloat16
    )
    side_src, side_dst = (
        lax.all_gather(src_share, "gx", axis=0, tiled=True),
        lax.all_gather(dst_share, "gx", axis=0, tiled=True),
    )
    extended = frame_column(side_src)
    count = coarse_src.shape[0] // count_x
    mine_src = lax.dynamic_slice_in_dim(coarse_src, place_x * count, count)
    mine_dst = lax.dynamic_slice_in_dim(coarse_dst, place_x * count, count)
    coarse_part = coarse_messages(extended, side_dst, mine_src, mine_dst, w_cedge_out)
    sum_share = lax.psum_scatter(
        coarse_part.astype(jnp.bfloat16), "gx", scatter_dimension=0, tiled=True
    )
    one_share = coarse_update(zero_share, sum_share, w_cnode_in, w_cnode_out, coarse_gain)
    coarse_one = lax.all_gather(one_share, "gx", axis=0, tiled=True)
    lifted = jnp.dot(onehot, coarse_one, preferred_element_type=jnp.float32).astype(jnp.bfloat16)
    upre = jnp.dot(level_one, w_up_in[:width], preferred_element_type=jnp.float32)
    upre = upre + jnp.dot(lifted, w_up_in[width:], preferred_element_type=jnp.float32)
    fine_out = (level_one.astype(jnp.float32) + mlp_tail(upre, w_up_out, up_gain)).astype(
        jnp.bfloat16
    )
    return (fine_out, edges_out)


def solution(mesh):
    return jax.shard_map(
        per_device,
        mesh=mesh,
        in_specs=(
            P(("gx", "gy"), None),
            P(("gx", "gy"), None),
            P(("gx", "gy")),
            P(("gx", "gy")),
            P(("gx", "gy"), None, None),
            P(("gx", "gy")),
            P("gy"),
            P("gy"),
            P(),
            P(),
            P(),
            P(),
            P(),
            P(),
            P(),
            P(),
            P(),
            P(),
            P(),
            P(),
            P(),
            P(),
        ),
        out_specs=(P(("gx", "gy"), None), P(("gx", "gy"), None)),
        check_vma=False,
    )
```

profile of v0, /device:TPU:1, one launch (start us, length us, event | category | flops | bytes accessed | tf_op | source)
XLA Modules:
  0.0 265.8 jit_solution(7965018102377693784)
XLA Ops:
  8.1 1.6 convolution_convert_fusion.1
  11.6 4.6 %collective-permute-start = (bf16[1,3,32,512]{3,2,1,0:T(8,128)(2,1)}, bf16[1,3,32,512]{3,2,1,0:T(8,128)(2,1)S(1)}, u32[]{:S(2)}, u32[]{:S(2)}) collective-permute-start(bf16[1,3,32,512]{3,2,1,0:T(8,128)(2,1)} %bitcast.1), channel_id=1, source_target_pairs={{0,32},{32,64},{64,96},{96,128},{128,160},{160,192},{192,224},{224... | collective-permute-start | bytes 294920 | tf_op jit(solution)/shard_map/ppermute | solution.py:19
  16.2 5.5 %collective-permute-start.1 = (bf16[1,3,32,512]{3,2,1,0:T(8,128)(2,1)}, bf16[1,3,32,512]{3,2,1,0:T(8,128)(2,1)}, u32[]{:S(2)}, u32[]{:S(2)}) collective-permute-start(bf16[1,3,32,512]{3,2,1,0:T(8,128)(2,1)} %bitcast.5), channel_id=1, source_target_pairs={{32,0},{64,32},{96,64},{128,96},{160,128},{192,160},{224,192},{256... | collective-permute-start | bytes 294920 | tf_op jit(solution)/shard_map/ppermute | solution.py:20
  21.7 1.5 convolution_convert_fusion
  23.6 2.3 copy.30
  25.9 5.1 %gather_fusion.2 = bf16[1024,512]{1,0:T(8,128)(2,1)} fusion(bf16[512,512]{1,0:T(8,128)(2,1)S(1)} %convolution_convert_fusion, s32[1024]{0:T(1024)S(1)} %get-tuple-element.27), kind=kCustom, calls=%fused_computation.2 | custom fusion | bytes 2101248 | tf_op jit(solution)/shard_map/gather | solution.py:102
  33.1 2.5 fusion.23
  35.6 4.0 %collective-permute-start.3 = (bf16[5,1,32,512]{3,2,1,0:T(8,128)(2,1)S(1)}, bf16[5,1,32,512]{3,2,1,0:T(8,128)(2,1)S(1)}, u32[]{:S(2)}, u32[]{:S(2)}) collective-permute-start(bf16[5,1,32,512]{3,2,1,0:T(8,128)(2,1)S(1)} %get-tuple-element.10), channel_id=1, source_target_pairs={{0,1},{1,2},{2,3},{3,4},{4,5},{5,6},{6,7},{7,8},{8,9},{9,10},{10,1... | collective-permute-start | bytes 491528 | tf_op jit(solution)/shard_map/ppermute | solution.py:19
  40.4 3.0 %collective-permute-done.3 = bf16[5,1,32,512]{3,2,1,0:T(8,128)(2,1)S(1)} collective-permute-done((bf16[5,1,32,512]{3,2,1,0:T(8,128)(2,1)S(1)}, bf16[5,1,32,512]{3,2,1,0:T(8,128)(2,1)S(1)}, u32[]{:S(2)}, u32[]{:S(2)}) %collective-permute-start.3) | collective-permute-done | bytes 163872 | tf_op jit(solution)/shard_map/ppermute | solution.py:19
  43.5 5.1 %gather_fusion.1 = bf16[1024,512]{1,0:T(8,128)(2,1)} fusion(bf16[768,512]{1,0:T(8,128)(2,1)S(1)} %pad_maximum_fusion, s32[1024]{0:T(1024)S(1)} %get-tuple-element.26), kind=kCustom, calls=%fused_computation.1 | custom fusion | bytes 2101248 | tf_op jit(solution)/shard_map/gather | solution.py:102
  48.6 3.6 %fusion.66 = (f32[1024]{0:T(1024)S(1)}, f32[1024,512]{0,1:T(8,128)S(1)}) fusion(bf16[512,512]{1,0:T(8,128)(2,1)S(1)} %copy-done, bf16[1024,512]{1,0:T(8,128)(2,1)} %gather_fusion.2, bf16[1024,512]{1,0:T(8,128)(2,1)} %gather_fusion.1, bf16[1024,512]{1,0:T(8,128)(2,1)} %param.23, bf16[1536,512]{1,0:T(8,128)(2,1)} %param.30), kind=kOutput, calls=%fused_computation.122 | convolution fusion | flops 1078983680 | bytes 6295552 | tf_op jit(solution)/shard_map/dot_general | solution.py:34
  53.5 2.1 add_convert_fusion
  55.6 1.9 copy.29
  57.5 7.6 %scatter_custom_fusion = f32[512,512]{1,0:T(8,128)} fusion(s32[1024]{0:T(1024)S(1)} %copy-done.9, f32[1024,512]{1,0:T(8,128)S(1)} %copy.29, f32[]{:T(128)} %constant.19.clone.1), kind=kCustom, calls=%fused_computation.47 | custom fusion | flops 524288 | bytes 1048580 | tf_op jit(solution)/shard_map/scatter-add | solution.py:105
  65.1 2.8 %fusion.69 = (f32[512]{0:T(512)S(1)}, f32[512,512]{0,1:T(8,128)S(1)}) fusion(bf16[512,512]{1,0:T(8,128)(2,1)} %param.34, f32[512,512]{1,0:T(8,128)} %fusion.23, bf16[1024,512]{1,0:T(8,128)(2,1)} %param.33, f32[512,512]{1,0:T(8,128)} %scatter_custom_fusion), kind=kOutput, calls=%fused_computation.123 | convolution fusion | flops 538967552 | bytes 4196352 | tf_op jit(solution)/shard_map/dot_general | solution.py:34
  71.4 60.0 %reduce-scatter.3.cloned.1.call-done = bf16[16,512]{1,0:T(8,128)(2,1)} async-done(((bf16[256,512]{1,0:T(8,128)(2,1)}), bf16[16,512]{1,0:T(8,128)(2,1)}) %reduce-scatter.3.cloned.1.call-update) | async-done | bytes 16400 | tf_op jit(solution)/shard_map/reduce_scatter | solution.py:114
  134.5 17.0 %all_gather.9 = bf16[256,512]{1,0:T(8,128)(2,1)S(1)} all-gather(bf16[16,512]{1,0:T(8,128)(2,1)S(1)} %convolution_convert_fusion.5), channel_id=1, replica_groups=mesh['gx'=16,'gy'=32] {'gx'}, dimensions={0}, use_global_device_ids=true | all-gather | bytes 278528 | tf_op jit(solution)/shard_map/all_gather | solution.py:125
  151.6 3.3 %collective-permute-start.4 = (bf16[256,512]{1,0:T(8,128)(2,1)S(1)}, bf16[256,512]{1,0:T(8,128)(2,1)S(1)}, u32[]{:S(2)}, u32[]{:S(2)}) collective-permute-start(bf16[256,512]{1,0:T(8,128)(2,1)S(1)} %all_gather.9), channel_id=1, source_target_pairs={{0,1},{1,2},{2,3},{3,4},{4,5},{5,6},{6,7},{7,8},{8,9},{9,10},{10,1... | collective-permute-start | bytes 786440 | tf_op jit(solution)/shard_map/ppermute | solution.py:19
  157.4 17.3 %all_gather.10 = bf16[256,512]{1,0:T(8,128)(2,1)S(1)} all-gather(bf16[16,512]{1,0:T(8,128)(2,1)S(1)} %convolution_convert_fusion.4), channel_id=1, replica_groups=mesh['gx'=16,'gy'=32] {'gx'}, dimensions={0}, use_global_device_ids=true | all-gather | bytes 278528 | tf_op jit(solution)/shard_map/all_gather | solution.py:126
  180.0 1.6 fusion.10
  181.8 54.3 %reduce-scatter.5.cloned.1.call-done = bf16[16,512]{1,0:T(8,128)(2,1)} async-done(((bf16[256,512]{1,0:T(8,128)(2,1)}), bf16[16,512]{1,0:T(8,128)(2,1)}) %reduce-scatter.5.cloned.1.call-update) | async-done | bytes 16400 | tf_op jit(solution)/shard_map/reduce_scatter | solution.py:133
  236.2 1.5 fusion.75
  238.0 17.1 %all_gather.11 = bf16[256,512]{1,0:T(8,128)(2,1)S(1)} all-gather(bf16[16,512]{1,0:T(8,128)(2,1)S(1)} %add_convert_fusion.3), channel_id=1, replica_groups=mesh['gx'=16,'gy'=32] {'gx'}, dimensions={0}, use_global_device_ids=true | all-gather | bytes 278528 | tf_op jit(solution)/shard_map/all_gather | solution.py:137
  255.1 1.9 multiply_convert_fusion.1
  (104 shorter events, 24.1 us)
Async XLA Ops:
  7.2 41.5 %copy-start = (bf16[512,512]{1,0:T(8,128)(2,1)S(1)}, bf16[512,512]{1,0:T(8,128)(2,1)}, u32[]{:S(2)}) copy-start(bf16[512,512]{1,0:T(8,128)(2,1)} %param.31) | copy-start | bytes 1572868
  7.2 124.3 %reduce-scatter.3.cloned.1.call-start = ((), (), s32[]{:S(2)}) async-start(), calls=%async_computation.2 | async-start | bytes 278528 | tf_op jit(solution)/shard_map/reduce_scatter | solution.py:114
  9.7 12.0 %copy-start.3 = (bf16[512,512]{1,0:T(8,128)(2,1)S(1)}, bf16[512,512]{1,0:T(8,128)(2,1)}, u32[]{:S(2)}) copy-start(bf16[512,512]{1,0:T(8,128)(2,1)} %param.22) | copy-start | bytes 1572868
  10.9 12.5 %copy-start.8 = (s32[1024]{0:T(1024)S(1)}, s32[1024]{0:T(1024)}, u32[]{:S(2)}) copy-start(s32[1024]{0:T(1024)} %param.24) | copy-start | bytes 12292
  10.9 12.5 %copy-start.9 = (s32[1024]{0:T(1024)S(1)}, s32[1024]{0:T(1024)}, u32[]{:S(2)}) copy-start(s32[1024]{0:T(1024)} %param.25) | copy-start | bytes 12292
  11.6 19.4 %collective-permute-start = (bf16[1,3,32,512]{3,2,1,0:T(8,128)(2,1)}, bf16[1,3,32,512]{3,2,1,0:T(8,128)(2,1)S(1)}, u32[]{:S(2)}, u32[]{:S(2)}) collective-permute-start(bf16[1,3,32,512]{3,2,1,0:T(8,128)(2,1)} %bitcast.1), channel_id=1, source_target_pairs={{0,32},{32,64},{64,96},{96,128},{128,160},{160,192},{192,224},{224... | collective-permute-start | bytes 294920 | tf_op jit(solution)/shard_map/ppermute | solution.py:19
  16.2 14.8 %collective-permute-start.1 = (bf16[1,3,32,512]{3,2,1,0:T(8,128)(2,1)}, bf16[1,3,32,512]{3,2,1,0:T(8,128)(2,1)}, u32[]{:S(2)}, u32[]{:S(2)}) collective-permute-start(bf16[1,3,32,512]{3,2,1,0:T(8,128)(2,1)} %bitcast.5), channel_id=1, source_target_pairs={{32,0},{64,32},{96,64},{128,96},{160,128},{192,160},{224,192},{256... | collective-permute-start | bytes 294920 | tf_op jit(solution)/shard_map/ppermute | solution.py:20
  31.8 7.8 %collective-permute-start.2 = (bf16[5,1,32,512]{3,2,1,0:T(8,128)(2,1)S(1)}, bf16[5,1,32,512]{3,2,1,0:T(8,128)(2,1)S(1)}, u32[]{:S(2)}, u32[]{:S(2)}) collective-permute-start(bf16[5,1,32,512]{3,2,1,0:T(8,128)(2,1)S(1)} %get-tuple-element.11), channel_id=1, source_target_pairs={{1,0},{2,1},{3,2},{4,3},{5,4},{6,5},{7,6},{8,7},{9,8},{10,9},{11,1... | collective-permute-start | bytes 491528 | tf_op jit(solution)/shard_map/ppermute | solution.py:20
  35.6 7.9 %collective-permute-start.3 = (bf16[5,1,32,512]{3,2,1,0:T(8,128)(2,1)S(1)}, bf16[5,1,32,512]{3,2,1,0:T(8,128)(2,1)S(1)}, u32[]{:S(2)}, u32[]{:S(2)}) collective-permute-start(bf16[5,1,32,512]{3,2,1,0:T(8,128)(2,1)S(1)} %get-tuple-element.10), channel_id=1, source_target_pairs={{0,1},{1,2},{2,3},{3,4},{4,5},{5,6},{6,7},{7,8},{8,9},{9,10},{10,1... | collective-permute-start | bytes 491528 | tf_op jit(solution)/shard_map/ppermute | solution.py:19
  52.2 1.2 copy-start.2
  52.3 1.2 copy-start.10
  65.1 3.1 %copy-start.11 = (f32[512]{0:T(512)S(1)}, f32[512]{0:T(512)}, u32[]{:S(2)}) copy-start(f32[512]{0:T(512)} %param.35) | copy-start | bytes 6148
  69.8 166.4 %reduce-scatter.5.cloned.1.call-start = ((), (), s32[]{:S(2)}) async-start(), calls=%async_computation.3 | async-start | bytes 278528 | tf_op jit(solution)/shard_map/reduce_scatter | solution.py:133
  133.2 43.0 %copy-start.14 = (bf16[512,512]{1,0:T(8,128)(2,1)S(1)}, bf16[512,512]{1,0:T(8,128)(2,1)}, u32[]{:S(2)}) copy-start(bf16[512,512]{1,0:T(8,128)(2,1)} %param.37) | copy-start | bytes 1572868
  151.6 23.8 %collective-permute-start.4 = (bf16[256,512]{1,0:T(8,128)(2,1)S(1)}, bf16[256,512]{1,0:T(8,128)(2,1)S(1)}, u32[]{:S(2)}, u32[]{:S(2)}) collective-permute-start(bf16[256,512]{1,0:T(8,128)(2,1)S(1)} %all_gather.9), channel_id=1, source_target_pairs={{0,1},{1,2},{2,3},{3,4},{4,5},{5,6},{6,7},{7,8},{8,9},{9,10},{10,1... | collective-permute-start | bytes 786440 | tf_op jit(solution)/shard_map/ppermute | solution.py:19
  154.8 20.6 %collective-permute-start.5 = (bf16[256,512]{1,0:T(8,128)(2,1)S(1)}, bf16[256,512]{1,0:T(8,128)(2,1)S(1)}, u32[]{:S(2)}, u32[]{:S(2)}) collective-permute-start(bf16[256,512]{1,0:T(8,128)(2,1)S(1)} %all_gather.9), channel_id=1, source_target_pairs={{1,0},{2,1},{3,2},{4,3},{5,4},{6,5},{7,6},{8,7},{9,8},{10,9},{11,1... | collective-permute-start | bytes 786440 | tf_op jit(solution)/shard_map/ppermute | solution.py:20
  175.5 3.2 %copy-start.1 = (bf16[1024,512]{0,1:T(8,128)(2,1)S(1)}, bf16[1024,512]{0,1:T(8,128)(2,1)}, u32[]{:S(2)}) copy-start(bf16[1024,512]{0,1:T(8,128)(2,1)} %get-tuple-element.6) | copy-start | bytes 3145732
  178.7 2.9 %copy-start.7 = (bf16[16,512]{1,0:T(8,128)(2,1)S(1)}, bf16[16,512]{1,0:T(8,128)(2,1)}, u32[]{:S(2)}) copy-start(bf16[16,512]{1,0:T(8,128)(2,1)} %reduce-scatter.3.cloned.1.call-done) | copy-start | bytes 49156
  178.7 57.5 %copy-start.5 = (bf16[512,512]{1,0:T(8,128)(2,1)S(1)}, bf16[512,512]{1,0:T(8,128)(2,1)}, u32[]{:S(2)}) copy-start(bf16[512,512]{1,0:T(8,128)(2,1)} %param.39) | copy-start | bytes 1572868
  180.0 1.6 copy-start.6
  180.0 57.9 %copy-start.13 = (f32[512]{0:T(512)S(1)}, f32[512]{0:T(512)}, u32[]{:S(2)}) copy-start(f32[512]{0:T(512)} %param.40) | copy-start | bytes 6148
  180.0 75.1 %copy-start.16 = (s32[512]{0:T(512)S(1)}, s32[512]{0:T(512)}, u32[]{:S(2)}) copy-start(s32[512]{0:T(512)} %param.27) | copy-start | bytes 6148
  255.1 1.9 copy-start.4
  257.0 0.7 copy-start.12
  (1 other events, 0.7 us)
Sparse Core Ops, SparseCore 0:
  70.0 61.4 reduce-scatter.2
  178.8 57.3 reduce-scatter.4
where the time goes:
time: 267 us; the launch traced here: 266 us
  waiting for transfers between devices  118 us (44%)
  blocking collectives  51.4 us (19%)
  local copies, waits for them, and re-layouts  22.3 us (8%)
  matrix products  21.8 us (8%)
  starting transfers between devices  20 us (7%)
  other arithmetic  18.3 us (7%)
  between operations  14.5 us (5%)
    reduce_scatter x1, waiting for transfers between devices, per_device(): lax.psum_scatter(partial_value.astype(jnp.bfloat16), 'gx', scatter_dimens...  60 us
    reduce_scatter x1, waiting for transfers between devices, per_device(): lax.psum_scatter(coarse_part.astype(jnp.bfloat16), 'gx', scatter_dimensio...  54.3 us
    all_gather x1, blocking collectives, per_device(): lax.all_gather(dst_share, 'gx', axis=0, tiled=True)  17.3 us
    all_gather x1, blocking collectives, per_device(): coarse_one = lax.all_gather(one_share, 'gx', axis=0, tiled=True)  17.1 us
    all_gather x1, blocking collectives, per_device(): lax.all_gather(src_share, 'gx', axis=0, tiled=True)  17 us
    ppermute x3, starting transfers between devices, extended_2(): before = lax.ppermute(last, axis, up)  11.8 us
    dot_general x4, matrix products, mlp_tail(): jnp.dot(act, w_out, preferred_element_type=jnp.float32)  8.47 us
    ppermute x3, starting transfers between devices, extended_2(): after = lax.ppermute(first, axis, down)  8.07 us
  transfers between devices with their start and end apart: 8, of which 4 were waited for; matrix products, arithmetic and copies ran while one was open for 7% of the time, Pallas kernels for 0%

commit v1 on v0

v1 whole, which is shorter than its diff:
```python
import jax
import jax.numpy as jnp
from jax import lax
from jax.experimental import pallas as pl
from jax.experimental.pallas import tpu as pltpu
from jax.sharding import PartitionSpec as P

COARSE = 256
OFFSETS = ((-1, -1), (-1, 0), (-1, 1), (0, -1), (0, 1), (1, -1), (1, 0), (1, 1))
BF16 = jnp.bfloat16
F32 = jnp.float32


def dot(a, b):
    return jnp.dot(a, b, preferred_element_type=F32)


def silu(v):
    return v / (1.0 + jnp.exp(-v))


def layer_norm(values):
    mean = jnp.mean(values, axis=-1, keepdims=True)
    centred = values - mean
    spread = jnp.mean(centred * centred, axis=-1, keepdims=True)
    return centred * lax.rsqrt(spread + 1e-05)


def mlp_tail(pre, w_out, gain):
    return layer_norm(dot(silu(pre).astype(BF16), w_out)) * gain


def pick(column, width, base=0):
    lanes = lax.broadcasted_iota(jnp.int32, (column.shape[0], width), 1) + base
    return jnp.where(lanes == column, 1.0, 0.0).astype(BF16)


def spread(row, height):
    rows = lax.broadcasted_iota(jnp.int32, (height, row.shape[1]), 0)
    return jnp.where(rows == row, 1.0, 0.0).astype(BF16)


def columns(table, start, count):
    return jnp.concatenate([table[:, k : k + 1] for k in range(start, start + count)], 0)


def outgoing_kernel(nodes, lists, out):
    picks = jnp.transpose(lists[...])
    nodes = nodes[...]
    for k in range(8):
        out[32 * k : 32 * k + 32, :] = dot(pick(picks[:, k : k + 1], 512), nodes).astype(BF16)


def before_halo_kernel(nodes, edges, src, dst, w_in, w_node, pre, node_pre):
    nodes = nodes[...]
    src_proj = dot(nodes, w_in[512:1024, :]).astype(BF16)
    dst_proj = dot(nodes, w_in[1024:1536, :]).astype(BF16)
    src_t, dst_t = jnp.transpose(src[...]), jnp.transpose(dst[...])
    for c in range(4):
        rows = slice(256 * c, 256 * c + 256)
        part = dot(edges[rows, :], w_in[0:512, :])
        part = part + dot(pick(columns(src_t, 2 * c, 2), 512), src_proj)
        pre[rows, :] = part + dot(pick(columns(dst_t, 2 * c, 2), 512), dst_proj)
    node_pre[...] = dot(nodes, w_node[0:512, :])


def after_halo_kernel(
    received, pre, node_pre, nodes, edges, src, dst, parents,
    w_in, w_out, gain, w_node, w_node_out, node_gain,
    edges_out, level_one, pooled, total,
):
    halo = dot(received[...], w_in[512:1024, :]).astype(BF16)
    src_t = jnp.transpose(src[...])
    for c in range(4):
        rows = slice(256 * c, 256 * c + 256)
        part = pre[rows, :] + dot(pick(columns(src_t, 2 * c, 2), 256, 512), halo)
        message = mlp_tail(part, w_out[...], gain[...])
        edges_out[rows, :] = (edges[rows, :].astype(F32) + message).astype(BF16)
        target = jnp.concatenate([dst[2 * c : 2 * c + 1, :], dst[2 * c + 1 : 2 * c + 2, :]], 1)
        added = dot(spread(target, 512), message.astype(BF16))
        if c == 0:
            total[...] = added
        else:
            total[...] += added
    summed = total[...].astype(BF16)
    part = node_pre[...] + dot(summed, w_node[512:1024, :])
    level = nodes[...].astype(F32) + mlp_tail(part, w_node_out[...], node_gain[...])
    level = level.astype(BF16)
    level_one[...] = level
    owner = jnp.concatenate([parents[k : k + 1, :] for k in range(4)], 1)
    pooled[...] = dot(spread(owner, COARSE), level).astype(BF16)


def share_kernel(parts, out):
    total = parts[0].astype(F32)
    for k in range(1, parts.shape[0]):
        total = total + parts[k].astype(F32)
    out[...] = layer_norm(total).astype(BF16)


def up_first_kernel(level_one, w_up, out):
    out[...] = dot(level_one[...], w_up[0:512, :])


def coarse_kernel(
    zero, csrc, cdst, parents, level_one, up_pre,
    w_cin, w_cout, w_nin, w_nout, coarse_gain, w_up, w_up_out, up_gain,
    out, total,
):
    side_src = dot(zero[...], w_cin[0:512, :]).astype(BF16)
    own = zero[256:512, :]
    side_dst = dot(own, w_cin[512:1024, :]).astype(BF16)
    src_t, dst_t = jnp.transpose(csrc[...]), jnp.transpose(cdst[...])
    for c in range(4):
        part = dot(pick(columns(src_t, 2 * c, 2), 768), side_src)
        part = part + dot(pick(columns(dst_t, 2 * c, 2), 256), side_dst)
        message = layer_norm(dot(silu(part).astype(BF16), w_cout[...]))
        target = jnp.concatenate([cdst[2 * c : 2 * c + 1, :], cdst[2 * c + 1 : 2 * c + 2, :]], 1)
        added = dot(spread(target, COARSE), message.astype(BF16))
        if c == 0:
            total[...] = added
        else:
            total[...] += added
    summed = total[...].astype(BF16)
    part = dot(own, w_nin[0:512, :]) + dot(summed, w_nin[512:1024, :])
    one = (own.astype(F32) + mlp_tail(part, w_nout[...], coarse_gain[...])).astype(BF16)
    owner_t = jnp.transpose(parents[...])
    for c in range(2):
        rows = slice(256 * c, 256 * c + 256)
        lifted = dot(pick(columns(owner_t, 2 * c, 2), COARSE), one).astype(BF16)
        part = up_pre[rows, :] + dot(lifted, w_up[512:1024, :])
        tail = mlp_tail(part, w_up_out[...], up_gain[...])
        out[rows, :] = (level_one[rows, :].astype(F32) + tail).astype(BF16)


def call(kernel, outs, *args, scratch=(), flops=0, name=None):
    shapes = [jax.ShapeDtypeStruct(s, d) for s, d in outs]
    moved = sum(a.size * a.dtype.itemsize for a in args) + sum(s.size * s.dtype.itemsize for s in shapes)
    result = pl.pallas_call(
        kernel,
        out_shape=shapes,
        in_specs=[pl.BlockSpec(memory_space=pltpu.VMEM)] * len(args),
        out_specs=[pl.BlockSpec(memory_space=pltpu.VMEM)] * len(shapes),
        scratch_shapes=list(scratch),
        compiler_params=pltpu.CompilerParams(vmem_limit_bytes=48 * 1024 * 1024),
        cost_estimate=pl.CostEstimate(flops=flops, bytes_accessed=moved, transcendentals=0),
        name=name,
    )(*args)
    return result if len(result) > 1 else result[0]


def grid_pairs(step_x, step_y, count_x, count_y):
    pairs = []
    for i in range(count_x):
        for j in range(count_y):
            a, b = i + step_x, j + step_y
            if 0 <= a < count_x and 0 <= b < count_y:
                pairs.append((i * count_y + j, a * count_y + b))
    return pairs


def per_device(
    fine_nodes, fine_edges, edge_src, edge_dst, send_rows, parents, coarse_src, coarse_dst,
    w_edge_in, w_edge_out, edge_gain, w_node_in, w_node_out, node_gain, w_cedge_in, w_cedge_out,
    w_cnode_in, w_cnode_out, coarse_gain, w_up_in, w_up_out, up_gain,
):
    count_x, count_y = lax.axis_size("gx"), lax.axis_size("gy")
    src, dst = edge_src.reshape(8, 128), edge_dst.reshape(8, 128)
    csrc, cdst = coarse_src.reshape(8, 128), coarse_dst.reshape(8, 128)
    owner = parents.reshape(4, 128)
    edge_gain, node_gain = edge_gain.reshape(1, 512), node_gain.reshape(1, 512)
    coarse_gain, up_gain = coarse_gain.reshape(1, 512), up_gain.reshape(1, 512)

    outgoing = call(
        outgoing_kernel, [((256, 512), BF16)], fine_nodes, send_rows[0],
        flops=2 * 256 * 512 * 512, name="outgoing",
    )
    received = [
        lax.ppermute(
            outgoing[32 * k : 32 * k + 32], ("gx", "gy"), grid_pairs(dx, dy, count_x, count_y)
        )
        for k, (dx, dy) in enumerate(OFFSETS)
    ]
    received = jnp.concatenate(received, 0)
    pre, node_pre = call(
        before_halo_kernel, [((1024, 512), F32), ((512, 512), F32)],
        fine_nodes, fine_edges, src, dst, w_edge_in, w_node_in,
        flops=2 * 9 * 512**3, name="before_halo",
    )
    edges_out, level_one, pooled = call(
        after_halo_kernel, [((1024, 512), BF16), ((512, 512), BF16), ((COARSE, 512), BF16)],
        received, pre, node_pre, fine_nodes, fine_edges, src, dst, owner,
        w_edge_in, w_edge_out, edge_gain, w_node_in, w_node_out, node_gain,
        scratch=[pltpu.VMEM((512, 512), F32)], flops=2 * 8 * 512**3, name="after_halo",
    )
    parts = lax.all_to_all(pooled, "gx", 0, 0, tiled=True)
    share = call(
        share_kernel, [((COARSE // count_x, 512), BF16)], parts.reshape(count_x, -1, 512),
        flops=COARSE * 512, name="share",
    )
    up = [(j, j + 1) for j in range(count_y - 1)]
    down = [(j + 1, j) for j in range(count_y - 1)]
    left = lax.ppermute(share, "gy", up)
    right = lax.ppermute(share, "gy", down)
    trio = jnp.stack([left, share, right])
    zero = lax.all_gather(trio, "gx", axis=1, tiled=True).reshape(768, 512)
    up_pre = call(up_first_kernel, [((512, 512), F32)], level_one, w_up_in, flops=2 * 512**3, name="up_first")
    fine_out = call(
        coarse_kernel, [((512, 512), BF16)],
        zero, csrc, cdst, owner, level_one, up_pre,
        w_cedge_in, w_cedge_out, w_cnode_in, w_cnode_out, coarse_gain, w_up_in, w_up_out, up_gain,
        scratch=[pltpu.VMEM((COARSE, 512), F32)], flops=2 * 14 * 512**3, name="coarse",
    )
    return fine_out, edges_out


def solution(mesh):
    fine, flat = P(("gx", "gy"), None), P(("gx", "gy"))
    return jax.shard_map(
        per_device,
        mesh=mesh,
        in_specs=(fine, fine, flat, flat, P(("gx", "gy"), None, None), flat, P("gy"), P("gy")) + (P(),) * 14,
        out_specs=(fine, fine),
        check_vma=False,
    )
```

time: 267 us -> 124 us (0.46)
  the two profiles are of different devices: /device:TPU:1 before, /device:TPU:265 now
where the time goes in v1:
time: 124 us; the launch traced here: 123 us
  blocking collectives  37.6 us (30%)
  starting transfers between devices  36.4 us (29%)
  Pallas kernels  22.4 us (18%)
  waiting for transfers between devices  18.4 us (15%)
  local copies, waits for them, and re-layouts  7.09 us (6%)
    ppermute x8, starting transfers between devices, per_device(): lax.ppermute(outgoing[32 * k:32 * k + 32], ('gx', 'gy'), grid_pairs(dx, d...  28.1 us
    pallas_call x6, Pallas kernels, call(): pl.pallas_call(kernel, out_shape=shapes, in_specs=[pl.BlockSpec(memory_sp...  22.4 us
    all_gather x1, blocking collectives, per_device(): zero = lax.all_gather(trio, 'gx', axis=1, tiled=True).reshape(768, 512)  19.5 us
    all_to_all x1, blocking collectives, per_device(): parts = lax.all_to_all(pooled, 'gx', 0, 0, tiled=True)  18 us
    ppermute x8, waiting for transfers between devices, per_device(): lax.ppermute(outgoing[32 * k:32 * k + 32], ('gx', 'gy'), grid_pairs(dx, d...  13 us
    unnamed x53, local copies, waits for them, and re-layouts  7.05 us
    ppermute x1, starting transfers between devices, per_device(): right = lax.ppermute(share, 'gy', down)  6.38 us
    ppermute x1, waiting for transfers between devices, per_device(): left = lax.ppermute(share, 'gy', up)  5.42 us
  transfers between devices with their start and end apart: 10, of which 4 were waited for; matrix products, arithmetic and copies ran while one was open for 0% of the time, Pallas kernels for 3%

profile of v1, /device:TPU:265, one launch (start us, length us, event | category | flops | bytes accessed | tf_op | source)
XLA Modules:
  0.0 122.9 jit_solution(16149439617023244967)
XLA Ops:
  0.6 1.0 copy-done
  2.4 0.9 outgoing.1
  3.3 4.7 %collective-permute-start.7 = (bf16[32,512]{1,0:T(8,128)(2,1)S(1)}, bf16[32,512]{1,0:T(8,128)(2,1)S(1)}, u32[]{:S(2)}, u32[]{:S(2)}) collective-permute-start(bf16[32,512]{1,0:T(8,128)(2,1)S(1)} %get-tuple-element.12), channel_id=1, source_target_pairs={{0,33},{1,34},{2,35},{3,36},{4,37},{5,38},{6,39},{7,40},{8,41},{9,... | collective-permute-start | bytes 98312 | tf_op jit(solution)/shard_map/ppermute | solution.py:179
  8.0 1.9 %collective-permute-start.6 = (bf16[32,512]{1,0:T(8,128)(2,1)S(1)}, bf16[32,512]{1,0:T(8,128)(2,1)S(1)}, u32[]{:S(2)}, u32[]{:S(2)}) collective-permute-start(bf16[32,512]{1,0:T(8,128)(2,1)S(1)} %get-tuple-element.13), channel_id=1, source_target_pairs={{0,32},{1,33},{2,34},{3,35},{4,36},{5,37},{6,38},{7,39},{8,40},{9,... | collective-permute-start | bytes 98312 | tf_op jit(solution)/shard_map/ppermute | solution.py:179
  10.0 6.9 %collective-permute-start.5 = (bf16[32,512]{1,0:T(8,128)(2,1)S(1)}, bf16[32,512]{1,0:T(8,128)(2,1)S(1)}, u32[]{:S(2)}, u32[]{:S(2)}) collective-permute-start(bf16[32,512]{1,0:T(8,128)(2,1)S(1)} %get-tuple-element.14), channel_id=1, source_target_pairs={{1,32},{2,33},{3,34},{4,35},{5,36},{6,37},{7,38},{8,39},{9,40},{10... | collective-permute-start | bytes 98312 | tf_op jit(solution)/shard_map/ppermute | solution.py:179
  16.8 1.9 %collective-permute-start.4 = (bf16[32,512]{1,0:T(8,128)(2,1)S(1)}, bf16[32,512]{1,0:T(8,128)(2,1)S(1)}, u32[]{:S(2)}, u32[]{:S(2)}) collective-permute-start(bf16[32,512]{1,0:T(8,128)(2,1)S(1)} %get-tuple-element.15), channel_id=1, source_target_pairs={{0,1},{1,2},{2,3},{3,4},{4,5},{5,6},{6,7},{7,8},{8,9},{9,10},{10,1... | collective-permute-start | bytes 98312 | tf_op jit(solution)/shard_map/ppermute | solution.py:179
  18.8 5.8 %collective-permute-start = (bf16[32,512]{1,0:T(8,128)(2,1)S(1)}, bf16[32,512]{1,0:T(8,128)(2,1)S(1)}, u32[]{:S(2)}, u32[]{:S(2)}) collective-permute-start(bf16[32,512]{1,0:T(8,128)(2,1)S(1)} %get-tuple-element.19), channel_id=1, source_target_pairs={{33,0},{34,1},{35,2},{36,3},{37,4},{38,5},{39,6},{40,7},{41,8},{42... | collective-permute-start | bytes 98312 | tf_op jit(solution)/shard_map/ppermute | solution.py:179
  24.6 1.4 %copy-done.1 = bf16[1536,512]{1,0:T(8,128)(2,1)S(1)} copy-done((bf16[1536,512]{1,0:T(8,128)(2,1)S(1)}, bf16[1536,512]{1,0:T(8,128)(2,1)}, u32[]{:S(2)}) %copy-start.1) | copy-done | bytes 1572888
  26.0 1.2 copy-done.2
  27.3 1.2 copy-done.3
  29.9 3.7 %before_halo.1 = (f32[1024,512]{1,0:T(8,128)}, f32[512,512]{1,0:T(8,128)S(1)}) custom-call(bf16[512,512]{1,0:T(8,128)(2,1)S(1)} %copy-done, bf16[1024,512]{1,0:T(8,128)(2,1)S(1)} %copy-done.2, s32[8,128]{1,0:T(8,128)S(1)} %bitcast.18, s32[8,128]{1,0:T(8,128)S(1)} %bitcast.20, bf16[1536,512]{1,0:T(8,128)(2,1)S(1)} %copy-done.1, bf16[1024,512]{1,0:T(8,128)(2,1)S(1)} %copy-done.3), custom_call_target="tpu_custom_call" | custom-call | flops 2415919104 | bytes 7348224 | tf_op jit(solution)/shard_map/before_halo/pallas_call | solution.py:139
  33.6 3.0 %collective-permute-start.1 = (bf16[32,512]{1,0:T(8,128)(2,1)S(1)}, bf16[32,512]{1,0:T(8,128)(2,1)S(1)}, u32[]{:S(2)}, u32[]{:S(2)}) collective-permute-start(bf16[32,512]{1,0:T(8,128)(2,1)S(1)} %get-tuple-element.18), channel_id=1, source_target_pairs={{32,0},{33,1},{34,2},{35,3},{36,4},{37,5},{38,6},{39,7},{40,8},{41... | collective-permute-start | bytes 98312 | tf_op jit(solution)/shard_map/ppermute | solution.py:179
  36.7 2.8 %collective-permute-done.1 = bf16[32,512]{1,0:T(8,128)(2,1)S(1)} collective-permute-done((bf16[32,512]{1,0:T(8,128)(2,1)S(1)}, bf16[32,512]{1,0:T(8,128)(2,1)S(1)}, u32[]{:S(2)}, u32[]{:S(2)}) %collective-permute-start.1) | collective-permute-done | bytes 32800 | tf_op jit(solution)/shard_map/ppermute | solution.py:179
  39.4 1.9 %collective-permute-start.2 = (bf16[32,512]{1,0:T(8,128)(2,1)S(1)}, bf16[32,512]{1,0:T(8,128)(2,1)S(1)}, u32[]{:S(2)}, u32[]{:S(2)}) collective-permute-start(bf16[32,512]{1,0:T(8,128)(2,1)S(1)} %get-tuple-element.17), channel_id=1, source_target_pairs={{32,1},{33,2},{34,3},{35,4},{36,5},{37,6},{38,7},{39,8},{40,9},{41... | collective-permute-start | bytes 98312 | tf_op jit(solution)/shard_map/ppermute | solution.py:179
  41.3 7.5 %collective-permute-done.2 = bf16[32,512]{1,0:T(8,128)(2,1)S(1)} collective-permute-done((bf16[32,512]{1,0:T(8,128)(2,1)S(1)}, bf16[32,512]{1,0:T(8,128)(2,1)S(1)}, u32[]{:S(2)}, u32[]{:S(2)}) %collective-permute-start.2) | collective-permute-done | bytes 32800 | tf_op jit(solution)/shard_map/ppermute | solution.py:179
  48.9 1.9 %collective-permute-start.3 = (bf16[32,512]{1,0:T(8,128)(2,1)S(1)}, bf16[32,512]{1,0:T(8,128)(2,1)S(1)}, u32[]{:S(2)}, u32[]{:S(2)}) collective-permute-start(bf16[32,512]{1,0:T(8,128)(2,1)S(1)} %get-tuple-element.16), channel_id=1, source_target_pairs={{1,0},{2,1},{3,2},{4,3},{5,4},{6,5},{7,6},{8,7},{9,8},{10,9},{11,1... | collective-permute-start | bytes 98312 | tf_op jit(solution)/shard_map/ppermute | solution.py:179
  50.8 2.7 %collective-permute-done.3 = bf16[32,512]{1,0:T(8,128)(2,1)S(1)} collective-permute-done((bf16[32,512]{1,0:T(8,128)(2,1)S(1)}, bf16[32,512]{1,0:T(8,128)(2,1)S(1)}, u32[]{:S(2)}, u32[]{:S(2)}) %collective-permute-start.3) | collective-permute-done | bytes 32800 | tf_op jit(solution)/shard_map/ppermute | solution.py:179
  53.7 8.0 %after_halo.1 = (bf16[1024,512]{1,0:T(8,128)(2,1)}, bf16[512,512]{1,0:T(8,128)(2,1)S(1)}, bf16[256,512]{1,0:T(8,128)(2,1)S(1)}) custom-call(bf16[256,512]{1,0:T(8,128)(2,1)S(1)} %constant_dynamic-update-slice_fusion.received, f32[1024,512]{1,0:T(8,128)} %get-tuple-element.7.pre, f32[512,512]{1,0:T(8,128)S(1)} %get-tuple-element.8.node_pre, ...), custom_call_target="tpu_custom_call" | custom-call | flops 2147483648 | bytes 10500096 | tf_op jit(solution)/shard_map/after_halo/pallas_call | solution.py:139
  61.7 18.0 %all_to_all.9.parts = bf16[16,16,512]{2,1,0:T(8,128)(2,1)S(1)} all-to-all(bf16[16,16,512]{2,1,0:T(8,128)(2,1)S(1)} %bitcast.16), channel_id=1, replica_groups=mesh['gx'=16,'gy'=32] {'gx'}, dimensions={0} | all-to-all | bytes 524288 | tf_op jit(solution)/shard_map/all_to_all | solution.py:196
  79.9 6.4 %collective-permute-start.9 = (bf16[16,512]{1,0:T(8,128)(2,1)S(1)}, bf16[16,512]{1,0:T(8,128)(2,1)S(1)}, u32[]{:S(2)}, u32[]{:S(2)}) collective-permute-start(bf16[16,512]{1,0:T(8,128)(2,1)S(1)} %share.1), channel_id=1, source_target_pairs={{1,0},{2,1},{3,2},{4,3},{5,4},{6,5},{7,6},{8,7},{9,8},{10,9},{11,1... | collective-permute-start | bytes 49160 | tf_op jit(solution)/shard_map/ppermute | solution.py:204
  86.3 1.9 %collective-permute-start.8 = (bf16[16,512]{1,0:T(8,128)(2,1)S(1)}, bf16[16,512]{1,0:T(8,128)(2,1)S(1)}, u32[]{:S(2)}, u32[]{:S(2)}) collective-permute-start(bf16[16,512]{1,0:T(8,128)(2,1)S(1)} %share.1), channel_id=1, source_target_pairs={{0,1},{1,2},{2,3},{3,4},{4,5},{5,6},{6,7},{7,8},{8,9},{9,10},{10,1... | collective-permute-start | bytes 49160 | tf_op jit(solution)/shard_map/ppermute | solution.py:203
  88.7 5.4 %collective-permute-done.8 = bf16[16,512]{1,0:T(8,128)(2,1)S(1)} collective-permute-done((bf16[16,512]{1,0:T(8,128)(2,1)S(1)}, bf16[16,512]{1,0:T(8,128)(2,1)S(1)}, u32[]{:S(2)}, u32[]{:S(2)}) %collective-permute-start.8) | collective-permute-done | bytes 16416 | tf_op jit(solution)/shard_map/ppermute | solution.py:203
  94.1 19.5 %all_gather.3 = bf16[3,256,512]{2,1,0:T(8,128)(2,1)S(1)} all-gather(bf16[3,16,512]{2,1,0:T(8,128)(2,1)S(1)} %pad_maximum_fusion), channel_id=1, replica_groups=mesh['gx'=16,'gy'=32] {'gx'}, dimensions={1}, use_global_device_ids=true | all-gather | bytes 835584 | tf_op jit(solution)/shard_map/all_gather | solution.py:206
  113.8 9.1 %coarse.1 = bf16[512,512]{1,0:T(8,128)(2,1)} custom-call(bf16[768,512]{1,0:T(8,128)(2,1)S(1)} %bitcast.15, s32[8,128]{1,0:T(8,128)S(1)} %bitcast.27, s32[8,128]{1,0:T(8,128)S(1)} %bitcast.28, s32[4,128]{1,0:T(4,128)S(1)} %bitcast.26, bf16[512,512]{1,0:T(8,128)(2,1)S(1)} %get-tuple-element.10.level_one, f32[512,512]{1,0:T(8,128)S(1)} %up_first.1.up_pre, ...), custom_call_target="tpu_custom_call" | custom-call | flops 3758096384 | bytes 7616512 | tf_op jit(solution)/shard_map/coarse/pallas_call | solution.py:139
  (60 shorter events, 2.9 us)
Async XLA Ops:
  3.3 50.2 %collective-permute-start.7 = (bf16[32,512]{1,0:T(8,128)(2,1)S(1)}, bf16[32,512]{1,0:T(8,128)(2,1)S(1)}, u32[]{:S(2)}, u32[]{:S(2)}) collective-permute-start(bf16[32,512]{1,0:T(8,128)(2,1)S(1)} %get-tuple-element.12), channel_id=1, source_target_pairs={{0,33},{1,34},{2,35},{3,36},{4,37},{5,38},{6,39},{7,40},{8,41},{9,... | collective-permute-start | bytes 98312 | tf_op jit(solution)/shard_map/ppermute | solution.py:179
  8.0 45.5 %collective-permute-start.6 = (bf16[32,512]{1,0:T(8,128)(2,1)S(1)}, bf16[32,512]{1,0:T(8,128)(2,1)S(1)}, u32[]{:S(2)}, u32[]{:S(2)}) collective-permute-start(bf16[32,512]{1,0:T(8,128)(2,1)S(1)} %get-tuple-element.13), channel_id=1, source_target_pairs={{0,32},{1,33},{2,34},{3,35},{4,36},{5,37},{6,38},{7,39},{8,40},{9,... | collective-permute-start | bytes 98312 | tf_op jit(solution)/shard_map/ppermute | solution.py:179
  10.0 43.6 %collective-permute-start.5 = (bf16[32,512]{1,0:T(8,128)(2,1)S(1)}, bf16[32,512]{1,0:T(8,128)(2,1)S(1)}, u32[]{:S(2)}, u32[]{:S(2)}) collective-permute-start(bf16[32,512]{1,0:T(8,128)(2,1)S(1)} %get-tuple-element.14), channel_id=1, source_target_pairs={{1,32},{2,33},{3,34},{4,35},{5,36},{6,37},{7,38},{8,39},{9,40},{10... | collective-permute-start | bytes 98312 | tf_op jit(solution)/shard_map/ppermute | solution.py:179
  16.8 36.7 %collective-permute-start.4 = (bf16[32,512]{1,0:T(8,128)(2,1)S(1)}, bf16[32,512]{1,0:T(8,128)(2,1)S(1)}, u32[]{:S(2)}, u32[]{:S(2)}) collective-permute-start(bf16[32,512]{1,0:T(8,128)(2,1)S(1)} %get-tuple-element.15), channel_id=1, source_target_pairs={{0,1},{1,2},{2,3},{3,4},{4,5},{5,6},{6,7},{7,8},{8,9},{9,10},{10,1... | collective-permute-start | bytes 98312 | tf_op jit(solution)/shard_map/ppermute | solution.py:179
  18.8 14.9 %collective-permute-start = (bf16[32,512]{1,0:T(8,128)(2,1)S(1)}, bf16[32,512]{1,0:T(8,128)(2,1)S(1)}, u32[]{:S(2)}, u32[]{:S(2)}) collective-permute-start(bf16[32,512]{1,0:T(8,128)(2,1)S(1)} %get-tuple-element.19), channel_id=1, source_target_pairs={{33,0},{34,1},{35,2},{36,3},{37,4},{38,5},{39,6},{40,7},{41,8},{42... | collective-permute-start | bytes 98312 | tf_op jit(solution)/shard_map/ppermute | solution.py:179
  29.9 23.7 %copy-start.7 = (bf16[512,512]{1,0:T(8,128)(2,1)S(1)}, bf16[512,512]{1,0:T(8,128)(2,1)}, u32[]{:S(2)}) copy-start(bf16[512,512]{1,0:T(8,128)(2,1)} %w_node_out.1) | copy-start | bytes 1572868
  29.9 23.8 %copy-start.11 = (f32[512]{0:T(512)S(1)}, f32[512]{0:T(512)}, u32[]{:S(2)}) copy-start(f32[512]{0:T(512)} %param.32) | copy-start | bytes 6148
  29.9 23.8 %copy-start.12 = (f32[512]{0:T(512)S(1)}, f32[512]{0:T(512)}, u32[]{:S(2)}) copy-start(f32[512]{0:T(512)} %param.35) | copy-start | bytes 6148
  29.9 23.8 %copy-start.13 = (s32[512]{0:T(512)S(1)}, s32[512]{0:T(512)}, u32[]{:S(2)}) copy-start(s32[512]{0:T(512)} %param.27) | copy-start | bytes 6148
  33.6 5.8 %collective-permute-start.1 = (bf16[32,512]{1,0:T(8,128)(2,1)S(1)}, bf16[32,512]{1,0:T(8,128)(2,1)S(1)}, u32[]{:S(2)}, u32[]{:S(2)}) collective-permute-start(bf16[32,512]{1,0:T(8,128)(2,1)S(1)} %get-tuple-element.18), channel_id=1, source_target_pairs={{32,0},{33,1},{34,2},{35,3},{36,4},{37,5},{38,6},{39,7},{40,8},{41... | collective-permute-start | bytes 98312 | tf_op jit(solution)/shard_map/ppermute | solution.py:179
  39.4 9.4 %collective-permute-start.2 = (bf16[32,512]{1,0:T(8,128)(2,1)S(1)}, bf16[32,512]{1,0:T(8,128)(2,1)S(1)}, u32[]{:S(2)}, u32[]{:S(2)}) collective-permute-start(bf16[32,512]{1,0:T(8,128)(2,1)S(1)} %get-tuple-element.17), channel_id=1, source_target_pairs={{32,1},{33,2},{34,3},{35,4},{36,5},{37,6},{38,7},{39,8},{40,9},{41... | collective-permute-start | bytes 98312 | tf_op jit(solution)/shard_map/ppermute | solution.py:179
  48.9 4.6 %collective-permute-start.3 = (bf16[32,512]{1,0:T(8,128)(2,1)S(1)}, bf16[32,512]{1,0:T(8,128)(2,1)S(1)}, u32[]{:S(2)}, u32[]{:S(2)}) collective-permute-start(bf16[32,512]{1,0:T(8,128)(2,1)S(1)} %get-tuple-element.16), channel_id=1, source_target_pairs={{1,0},{2,1},{3,2},{4,3},{5,4},{6,5},{7,6},{8,7},{9,8},{10,9},{11,1... | collective-permute-start | bytes 98312 | tf_op jit(solution)/shard_map/ppermute | solution.py:179
  53.7 34.6 %copy-start.5 = (bf16[1024,512]{1,0:T(8,128)(2,1)S(1)}, bf16[1024,512]{1,0:T(8,128)(2,1)}, u32[]{:S(2)}) copy-start(bf16[1024,512]{1,0:T(8,128)(2,1)} %w_up.3) | copy-start | bytes 3145732
  61.6 52.1 %copy-start.14 = (bf16[1024,512]{1,0:T(8,128)(2,1)S(1)}, bf16[1024,512]{1,0:T(8,128)(2,1)}, u32[]{:S(2)}) copy-start(bf16[1024,512]{1,0:T(8,128)(2,1)} %w_cin.1) | copy-start | bytes 3145732
  61.6 52.1 %copy-start.15 = (bf16[1024,512]{1,0:T(8,128)(2,1)S(1)}, bf16[1024,512]{1,0:T(8,128)(2,1)}, u32[]{:S(2)}) copy-start(bf16[1024,512]{1,0:T(8,128)(2,1)} %w_nin.1) | copy-start | bytes 3145732
  61.6 52.1 %copy-start.16 = (bf16[512,512]{1,0:T(8,128)(2,1)S(1)}, bf16[512,512]{1,0:T(8,128)(2,1)}, u32[]{:S(2)}) copy-start(bf16[512,512]{1,0:T(8,128)(2,1)} %w_cout.1) | copy-start | bytes 1572868
  61.6 52.1 %copy-start.17 = (bf16[512,512]{1,0:T(8,128)(2,1)S(1)}, bf16[512,512]{1,0:T(8,128)(2,1)}, u32[]{:S(2)}) copy-start(bf16[512,512]{1,0:T(8,128)(2,1)} %w_nout.1) | copy-start | bytes 1572868
  61.6 52.1 %copy-start.18 = (bf16[512,512]{1,0:T(8,128)(2,1)S(1)}, bf16[512,512]{1,0:T(8,128)(2,1)}, u32[]{:S(2)}) copy-start(bf16[512,512]{1,0:T(8,128)(2,1)} %w_up_out.1) | copy-start | bytes 1572868
  61.6 52.1 %copy-start.19 = (s32[1024]{0:T(1024)S(1)}, s32[1024]{0:T(1024)}, u32[]{:S(2)}) copy-start(s32[1024]{0:T(1024)} %param.28) | copy-start | bytes 12292
  61.7 52.1 %copy-start.20 = (s32[1024]{0:T(1024)S(1)}, s32[1024]{0:T(1024)}, u32[]{:S(2)}) copy-start(s32[1024]{0:T(1024)} %param.29) | copy-start | bytes 12292
  61.7 52.1 %copy-start.21 = (f32[512]{0:T(512)S(1)}, f32[512]{0:T(512)}, u32[]{:S(2)}) copy-start(f32[512]{0:T(512)} %param.40) | copy-start | bytes 6148
  61.7 52.1 %copy-start.22 = (f32[512]{0:T(512)S(1)}, f32[512]{0:T(512)}, u32[]{:S(2)}) copy-start(f32[512]{0:T(512)} %param.43) | copy-start | bytes 6148
  79.9 8.8 %collective-permute-start.9 = (bf16[16,512]{1,0:T(8,128)(2,1)S(1)}, bf16[16,512]{1,0:T(8,128)(2,1)S(1)}, u32[]{:S(2)}, u32[]{:S(2)}) collective-permute-start(bf16[16,512]{1,0:T(8,128)(2,1)S(1)} %share.1), channel_id=1, source_target_pairs={{1,0},{2,1},{3,2},{4,3},{5,4},{6,5},{7,6},{8,7},{9,8},{10,9},{11,1... | collective-permute-start | bytes 49160 | tf_op jit(solution)/shard_map/ppermute | solution.py:204
  86.3 7.8 %collective-permute-start.8 = (bf16[16,512]{1,0:T(8,128)(2,1)S(1)}, bf16[16,512]{1,0:T(8,128)(2,1)S(1)}, u32[]{:S(2)}, u32[]{:S(2)}) collective-permute-start(bf16[16,512]{1,0:T(8,128)(2,1)S(1)} %share.1), channel_id=1, source_target_pairs={{0,1},{1,2},{2,3},{3,4},{4,5},{5,6},{6,7},{7,8},{8,9},{9,10},{10,1... | collective-permute-start | bytes 49160 | tf_op jit(solution)/shard_map/ppermute | solution.py:203
  (9 other events, 54.4 us)

commit v2 on v1

v2 whole, which is shorter than its diff:
```python
import jax
import jax.numpy as jnp
from jax import lax
from jax.experimental import pallas as pl
from jax.experimental.pallas import tpu as pltpu
from jax.sharding import PartitionSpec as P

COARSE = 256
CHUNK = 1024
BF16 = jnp.bfloat16
F32 = jnp.float32


def dot(a, b):
    return jnp.dot(a, b, preferred_element_type=F32)


def silu(v):
    half = 0.5 * v
    return half + half * jnp.tanh(half)


def layer_norm(values):
    mean = jnp.mean(values, axis=-1, keepdims=True)
    centred = values - mean
    spread = jnp.mean(centred * centred, axis=-1, keepdims=True)
    return centred * lax.rsqrt(spread + 1e-05)


def mlp_tail(pre, w_out, gain):
    return layer_norm(dot(silu(pre).astype(BF16), w_out)) * gain


def pick(column, width, base=0):
    lanes = lax.broadcasted_iota(jnp.int32, (column.shape[0], width), 1) + base
    return jnp.where(lanes == column, 1.0, 0.0).astype(BF16)


def spread(row, height):
    rows = lax.broadcasted_iota(jnp.int32, (height, row.shape[1]), 0)
    return jnp.where(rows == row, 1.0, 0.0).astype(BF16)


def columns(table, start, count):
    return jnp.concatenate([table[:, k : k + 1] for k in range(start, start + count)], 0)


def outgoing_kernel(nodes, lists, before, left, right, after):
    picks = jnp.transpose(lists[...])
    nodes = nodes[...]
    picked = dot(jnp.concatenate([pick(picks[:, k : k + 1], 512) for k in range(8)], 0), nodes)
    picked = picked.astype(BF16)
    before[...] = picked[0:96, :]
    left[...] = picked[96:128, :]
    right[...] = picked[128:160, :]
    after[...] = picked[160:256, :]


def tables_kernel(nodes, src, dst, w_in, gathered):
    nodes = nodes[...]
    src_proj = dot(nodes, w_in[512:1024, :]).astype(BF16)
    dst_proj = dot(nodes, w_in[1024:1536, :]).astype(BF16)
    src_t, dst_t = jnp.transpose(src[...]), jnp.transpose(dst[...])
    for c in range(1024 // CHUNK):
        rows = slice(CHUNK * c, CHUNK * c + CHUNK)
        part = dot(pick(columns(src_t, CHUNK // 128 * c, CHUNK // 128), 512), src_proj)
        gathered[rows, :] = part + dot(pick(columns(dst_t, CHUNK // 128 * c, CHUNK // 128), 512), dst_proj)


def edges_kernel(nodes, edges, gathered, w_in, w_node, pre, node_pre):
    pre[...] = gathered[...] + dot(edges[...], w_in[0:512, :])
    node_pre[...] = dot(nodes[...], w_node[0:512, :])


def after_halo_kernel(
    above, below, from_right, from_left, pre, node_pre, nodes, edges, src, dst, parents,
    w_in, w_out, gain, w_node, w_node_out, node_gain,
    edges_out, level_one, pooled, total,
):
    received = jnp.concatenate(
        [
            from_right[0:32, :], above[32:64, :], from_left[0:32, :], from_right[32:64, :],
            from_left[32:64, :], from_right[64:96, :], below[32:64, :], from_left[64:96, :],
        ],
        0,
    )
    halo = dot(received, w_in[512:1024, :]).astype(BF16)
    src_t = jnp.transpose(src[...])
    for c in range(1024 // CHUNK):
        rows = slice(CHUNK * c, CHUNK * c + CHUNK)
        part = pre[rows, :] + dot(pick(columns(src_t, CHUNK // 128 * c, CHUNK // 128), 256, 512), halo)
        message = mlp_tail(part, w_out[...], gain[...])
        edges_out[rows, :] = (edges[rows, :].astype(F32) + message).astype(BF16)
        target = jnp.concatenate([dst[k : k + 1, :] for k in range(CHUNK // 128 * c, CHUNK // 128 * (c + 1))], 1)
        added = dot(spread(target, 512), message.astype(BF16))
        if c == 0:
            total[...] = added
        else:
            total[...] += added
    summed = total[...].astype(BF16)
    part = node_pre[...] + dot(summed, w_node[512:1024, :])
    level = nodes[...].astype(F32) + mlp_tail(part, w_node_out[...], node_gain[...])
    level = level.astype(BF16)
    level_one[...] = level
    owner = jnp.concatenate([parents[k : k + 1, :] for k in range(4)], 1)
    pooled[...] = dot(spread(owner, COARSE), level).astype(BF16)


def share_kernel(parts, out):
    total = parts[0].astype(F32)
    for k in range(1, parts.shape[0]):
        total = total + parts[k].astype(F32)
    share = layer_norm(total).astype(BF16)
    for k in range(out.shape[0]):
        out[k] = share


def own_kernel(
    zero, csrc, cdst, level_one, w_cin, w_nin, w_up, pre, node_pre, up_pre
):
    zero = zero[...]
    side_src = dot(zero, w_cin[0:512, :]).astype(BF16)
    side_dst = dot(zero, w_cin[512:1024, :]).astype(BF16)
    src_t, dst_t = jnp.transpose(csrc[...]), jnp.transpose(cdst[...])
    for c in range(1024 // CHUNK):
        rows = slice(CHUNK * c, CHUNK * c + CHUNK)
        part = dot(pick(columns(src_t, CHUNK // 128 * c, CHUNK // 128), COARSE, COARSE), side_src)
        pre[rows, :] = part + dot(pick(columns(dst_t, CHUNK // 128 * c, CHUNK // 128), COARSE), side_dst)
    node_pre[...] = dot(zero, w_nin[0:512, :])
    up_pre[...] = dot(level_one[...], w_up[0:512, :])


def coarse_kernel(
    left, right, zero, pre, node_pre, up_pre, csrc, cdst, parents, level_one,
    w_cin, w_cout, w_nin, w_nout, coarse_gain, w_up, w_up_out, up_gain,
    out, total,
):
    sides = dot(jnp.concatenate([left[...], right[...]], 0), w_cin[0:512, :]).astype(BF16)
    src = csrc[...]
    src_t = jnp.transpose(jnp.where(src < 256, src, src - 256))
    src_t = jnp.where(jnp.transpose((src >> 8)) == 1, -1, src_t)
    for c in range(1024 // CHUNK):
        rows = slice(CHUNK * c, CHUNK * c + CHUNK)
        part = pre[rows, :] + dot(pick(columns(src_t, CHUNK // 128 * c, CHUNK // 128), 512), sides)
        message = layer_norm(dot(silu(part).astype(BF16), w_cout[...]))
        target = jnp.concatenate([cdst[k : k + 1, :] for k in range(CHUNK // 128 * c, CHUNK // 128 * (c + 1))], 1)
        added = dot(spread(target, COARSE), message.astype(BF16))
        if c == 0:
            total[...] = added
        else:
            total[...] += added
    summed = total[...].astype(BF16)
    part = node_pre[...] + dot(summed, w_nin[512:1024, :])
    one = (zero[...].astype(F32) + mlp_tail(part, w_nout[...], coarse_gain[...])).astype(BF16)
    owner_t = jnp.transpose(parents[...])
    for c in range(2):
        rows = slice(256 * c, 256 * c + 256)
        lifted = dot(pick(columns(owner_t, 2 * c, 2), COARSE), one).astype(BF16)
        part = up_pre[rows, :] + dot(lifted, w_up[512:1024, :])
        tail = mlp_tail(part, w_up_out[...], up_gain[...])
        out[rows, :] = (level_one[rows, :].astype(F32) + tail).astype(BF16)


def kept(shape, dtype):
    return pltpu.VMEM(shape, dtype)


def call(kernel, outs, *args, scratch=(), flops=0, name=None):
    shapes = [kept(s, d) if d == F32 else jax.ShapeDtypeStruct(s, d) for s, d in outs]
    args = [pltpu.with_memory_space_constraint(a, pltpu.VMEM) if a.dtype == F32 and a.shape[0] > 1 else a for a in args]
    moved = sum(a.size * a.dtype.itemsize for a in args)
    result = pl.pallas_call(
        kernel,
        out_shape=shapes,
        in_specs=[pl.BlockSpec(memory_space=pltpu.VMEM)] * len(args),
        out_specs=[pl.BlockSpec(memory_space=pltpu.VMEM)] * len(shapes),
        scratch_shapes=list(scratch),
        compiler_params=pltpu.CompilerParams(vmem_limit_bytes=48 * 1024 * 1024),
        cost_estimate=pl.CostEstimate(flops=flops, bytes_accessed=moved, transcendentals=0),
        name=name,
    )(*args)
    return result if len(result) > 1 else result[0]


def steps(count):
    up = [(k, k + 1) for k in range(count - 1)]
    return up, [(b, a) for a, b in up]


def per_device(
    fine_nodes, fine_edges, edge_src, edge_dst, send_rows, parents, coarse_src, coarse_dst,
    w_edge_in, w_edge_out, edge_gain, w_node_in, w_node_out, node_gain, w_cedge_in, w_cedge_out,
    w_cnode_in, w_cnode_out, coarse_gain, w_up_in, w_up_out, up_gain,
):
    count_x, count_y = lax.axis_size("gx"), lax.axis_size("gy")
    src, dst = edge_src.reshape(8, 128), edge_dst.reshape(8, 128)
    csrc, cdst = coarse_src.reshape(8, 128), coarse_dst.reshape(8, 128)
    owner = parents.reshape(4, 128)
    edge_gain, node_gain = edge_gain.reshape(1, 512), node_gain.reshape(1, 512)
    coarse_gain, up_gain = coarse_gain.reshape(1, 512), up_gain.reshape(1, 512)

    before, left, right, after = call(
        outgoing_kernel, [((96, 512), BF16), ((32, 512), BF16), ((32, 512), BF16), ((96, 512), BF16)],
        fine_nodes, send_rows[0], flops=100 * 2 * 256 * 512 * 512, name="outgoing",
    )
    up_x, down_x = steps(count_x)
    up_y, down_y = steps(count_y)
    above = lax.ppermute(before, "gx", down_x)
    below = lax.ppermute(after, "gx", up_x)
    gathered = call(
        tables_kernel, [((1024, 512), F32)], fine_nodes, src, dst, w_edge_in, flops=2 * 6 * 512**3, name="tables"
    )
    above, below, gathered = lax.optimization_barrier((above, below, gathered))
    from_right = lax.ppermute(jnp.concatenate([above[0:32], left, below[0:32]], 0), "gy", down_y)
    from_left = lax.ppermute(jnp.concatenate([above[64:96], right, below[64:96]], 0), "gy", up_y)
    pre, node_pre = call(
        edges_kernel, [((1024, 512), F32), ((512, 512), F32)],
        fine_nodes, fine_edges, gathered, w_edge_in, w_node_in, flops=2 * 3 * 512**3, name="edges",
    )
    edges_out, level_one, pooled = call(
        after_halo_kernel, [((1024, 512), BF16), ((512, 512), BF16), ((COARSE, 512), BF16)],
        above, below, from_right, from_left, pre, node_pre, fine_nodes, fine_edges, src, dst, owner,
        w_edge_in, w_edge_out, edge_gain, w_node_in, w_node_out, node_gain,
        scratch=[pltpu.VMEM((512, 512), F32)], flops=2 * 8 * 512**3, name="after_halo",
    )
    parts = lax.all_to_all(pooled, "gx", 0, 0, tiled=True)
    shares = call(
        share_kernel, [((count_x, COARSE // count_x, 512), BF16)], parts.reshape(count_x, -1, 512),
        flops=COARSE * 512, name="share",
    )
    zero = lax.all_to_all(shares, "gx", 0, 0, tiled=True).reshape(COARSE, 512)
    left, right = lax.ppermute(zero, "gy", up_y), lax.ppermute(zero, "gy", down_y)
    pre, node_pre, up_pre = call(
        own_kernel, [((1024, 512), F32), ((COARSE, 512), F32), ((512, 512), F32)],
        zero, csrc, cdst, level_one, w_cedge_in, w_cnode_in, w_up_in,
        flops=2 * 5 * 512**3, name="own_column",
    )
    fine_out = call(
        coarse_kernel, [((512, 512), BF16)],
        left, right, zero, pre, node_pre, up_pre, csrc, cdst, owner, level_one,
        w_cedge_in, w_cedge_out, w_cnode_in, w_cnode_out, coarse_gain, w_up_in, w_up_out, up_gain,
        scratch=[pltpu.VMEM((COARSE, 512), F32)], flops=2 * 9 * 512**3, name="coarse",
    )
    return fine_out, edges_out


def solution(mesh):
    fine, flat = P(("gx", "gy"), None), P(("gx", "gy"))
    return jax.shard_map(
        per_device,
        mesh=mesh,
        in_specs=(fine, fine, flat, flat, P(("gx", "gy"), None, None), flat, P("gy"), P("gy")) + (P(),) * 14,
        out_specs=(fine, fine),
        check_vma=False,
    )
```

time: 124 us -> 89.7 us (0.72)
  the two profiles are of different devices: /device:TPU:265 before, /device:TPU:256 now
where the time goes in v2:
time: 89.7 us; the launch traced here: 89.3 us
  blocking collectives  34.4 us (38%)
  Pallas kernels  23 us (26%)
  starting transfers between devices  16.3 us (18%)
  waiting for transfers between devices  12.9 us (14%)
  local copies, waits for them, and re-layouts  1.82 us (2%)
  between operations  0.94 us (1%)
    pallas_call x7, Pallas kernels, call(): pl.pallas_call(kernel, out_shape=shapes, in_specs=[pl.BlockSpec(memory_sp...  23 us
    all_to_all x1, blocking collectives, per_device(): parts = lax.all_to_all(pooled, 'gx', 0, 0, tiled=True)  20 us
    all_to_all x1, blocking collectives, per_device(): zero = lax.all_to_all(shares, 'gx', 0, 0, tiled=True).reshape(COARSE, 512)  14.4 us
    ppermute x1, waiting for transfers between devices, per_device(): lax.ppermute(jnp.concatenate([above[64:96], right, below[64:96]], 0), 'gy...  5.72 us
    ppermute x1, waiting for transfers between devices, per_device(): lax.ppermute(zero, 'gy', up_y)  5.43 us
    ppermute x1, starting transfers between devices, per_device(): lax.ppermute(jnp.concatenate([above[0:32], left, below[0:32]], 0), 'gy',...  3.76 us
    ppermute x1, starting transfers between devices, per_device(): lax.ppermute(zero, 'gy', up_y)  3.46 us
    ppermute x1, starting transfers between devices, per_device(): below = lax.ppermute(after, 'gx', up_x)  3.04 us
  transfers between devices with their start and end apart: 6, of which 3 were waited for; matrix products, arithmetic and copies ran while one was open for 0% of the time, Pallas kernels for 9%

profile of v2, /device:TPU:256, one launch (start us, length us, event | category | flops | bytes accessed | tf_op | source)
XLA Modules:
  0.0 89.3 jit_solution(13742295603422153301)
XLA Ops:
  0.6 1.0 %copy-done.1 = bf16[512,512]{1,0:T(8,128)(2,1)S(1)} copy-done((bf16[512,512]{1,0:T(8,128)(2,1)S(1)}, bf16[512,512]{1,0:T(8,128)(2,1)}, u32[]{:S(2)}) %copy-start.1) | copy-done | bytes 524312
  1.7 0.7 copy-done.16
  2.4 0.4 outgoing.1
  2.8 1.4 %collective-permute-start = (bf16[96,512]{1,0:T(8,128)(2,1)S(1)}, bf16[96,512]{1,0:T(8,128)(2,1)S(1)}, u32[]{:S(2)}, u32[]{:S(2)}) collective-permute-start(bf16[96,512]{1,0:T(8,128)(2,1)S(1)} %get-tuple-element.17), channel_id=1, source_target_pairs={{32,0},{64,32},{96,64},{128,96},{160,128},{192,160},{224,192},{256... | collective-permute-start | bytes 294920 | tf_op jit(solution)/shard_map/ppermute | solution.py:208
  4.2 3.0 %collective-permute-start.1 = (bf16[96,512]{1,0:T(8,128)(2,1)S(1)}, bf16[96,512]{1,0:T(8,128)(2,1)S(1)}, u32[]{:S(2)}, u32[]{:S(2)}) collective-permute-start(bf16[96,512]{1,0:T(8,128)(2,1)S(1)} %get-tuple-element.18), channel_id=1, source_target_pairs={{0,32},{32,64},{64,96},{96,128},{128,160},{160,192},{192,224},{224... | collective-permute-start | bytes 294920 | tf_op jit(solution)/shard_map/ppermute | solution.py:209
  7.3 1.9 %tables.1.gathered = f32[1024,512]{1,0:T(8,128)S(1)} custom-call(bf16[512,512]{1,0:T(8,128)(2,1)S(1)} %copy-done.1, s32[8,128]{1,0:T(8,128)S(1)} %bitcast.19, s32[8,128]{1,0:T(8,128)S(1)} %bitcast.21, bf16[1536,512]{1,0:T(8,128)(2,1)S(1)} %copy-done), custom_call_target="tpu_custom_call" | custom-call | flops 1610612736 | bytes 2105344 | tf_op jit(solution)/shard_map/tables/pallas_call | solution.py:172
  9.3 3.8 %collective-permute-start.2 = (bf16[96,512]{1,0:T(8,128)(2,1)S(1)}, bf16[96,512]{1,0:T(8,128)(2,1)S(1)}, u32[]{:S(2)}, u32[]{:S(2)}) collective-permute-start(bf16[96,512]{1,0:T(8,128)(2,1)S(1)} %pad_maximum_fusion), channel_id=1, source_target_pairs={{1,0},{2,1},{3,2},{4,3},{5,4},{6,5},{7,6},{8,7},{9,8},{10,9},{11,1... | collective-permute-start | bytes 294920 | tf_op jit(solution)/shard_map/ppermute | solution.py:214
  13.0 0.0 copy-start.5
  13.1 0.0 copy-start.6
  13.1 0.0 copy-start.15
  13.1 2.2 %collective-permute-start.3 = (bf16[96,512]{1,0:T(8,128)(2,1)S(1)}, bf16[96,512]{1,0:T(8,128)(2,1)S(1)}, u32[]{:S(2)}, u32[]{:S(2)}) collective-permute-start(bf16[96,512]{1,0:T(8,128)(2,1)S(1)} %pad_maximum_fusion.1), channel_id=1, source_target_pairs={{0,1},{1,2},{2,3},{3,4},{4,5},{5,6},{6,7},{7,8},{8,9},{9,10},{10,1... | collective-permute-start | bytes 294920 | tf_op jit(solution)/shard_map/ppermute | solution.py:215
  15.3 3.0 %edges.3 = (f32[1024,512]{1,0:T(8,128)S(1)}, f32[512,512]{1,0:T(8,128)S(1)}) custom-call(bf16[512,512]{1,0:T(8,128)(2,1)S(1)} %copy-done.1, bf16[1024,512]{1,0:T(8,128)(2,1)} %edges.5, f32[1024,512]{1,0:T(8,128)S(1)} %tables.1.gathered, bf16[1536,512]{1,0:T(8,128)(2,1)} %w_in.5, bf16[1024,512]{1,0:T(8,128)(2,1)} %w_node.3), custom_call_target="tpu_custom_call" | custom-call | flops 805306368 | bytes 6291456 | tf_op jit(solution)/shard_map/edges/pallas_call | solution.py:172
  18.3 5.7 %collective-permute-done.3.from_left = bf16[96,512]{1,0:T(8,128)(2,1)S(1)} collective-permute-done((bf16[96,512]{1,0:T(8,128)(2,1)S(1)}, bf16[96,512]{1,0:T(8,128)(2,1)S(1)}, u32[]{:S(2)}, u32[]{:S(2)}) %collective-permute-start.3) | collective-permute-done | bytes 98336 | tf_op jit(solution)/shard_map/ppermute | solution.py:215
  24.1 0.0 copy-start.2
  24.1 6.5 %after_halo.1 = (bf16[1024,512]{1,0:T(8,128)(2,1)}, bf16[512,512]{1,0:T(8,128)(2,1)S(1)}, bf16[256,512]{1,0:T(8,128)(2,1)S(1)}) custom-call(bf16[96,512]{1,0:T(8,128)(2,1)S(1)} %collective-permute-done.above, bf16[96,512]{1,0:T(8,128)(2,1)S(1)} %collective-permute-done.1.below, bf16[96,512]{1,0:T(8,128)(2,1)S(1)} %collective-permute-done.2.from_right, ...), custom_call_target="tpu_custom_call" | custom-call | flops 2147483648 | bytes 8796160 | tf_op jit(solution)/shard_map/after_halo/pallas_call | solution.py:172
  30.7 20.0 %all_to_all.14.parts = bf16[16,16,512]{2,1,0:T(8,128)(2,1)S(1)} all-to-all(bf16[16,16,512]{2,1,0:T(8,128)(2,1)S(1)} %bitcast.16), channel_id=1, replica_groups=mesh['gx'=16,'gy'=32] {'gx'}, dimensions={0} | all-to-all | bytes 524288 | tf_op jit(solution)/shard_map/all_to_all | solution.py:226
  50.6 0.2 share.1
  50.8 14.4 %all_to_all.15 = bf16[16,16,512]{2,1,0:T(8,128)(2,1)S(1)} all-to-all(bf16[16,16,512]{2,1,0:T(8,128)(2,1)S(1)} %share.1), channel_id=1, replica_groups=mesh['gx'=16,'gy'=32] {'gx'}, dimensions={0} | all-to-all | bytes 524288 | tf_op jit(solution)/shard_map/all_to_all | solution.py:231
  65.2 2.4 %collective-permute-start.5 = (bf16[256,512]{1,0:T(8,128)(2,1)S(1)}, bf16[256,512]{1,0:T(8,128)(2,1)S(1)}, u32[]{:S(2)}, u32[]{:S(2)}) collective-permute-start(bf16[256,512]{1,0:T(8,128)(2,1)S(1)} %bitcast.12), channel_id=1, source_target_pairs={{1,0},{2,1},{3,2},{4,3},{5,4},{6,5},{7,6},{8,7},{9,8},{10,9},{11,1... | collective-permute-start | bytes 786440 | tf_op jit(solution)/shard_map/ppermute | solution.py:232
  67.6 3.5 %collective-permute-start.4 = (bf16[256,512]{1,0:T(8,128)(2,1)S(1)}, bf16[256,512]{1,0:T(8,128)(2,1)S(1)}, u32[]{:S(2)}, u32[]{:S(2)}) collective-permute-start(bf16[256,512]{1,0:T(8,128)(2,1)S(1)} %bitcast.13), channel_id=1, source_target_pairs={{0,1},{1,2},{2,3},{3,4},{4,5},{5,6},{6,7},{7,8},{8,9},{9,10},{10,1... | collective-permute-start | bytes 786440 | tf_op jit(solution)/shard_map/ppermute | solution.py:232
  71.2 3.4 %own_column.1 = (f32[1024,512]{1,0:T(8,128)S(1)}, f32[256,512]{1,0:T(8,128)S(1)}, f32[512,512]{1,0:T(8,128)S(1)}) custom-call(bf16[256,512]{1,0:T(8,128)(2,1)S(1)} %bitcast.14, s32[8,128]{1,0:T(8,128)S(1)} %bitcast.23, s32[8,128]{1,0:T(8,128)S(1)} %bitcast.25, bf16[512,512]{1,0:T(8,128)(2,1)S(1)} %get-tuple-element.27.level_one, ...), custom_call_target="tpu_custom_call" | custom-call | flops 1342177280 | bytes 3940352 | tf_op jit(solution)/shard_map/own_column/pallas_call | solution.py:172
  74.6 1.7 %collective-permute-done.5.right = bf16[256,512]{1,0:T(8,128)(2,1)S(1)} collective-permute-done((bf16[256,512]{1,0:T(8,128)(2,1)S(1)}, bf16[256,512]{1,0:T(8,128)(2,1)S(1)}, u32[]{:S(2)}, u32[]{:S(2)}) %collective-permute-start.5) | collective-permute-done | bytes 262176 | tf_op jit(solution)/shard_map/ppermute | solution.py:232
  76.3 5.4 %collective-permute-done.4.left = bf16[256,512]{1,0:T(8,128)(2,1)S(1)} collective-permute-done((bf16[256,512]{1,0:T(8,128)(2,1)S(1)}, bf16[256,512]{1,0:T(8,128)(2,1)S(1)}, u32[]{:S(2)}, u32[]{:S(2)}) %collective-permute-start.4) | collective-permute-done | bytes 262176 | tf_op jit(solution)/shard_map/ppermute | solution.py:232
  81.7 7.5 %coarse.1 = bf16[512,512]{1,0:T(8,128)(2,1)} custom-call(bf16[256,512]{1,0:T(8,128)(2,1)S(1)} %collective-permute-done.4.left, bf16[256,512]{1,0:T(8,128)(2,1)S(1)} %collective-permute-done.5.right, bf16[256,512]{1,0:T(8,128)(2,1)S(1)} %bitcast.15, f32[1024,512]{1,0:T(8,128)S(1)} %get-tuple-element.28.pre, f32[256,512]{1,0:T(8,128)S(1)} %get-tuple-element.29.node_pre, ...), custom_call_target="tpu_custom_call" | custom-call | flops 2415919104 | bytes 9713664 | tf_op jit(solution)/shard_map/coarse/pallas_call | solution.py:172
  (34 shorter events, 0.1 us)
Async XLA Ops:
  0.6 1.0 %copy-start.1 = (bf16[512,512]{1,0:T(8,128)(2,1)S(1)}, bf16[512,512]{1,0:T(8,128)(2,1)}, u32[]{:S(2)}) copy-start(bf16[512,512]{1,0:T(8,128)(2,1)} %nodes.7) | copy-start | bytes 1572868
  1.7 0.7 copy-start.16
  2.4 4.9 %copy-start = (bf16[1536,512]{1,0:T(8,128)(2,1)S(1)}, bf16[1536,512]{1,0:T(8,128)(2,1)}, u32[]{:S(2)}) copy-start(bf16[1536,512]{1,0:T(8,128)(2,1)} %w_in.5) | copy-start | bytes 4718596
  2.4 4.9 %copy-start.8 = (s32[1024]{0:T(1024)S(1)}, s32[1024]{0:T(1024)}, u32[]{:S(2)}) copy-start(s32[1024]{0:T(1024)} %param.24) | copy-start | bytes 12292
  2.4 4.9 %copy-start.9 = (s32[1024]{0:T(1024)S(1)}, s32[1024]{0:T(1024)}, u32[]{:S(2)}) copy-start(s32[1024]{0:T(1024)} %param.25) | copy-start | bytes 12292
  2.8 6.4 %collective-permute-start = (bf16[96,512]{1,0:T(8,128)(2,1)S(1)}, bf16[96,512]{1,0:T(8,128)(2,1)S(1)}, u32[]{:S(2)}, u32[]{:S(2)}) collective-permute-start(bf16[96,512]{1,0:T(8,128)(2,1)S(1)} %get-tuple-element.17), channel_id=1, source_target_pairs={{32,0},{64,32},{96,64},{128,96},{160,128},{192,160},{224,192},{256... | collective-permute-start | bytes 294920 | tf_op jit(solution)/shard_map/ppermute | solution.py:208
  4.2 5.0 %collective-permute-start.1 = (bf16[96,512]{1,0:T(8,128)(2,1)S(1)}, bf16[96,512]{1,0:T(8,128)(2,1)S(1)}, u32[]{:S(2)}, u32[]{:S(2)}) collective-permute-start(bf16[96,512]{1,0:T(8,128)(2,1)S(1)} %get-tuple-element.18), channel_id=1, source_target_pairs={{0,32},{32,64},{64,96},{96,128},{128,160},{160,192},{192,224},{224... | collective-permute-start | bytes 294920 | tf_op jit(solution)/shard_map/ppermute | solution.py:209
  9.3 9.1 %collective-permute-start.2 = (bf16[96,512]{1,0:T(8,128)(2,1)S(1)}, bf16[96,512]{1,0:T(8,128)(2,1)S(1)}, u32[]{:S(2)}, u32[]{:S(2)}) collective-permute-start(bf16[96,512]{1,0:T(8,128)(2,1)S(1)} %pad_maximum_fusion), channel_id=1, source_target_pairs={{1,0},{2,1},{3,2},{4,3},{5,4},{6,5},{7,6},{8,7},{9,8},{10,9},{11,1... | collective-permute-start | bytes 294920 | tf_op jit(solution)/shard_map/ppermute | solution.py:214
  13.0 11.0 %copy-start.5 = (bf16[512,512]{1,0:T(8,128)(2,1)S(1)}, bf16[512,512]{1,0:T(8,128)(2,1)}, u32[]{:S(2)}) copy-start(bf16[512,512]{1,0:T(8,128)(2,1)} %w_out.1) | copy-start | bytes 1572868
  13.1 11.0 %copy-start.6 = (bf16[512,512]{1,0:T(8,128)(2,1)S(1)}, bf16[512,512]{1,0:T(8,128)(2,1)}, u32[]{:S(2)}) copy-start(bf16[512,512]{1,0:T(8,128)(2,1)} %w_node_out.1) | copy-start | bytes 1572868
  13.1 11.0 %copy-start.7 = (s32[512]{0:T(512)S(1)}, s32[512]{0:T(512)}, u32[]{:S(2)}) copy-start(s32[512]{0:T(512)} %param.27) | copy-start | bytes 6148
  13.1 11.0 %copy-start.14 = (f32[512]{0:T(512)S(1)}, f32[512]{0:T(512)}, u32[]{:S(2)}) copy-start(f32[512]{0:T(512)} %param.32) | copy-start | bytes 6148
  13.1 11.0 %copy-start.15 = (f32[512]{0:T(512)S(1)}, f32[512]{0:T(512)}, u32[]{:S(2)}) copy-start(f32[512]{0:T(512)} %param.35) | copy-start | bytes 6148
  13.1 11.0 %collective-permute-start.3 = (bf16[96,512]{1,0:T(8,128)(2,1)S(1)}, bf16[96,512]{1,0:T(8,128)(2,1)S(1)}, u32[]{:S(2)}, u32[]{:S(2)}) collective-permute-start(bf16[96,512]{1,0:T(8,128)(2,1)S(1)} %pad_maximum_fusion.1), channel_id=1, source_target_pairs={{0,1},{1,2},{2,3},{3,4},{4,5},{5,6},{6,7},{7,8},{8,9},{9,10},{10,1... | collective-permute-start | bytes 294920 | tf_op jit(solution)/shard_map/ppermute | solution.py:215
  24.1 47.0 %copy-start.2 = (bf16[1024,512]{1,0:T(8,128)(2,1)S(1)}, bf16[1024,512]{1,0:T(8,128)(2,1)}, u32[]{:S(2)}) copy-start(bf16[1024,512]{1,0:T(8,128)(2,1)} %w_cin.3) | copy-start | bytes 3145732
  24.1 47.0 %copy-start.10 = (s32[1024]{0:T(1024)S(1)}, s32[1024]{0:T(1024)}, u32[]{:S(2)}) copy-start(s32[1024]{0:T(1024)} %param.28) | copy-start | bytes 12292
  24.1 47.0 %copy-start.11 = (s32[1024]{0:T(1024)S(1)}, s32[1024]{0:T(1024)}, u32[]{:S(2)}) copy-start(s32[1024]{0:T(1024)} %param.29) | copy-start | bytes 12292
  65.2 11.0 %collective-permute-start.5 = (bf16[256,512]{1,0:T(8,128)(2,1)S(1)}, bf16[256,512]{1,0:T(8,128)(2,1)S(1)}, u32[]{:S(2)}, u32[]{:S(2)}) collective-permute-start(bf16[256,512]{1,0:T(8,128)(2,1)S(1)} %bitcast.12), channel_id=1, source_target_pairs={{1,0},{2,1},{3,2},{4,3},{5,4},{6,5},{7,6},{8,7},{9,8},{10,9},{11,1... | collective-permute-start | bytes 786440 | tf_op jit(solution)/shard_map/ppermute | solution.py:232
  67.6 14.1 %collective-permute-start.4 = (bf16[256,512]{1,0:T(8,128)(2,1)S(1)}, bf16[256,512]{1,0:T(8,128)(2,1)S(1)}, u32[]{:S(2)}, u32[]{:S(2)}) collective-permute-start(bf16[256,512]{1,0:T(8,128)(2,1)S(1)} %bitcast.13), channel_id=1, source_target_pairs={{0,1},{1,2},{2,3},{3,4},{4,5},{5,6},{6,7},{7,8},{8,9},{9,10},{10,1... | collective-permute-start | bytes 786440 | tf_op jit(solution)/shard_map/ppermute | solution.py:232
  71.1 10.6 %copy-start.3 = (bf16[512,512]{1,0:T(8,128)(2,1)S(1)}, bf16[512,512]{1,0:T(8,128)(2,1)}, u32[]{:S(2)}) copy-start(bf16[512,512]{1,0:T(8,128)(2,1)} %w_cout.1) | copy-start | bytes 1572868
  71.1 10.6 %copy-start.4 = (bf16[512,512]{1,0:T(8,128)(2,1)S(1)}, bf16[512,512]{1,0:T(8,128)(2,1)}, u32[]{:S(2)}) copy-start(bf16[512,512]{1,0:T(8,128)(2,1)} %w_nout.1) | copy-start | bytes 1572868
  71.1 10.6 %copy-start.12 = (f32[512]{0:T(512)S(1)}, f32[512]{0:T(512)}, u32[]{:S(2)}) copy-start(f32[512]{0:T(512)} %param.40) | copy-start | bytes 6148
  71.2 10.6 %copy-start.13 = (f32[512]{0:T(512)S(1)}, f32[512]{0:T(512)}, u32[]{:S(2)}) copy-start(f32[512]{0:T(512)} %param.43) | copy-start | bytes 6148

commit v3 on v2

v3 whole, which is shorter than its diff:
```python
import jax
import jax.numpy as jnp
from jax import lax
from jax.experimental import pallas as pl
from jax.experimental.pallas import tpu as pltpu
from jax.sharding import PartitionSpec as P

COARSE = 256
BF16 = jnp.bfloat16
F32 = jnp.float32
I32 = jnp.int32


def dot(a, b):
    return jnp.dot(a, b, preferred_element_type=F32)


def silu(v):
    half = 0.5 * v
    return half + half * jnp.tanh(half)


def layer_norm(values):
    mean = jnp.mean(values, axis=-1, keepdims=True)
    centred = values - mean
    spread = jnp.mean(centred * centred, axis=-1, keepdims=True)
    return centred * lax.rsqrt(spread + 1e-05)


def mlp_tail(pre, w_out, gain):
    return layer_norm(dot(silu(pre).astype(BF16), w_out)) * gain


def pick(column, width, base=0):
    lanes = lax.broadcasted_iota(I32, (column.shape[0], width), 1) + base
    return jnp.where(lanes == column, 1.0, 0.0).astype(BF16)


def spread(row, height):
    rows = lax.broadcasted_iota(I32, (height, row.shape[1]), 0)
    return jnp.where(rows == row, 1.0, 0.0).astype(BF16)


def as_column(table):
    turned = jnp.transpose(table)
    return jnp.concatenate([turned[:, k : k + 1] for k in range(table.shape[0])], 0)


def as_row(table):
    return jnp.concatenate([table[k : k + 1, :] for k in range(table.shape[0])], 1)


def odd_place():
    return lax.axis_index("gx") % 2 == 1, lax.axis_index("gy") % 2 == 1


def fetch(sems, *pairs):
    copies = [pltpu.make_async_copy(a, b, sems.at[k]) for k, (a, b) in enumerate(pairs)]
    for copy in copies:
        copy.start()
    return copies


def outgoing_kernel(nodes_hbm, lists_hbm, far, before, after, near, nodes, lists, sems):
    got_lists, got_nodes = fetch(sems, (lists_hbm, lists), (nodes_hbm, nodes))
    got_lists.wait()
    odd_x, odd_y = odd_place()
    rows = lists[...]
    rows = jnp.where(odd_x, jnp.concatenate([rows[5:8], rows[3:5], rows[0:3]], 0), rows)
    rows = jnp.where(odd_y, jnp.concatenate([rows[k : k + 1] for k in (2, 1, 0, 4, 3, 7, 6, 5)], 0), rows)
    picks = jnp.transpose(rows)
    picks = jnp.concatenate([pick(picks[:, k : k + 1], 512) for k in range(8)], 0)
    got_nodes.wait()
    picked = dot(picks, nodes[...]).astype(BF16)
    far[...] = picked[0:96, :]
    before[...] = picked[96:128, :]
    after[...] = picked[128:160, :]
    near[...] = picked[160:256, :]


def tables_kernel(nodes, src, dst, w_in, gathered):
    nodes = nodes[...]
    src_proj = dot(nodes, w_in[512:1024, :]).astype(BF16)
    dst_proj = dot(nodes, w_in[1024:1536, :]).astype(BF16)
    part = dot(pick(as_column(src[...]), 512), src_proj)
    gathered[...] = part + dot(pick(as_column(dst[...]), 512), dst_proj)


def edges_kernel(
    nodes, gathered, edges_hbm, w_in_hbm, w_node_hbm, pre, node_pre, edges, w_source, w_summed, w_in, w_node, sems
):
    got = fetch(
        sems, (w_node_hbm.at[0:512], w_node), (w_in_hbm.at[0:512], w_in),
        (edges_hbm.at[0:512], edges.at[0:512]), (edges_hbm.at[512:1024], edges.at[512:1024]),
        (w_in_hbm.at[512:1024], w_source), (w_node_hbm.at[512:1024], w_summed),
    )
    got[0].wait()
    node_pre[...] = dot(nodes[...], w_node[...])
    got[1].wait()
    for c in range(2):
        rows = slice(512 * c, 512 * c + 512)
        got[2 + c].wait()
        pre[rows, :] = gathered[rows, :] + dot(edges[rows, :], w_in[...])
    got[4].wait()
    got[5].wait()


def after_halo_kernel(
    far, near, side_a, side_b, pre, node_pre, nodes, edges, src, dst, parents,
    w_source, w_out, gain, w_summed, w_node_out, node_gain,
    edges_hbm, level_one, pooled, edges_out, sems,
):
    received = jnp.concatenate(
        [
            side_a[64:96, :], near[32:64, :], side_b[64:96, :], side_a[32:64, :],
            side_b[32:64, :], side_a[0:32, :], far[32:64, :], side_b[0:32, :],
        ],
        0,
    )
    halo = dot(received, w_source[...]).astype(BF16)
    odd_x, odd_y = odd_place()
    slot = src[...] - 512
    k = slot >> 5
    turn_x = jnp.where(k < 3, k + 5, jnp.where(k > 4, k - 5, k))
    k = jnp.where(odd_x, turn_x, k)
    turn_y = jnp.where(
        (k == 0) | (k == 5), k + 2, jnp.where((k == 2) | (k == 7), k - 2, jnp.where(k == 3, 4, jnp.where(k == 4, 3, k)))
    )
    k = jnp.where(odd_y, turn_y, k)
    slot = jnp.where(slot < 0, -1, k * 32 + (slot & 31))
    part = pre[...] + dot(pick(as_column(slot), 256), halo)
    message = mlp_tail(part, w_out[...], gain[...])
    edges_out[...] = (edges[...].astype(F32) + message).astype(BF16)
    (sent,) = fetch(sems, (edges_out, edges_hbm))
    summed = dot(spread(as_row(dst[...]), 512), message.astype(BF16)).astype(BF16)
    part = node_pre[...] + dot(summed, w_summed[...])
    level = nodes[...].astype(F32) + mlp_tail(part, w_node_out[...], node_gain[...])
    level = level.astype(BF16)
    level_one[...] = level
    pooled[...] = dot(spread(as_row(parents[...]), COARSE), level).astype(BF16)
    sent.wait()


def share_kernel(parts, out):
    total = parts[0].astype(F32)
    for k in range(1, parts.shape[0]):
        total = total + parts[k].astype(F32)
    share = layer_norm(total).astype(BF16)
    for k in range(out.shape[0]):
        out[k] = share


def own_kernel(
    zero, csrc, cdst, level_one, w_cin, w_cin_hbm, w_nin_hbm, w_up_hbm, w_up_out_hbm,
    pre, node_pre, up_pre, w_source, w_summed, w_lifted, w_up_out, w_nin, w_up, sems,
):
    got = fetch(
        sems, (w_nin_hbm.at[0:512], w_nin), (w_up_hbm.at[0:512], w_up), (w_cin_hbm.at[0:512], w_source),
        (w_nin_hbm.at[512:1024], w_summed), (w_up_hbm.at[512:1024], w_lifted), (w_up_out_hbm, w_up_out),
    )
    zero = zero[...]
    side_src = dot(zero, w_cin[0:512, :]).astype(BF16)
    side_dst = dot(zero, w_cin[512:1024, :]).astype(BF16)
    part = dot(pick(as_column(csrc[...]), COARSE, COARSE), side_src)
    pre[...] = part + dot(pick(as_column(cdst[...]), COARSE), side_dst)
    got[0].wait()
    node_pre[...] = dot(zero, w_nin[...])
    got[1].wait()
    up_pre[...] = dot(level_one[...], w_up[...])
    for copy in got[2:]:
        copy.wait()


def coarse_kernel(
    left, right, zero, pre, node_pre, up_pre, csrc, cdst, parents, level_one,
    w_source, w_cout, w_summed, w_nout, coarse_gain, w_lifted, w_up_out, up_gain,
    out_hbm, out, sems,
):
    sides = dot(jnp.concatenate([left[...], right[...]], 0), w_source[...]).astype(BF16)
    src = csrc[...]
    src = jnp.where(src < COARSE, src, jnp.where(src < 2 * COARSE, -1, src - COARSE))
    part = pre[...] + dot(pick(as_column(src), 2 * COARSE), sides)
    message = layer_norm(dot(silu(part).astype(BF16), w_cout[...]))
    summed = dot(spread(as_row(cdst[...]), COARSE), message.astype(BF16)).astype(BF16)
    part = node_pre[...] + dot(summed, w_summed[...])
    one = (zero[...].astype(F32) + mlp_tail(part, w_nout[...], coarse_gain[...])).astype(BF16)
    lifted = dot(pick(as_column(parents[...]), COARSE), one).astype(BF16)
    part = up_pre[...] + dot(lifted, w_lifted[...])
    tail = mlp_tail(part, w_up_out[...], up_gain[...])
    out[...] = (level_one[...].astype(F32) + tail).astype(BF16)
    (sent,) = fetch(sems, (out, out_hbm))
    sent.wait()


def kept(shape, dtype):
    return pltpu.VMEM(shape, dtype)


def hold(array):
    return pltpu.with_memory_space_constraint(array, pltpu.VMEM)


def call(kernel, outs, *args, hbm=(), hbm_outs=(), held=(), scratch=(), copies=0, flops=0, name=None):
    shapes = [kept(s, d) if k in held else jax.ShapeDtypeStruct(s, d) for k, (s, d) in enumerate(outs)]
    args = list(args)
    hbm = [pltpu.with_memory_space_constraint(a, pltpu.HBM) for a in hbm]
    moved = sum(a.size * a.dtype.itemsize for a in args + hbm)
    vmem, far = pl.BlockSpec(memory_space=pltpu.VMEM), pl.BlockSpec(memory_space=pl.ANY)
    result = pl.pallas_call(
        kernel,
        out_shape=shapes,
        in_specs=[vmem] * len(args) + [far] * len(hbm),
        out_specs=[far if k in hbm_outs else vmem for k in range(len(shapes))],
        scratch_shapes=list(scratch) + ([pltpu.SemaphoreType.DMA((copies,))] if copies else []),
        compiler_params=pltpu.CompilerParams(vmem_limit_bytes=20 * 1024 * 1024),
        cost_estimate=pl.CostEstimate(flops=flops, bytes_accessed=moved, transcendentals=0),
        name=name,
    )(*args, *hbm)
    return result if len(result) > 1 else result[0]


def steps(count):
    up = [(k, k + 1) for k in range(count - 1)]
    return up, [(b, a) for a, b in up]


def trades(count):
    even = [(k, k ^ 1) for k in range(count)]
    return even, [(k, ((k - 1) ^ 1) + 1) for k in range(1, count - 1)]


def per_device(
    fine_nodes, fine_edges, edge_src, edge_dst, send_rows, parents, coarse_src, coarse_dst,
    w_edge_in, w_edge_out, edge_gain, w_node_in, w_node_out, node_gain, w_cedge_in, w_cedge_out,
    w_cnode_in, w_cnode_out, coarse_gain, w_up_in, w_up_out, up_gain,
):
    count_x, count_y = lax.axis_size("gx"), lax.axis_size("gy")
    src, dst = edge_src.reshape(8, 128), edge_dst.reshape(8, 128)
    csrc, cdst = coarse_src.reshape(8, 128), coarse_dst.reshape(8, 128)
    owner = parents.reshape(4, 128)
    edge_gain, node_gain = edge_gain.reshape(1, 512), node_gain.reshape(1, 512)
    coarse_gain, up_gain = coarse_gain.reshape(1, 512), up_gain.reshape(1, 512)
    block = pltpu.VMEM((512, 512), BF16)

    far, before, after, near = call(
        outgoing_kernel, [((96, 512), BF16), ((32, 512), BF16), ((32, 512), BF16), ((96, 512), BF16)],
        hbm=(fine_nodes, send_rows[0]), scratch=[block, pltpu.VMEM((8, 32), I32)], copies=2,
        flops=100 * 2 * 256 * 512 * 512, name="outgoing",
    )
    even_x, odd_x = trades(count_x)
    even_y, odd_y = trades(count_y)
    far = lax.ppermute(far, "gx", odd_x)
    near = lax.ppermute(near, "gx", even_x)
    gathered = call(
        tables_kernel, [((1024, 512), F32)], fine_nodes, src, dst, w_edge_in, held=(0,),
        flops=2 * 6 * 512**3, name="tables",
    )
    far, near, gathered = lax.optimization_barrier((far, near, gathered))
    side_a = lax.ppermute(jnp.concatenate([far[64:96], after, near[64:96]], 0), "gy", even_y)
    side_b = lax.ppermute(jnp.concatenate([far[0:32], before, near[0:32]], 0), "gy", odd_y)
    square = ((512, 512), BF16)
    pre, node_pre, edges, w_source, w_summed = call(
        edges_kernel, [((1024, 512), F32), ((512, 512), F32), ((1024, 512), BF16), square, square],
        fine_nodes, hold(gathered), hbm=(fine_edges, w_edge_in, w_node_in), held=(0, 1, 2, 3, 4),
        scratch=[block, block], copies=6, flops=2 * 3 * 512**3, name="edges",
    )
    edges_out, level_one, pooled = call(
        after_halo_kernel, [((1024, 512), BF16), square, ((COARSE, 512), BF16)],
        far, near, side_a, side_b, hold(pre), hold(node_pre), fine_nodes, hold(edges), src, dst, owner,
        hold(w_source), w_edge_out, edge_gain, hold(w_summed), w_node_out, node_gain,
        hbm_outs=(0,), scratch=[pltpu.VMEM((1024, 512), BF16)], copies=1, flops=2 * 8 * 512**3, name="after_halo",
    )
    parts = lax.all_to_all(pooled, "gx", 0, 0, tiled=True)
    shares = call(
        share_kernel, [((count_x, COARSE // count_x, 512), BF16)], parts.reshape(count_x, -1, 512),
        flops=COARSE * 512, name="share",
    )
    zero = lax.all_to_all(shares, "gx", 0, 0, tiled=True).reshape(COARSE, 512)
    up_y, down_y = steps(count_y)
    left, right = lax.ppermute(zero, "gy", up_y), lax.ppermute(zero, "gy", down_y)
    pre, node_pre, up_pre, w_source, w_summed, w_lifted, w_last = call(
        own_kernel, [((1024, 512), F32), ((COARSE, 512), F32), ((512, 512), F32)] + [square] * 4,
        zero, csrc, cdst, level_one, w_cedge_in, hbm=(w_cedge_in, w_cnode_in, w_up_in, w_up_out),
        held=range(7), scratch=[block, block], copies=6, flops=2 * 5 * 512**3, name="own_column",
    )
    fine_out = call(
        coarse_kernel, [square],
        left, right, zero, hold(pre), hold(node_pre), hold(up_pre), csrc, cdst, owner, level_one,
        hold(w_source), w_cedge_out, hold(w_summed), w_cnode_out, coarse_gain, hold(w_lifted), hold(w_last), up_gain,
        hbm_outs=(0,), scratch=[block], copies=1, flops=2 * 9 * 512**3, name="coarse",
    )
    return fine_out, edges_out


def solution(mesh):
    fine, flat = P(("gx", "gy"), None), P(("gx", "gy"))
    return jax.shard_map(
        per_device,
        mesh=mesh,
        in_specs=(fine, fine, flat, flat, P(("gx", "gy"), None, None), flat, P("gy"), P("gy")) + (P(),) * 14,
        out_specs=(fine, fine),
        check_vma=False,
    )
```

time: 89.7 us -> 83.1 us (0.926)
  Pallas kernels: 23 us -> 19.3 us
  blocking collectives: 34.4 us -> 32.2 us
  local copies, waits for them, and re-layouts: 1.82 us -> 0.1 us
  starting transfers between devices: 16.3 us -> 18 us
    pallas_call x7, Pallas kernels: 23 us -> 19.3 us  [call(): pl.pallas_call(kernel, out_shape=shapes, in_specs=[vmem] * len(args) + [f...]
    all_to_all x1, blocking collectives: 20 us -> 17.8 us  [per_device(): parts = lax.all_to_all(pooled, 'gx', 0, 0, tiled=True)]
    unnamed x34 -> x30, local copies, waits for them, and re-layouts: 1.81 us -> 0.09 us
    ppermute x4, starting transfers between devices: 10.4 us -> 12.1 us  [the longest x1 4.84 us: per_device(): near = lax.ppermute(near, 'gx', even_x)]
    ppermute x4, waiting for transfers between devices: 5.72 us -> 4.3 us  [the longest x1 4.29 us: per_device(): lax.ppermute(jnp.concatenate([far[0:32], before, near[0:32]], 0), 'gy', o...]
where the time goes in v3:
time: 83.1 us; the launch traced here: 82.8 us
  blocking collectives  32.2 us (39%)
  Pallas kernels  19.3 us (23%)
  starting transfers between devices  18 us (22%)
  waiting for transfers between devices  12.2 us (15%)
  between operations  0.97 us (1%)
    pallas_call x7, Pallas kernels, call(): pl.pallas_call(kernel, out_shape=shapes, in_specs=[vmem] * len(args) + [f...  19.3 us
    all_to_all x1, blocking collectives, per_device(): parts = lax.all_to_all(pooled, 'gx', 0, 0, tiled=True)  17.8 us
    all_to_all x1, blocking collectives, per_device(): zero = lax.all_to_all(shares, 'gx', 0, 0, tiled=True).reshape(COARSE, 512)  14.4 us
    ppermute x1, waiting for transfers between devices, per_device(): lax.ppermute(zero, 'gy', up_y)  6.13 us
    ppermute x1, starting transfers between devices, per_device(): near = lax.ppermute(near, 'gx', even_x)  4.84 us
    ppermute x1, waiting for transfers between devices, per_device(): lax.ppermute(jnp.concatenate([far[0:32], before, near[0:32]], 0), 'gy', o...  4.29 us
    ppermute x1, starting transfers between devices, per_device(): lax.ppermute(jnp.concatenate([far[64:96], after, near[64:96]], 0), 'gy',...  3.4 us
    ppermute x1, starting transfers between devices, per_device(): lax.ppermute(jnp.concatenate([far[0:32], before, near[0:32]], 0), 'gy', o...  3.23 us
  transfers between devices with their start and end apart: 6, of which 3 were waited for; matrix products, arithmetic and copies ran while one was open for 0% of the time, Pallas kernels for 9%

profile of v3, /device:TPU:256, one launch (start us, length us, event | category | flops | bytes accessed | tf_op | source)
XLA Modules:
  0.0 82.8 jit_solution(2324149866672374304)
XLA Ops:
  0.6 0.0 copy-start
  0.7 1.5 %outgoing.1 = (bf16[96,512]{1,0:T(8,128)(2,1)S(1)}, bf16[32,512]{1,0:T(8,128)(2,1)S(1)}, bf16[32,512]{1,0:T(8,128)(2,1)S(1)}, bf16[96,512]{1,0:T(8,128)(2,1)S(1)}) custom-call(bf16[512,512]{1,0:T(8,128)(2,1)} %nodes.5, s32[8,32]{1,0:T(8,128)} %bitcast.31), custom_call_target="tpu_custom_call" | custom-call | flops 13421772800 | bytes 525312 | tf_op jit(solution)/shard_map/outgoing/pallas_call | solution.py:209
  2.2 0.7 collective-permute-start
  2.9 4.8 %collective-permute-start.1 = (bf16[96,512]{1,0:T(8,128)(2,1)S(1)}, bf16[96,512]{1,0:T(8,128)(2,1)S(1)}, u32[]{:S(2)}, u32[]{:S(2)}) collective-permute-start(bf16[96,512]{1,0:T(8,128)(2,1)S(1)} %get-tuple-element.25), channel_id=1, source_target_pairs={{0,32},{32,0},{64,96},{96,64},{128,160},{160,128},{192,224},{224,1... | collective-permute-start | bytes 294920 | tf_op jit(solution)/shard_map/ppermute | solution.py:253
  7.8 1.9 %tables.1.gathered = f32[1024,512]{1,0:T(8,128)S(1)} custom-call(bf16[512,512]{1,0:T(8,128)(2,1)S(1)} %copy-done.1, s32[8,128]{1,0:T(8,128)S(1)} %bitcast.21, s32[8,128]{1,0:T(8,128)S(1)} %bitcast.23, bf16[1536,512]{1,0:T(8,128)(2,1)S(1)} %copy-done), custom_call_target="tpu_custom_call" | custom-call | flops 1610612736 | bytes 2105344 | tf_op jit(solution)/shard_map/tables/pallas_call | solution.py:209
  9.7 3.4 %collective-permute-start.2 = (bf16[96,512]{1,0:T(8,128)(2,1)S(1)}, bf16[96,512]{1,0:T(8,128)(2,1)S(1)}, u32[]{:S(2)}, u32[]{:S(2)}) collective-permute-start(bf16[96,512]{1,0:T(8,128)(2,1)S(1)} %pad_maximum_fusion), channel_id=1, source_target_pairs={{0,1},{1,0},{2,3},{3,2},{4,5},{5,4},{6,7},{7,6},{8,9},{9,8},{10,11... | collective-permute-start | bytes 294920 | tf_op jit(solution)/shard_map/ppermute | solution.py:259
  13.2 0.0 copy-start.10
  13.2 0.0 copy-start.11
  13.2 3.2 %collective-permute-start.3 = (bf16[96,512]{1,0:T(8,128)(2,1)S(1)}, bf16[96,512]{1,0:T(8,128)(2,1)S(1)}, u32[]{:S(2)}, u32[]{:S(2)}) collective-permute-start(bf16[96,512]{1,0:T(8,128)(2,1)S(1)} %pad_maximum_fusion.1), channel_id=1, source_target_pairs={{1,2},{2,1},{3,4},{4,3},{5,6},{6,5},{7,8},{8,7},{9,10},{10,9},{11,... | collective-permute-start | bytes 294920 | tf_op jit(solution)/shard_map/ppermute | solution.py:260
  16.5 2.4 %edges.1 = (f32[1024,512]{1,0:T(8,128)S(1)}, f32[512,512]{1,0:T(8,128)S(1)}, bf16[1024,512]{1,0:T(8,128)(2,1)S(1)}, bf16[512,512]{1,0:T(8,128)(2,1)S(1)}, bf16[512,512]{1,0:T(8,128)(2,1)S(1)}) custom-call(bf16[512,512]{1,0:T(8,128)(2,1)S(1)} %copy-done.1, f32[1024,512]{1,0:T(8,128)S(1)} %tables.1.gathered, bf16[1024,512]{1,0:T(8,128)(2,1)} %edges_hbm.1, ...), custom_call_target="tpu_custom_call" | custom-call | flops 805306368 | bytes 6291456 | tf_op jit(solution)/shard_map/edges/pallas_call | solution.py:209
  18.9 4.3 %collective-permute-done.3.side_b = bf16[96,512]{1,0:T(8,128)(2,1)S(1)} collective-permute-done((bf16[96,512]{1,0:T(8,128)(2,1)S(1)}, bf16[96,512]{1,0:T(8,128)(2,1)S(1)}, u32[]{:S(2)}, u32[]{:S(2)}) %collective-permute-start.3) | collective-permute-done | bytes 98336 | tf_op jit(solution)/shard_map/ppermute | solution.py:260
  23.2 0.0 copy-start.3
  23.2 4.5 %after_halo.1 = (bf16[1024,512]{1,0:T(8,128)(2,1)}, bf16[512,512]{1,0:T(8,128)(2,1)S(1)}, bf16[256,512]{1,0:T(8,128)(2,1)S(1)}) custom-call(bf16[96,512]{1,0:T(8,128)(2,1)S(1)} %collective-permute-done.far, bf16[96,512]{1,0:T(8,128)(2,1)S(1)} %collective-permute-done.1.near, bf16[96,512]{1,0:T(8,128)(2,1)S(1)} %collective-permute-done.2.side_a, ...), custom_call_target="tpu_custom_call" | custom-call | flops 2147483648 | bytes 7223296 | tf_op jit(solution)/shard_map/after_halo/pallas_call | solution.py:209
  27.8 17.8 %all_to_all.14.parts = bf16[16,16,512]{2,1,0:T(8,128)(2,1)S(1)} all-to-all(bf16[16,16,512]{2,1,0:T(8,128)(2,1)S(1)} %bitcast.16), channel_id=1, replica_groups=mesh['gx'=16,'gy'=32] {'gx'}, dimensions={0} | all-to-all | bytes 524288 | tf_op jit(solution)/shard_map/all_to_all | solution.py:273
  45.6 0.2 share.1
  45.8 14.4 %all_to_all.15 = bf16[16,16,512]{2,1,0:T(8,128)(2,1)S(1)} all-to-all(bf16[16,16,512]{2,1,0:T(8,128)(2,1)S(1)} %share.1), channel_id=1, replica_groups=mesh['gx'=16,'gy'=32] {'gx'}, dimensions={0} | all-to-all | bytes 524288 | tf_op jit(solution)/shard_map/all_to_all | solution.py:278
  60.2 3.1 %collective-permute-start.5 = (bf16[256,512]{1,0:T(8,128)(2,1)S(1)}, bf16[256,512]{1,0:T(8,128)(2,1)S(1)}, u32[]{:S(2)}, u32[]{:S(2)}) collective-permute-start(bf16[256,512]{1,0:T(8,128)(2,1)S(1)} %bitcast.12), channel_id=1, source_target_pairs={{1,0},{2,1},{3,2},{4,3},{5,4},{6,5},{7,6},{8,7},{9,8},{10,9},{11,1... | collective-permute-start | bytes 786440 | tf_op jit(solution)/shard_map/ppermute | solution.py:280
  63.3 2.8 %collective-permute-start.4 = (bf16[256,512]{1,0:T(8,128)(2,1)S(1)}, bf16[256,512]{1,0:T(8,128)(2,1)S(1)}, u32[]{:S(2)}, u32[]{:S(2)}) collective-permute-start(bf16[256,512]{1,0:T(8,128)(2,1)S(1)} %bitcast.13), channel_id=1, source_target_pairs={{0,1},{1,2},{2,3},{3,4},{4,5},{5,6},{6,7},{7,8},{8,9},{9,10},{10,1... | collective-permute-start | bytes 786440 | tf_op jit(solution)/shard_map/ppermute | solution.py:280
  66.1 0.0 copy-start.6
  66.1 0.0 copy-start.7
  66.1 3.3 %own_column.1 = (f32[1024,512]{1,0:T(8,128)S(1)}, f32[256,512]{1,0:T(8,128)S(1)}, f32[512,512]{1,0:T(8,128)S(1)}, bf16[512,512]{1,0:T(8,128)(2,1)S(1)}, bf16[512...) custom-call(bf16[256,512]{1,0:T(8,128)(2,1)S(1)} %bitcast.14, ...), custom_call_target="tpu_custom_call" | custom-call | flops 1342177280 | bytes 5513216 | tf_op jit(solution)/shard_map/own_column/pallas_call | solution.py:209
  69.5 1.8 %collective-permute-done.5.right = bf16[256,512]{1,0:T(8,128)(2,1)S(1)} collective-permute-done((bf16[256,512]{1,0:T(8,128)(2,1)S(1)}, bf16[256,512]{1,0:T(8,128)(2,1)S(1)}, u32[]{:S(2)}, u32[]{:S(2)}) %collective-permute-start.5) | collective-permute-done | bytes 262176 | tf_op jit(solution)/shard_map/ppermute | solution.py:280
  71.3 6.1 %collective-permute-done.4.left = bf16[256,512]{1,0:T(8,128)(2,1)S(1)} collective-permute-done((bf16[256,512]{1,0:T(8,128)(2,1)S(1)}, bf16[256,512]{1,0:T(8,128)(2,1)S(1)}, u32[]{:S(2)}, u32[]{:S(2)}) %collective-permute-start.4) | collective-permute-done | bytes 262176 | tf_op jit(solution)/shard_map/ppermute | solution.py:280
  77.4 5.4 %coarse.1 = bf16[512,512]{1,0:T(8,128)(2,1)} custom-call(bf16[256,512]{1,0:T(8,128)(2,1)S(1)} %collective-permute-done.4.left, bf16[256,512]{1,0:T(8,128)(2,1)S(1)} %collective-permute-done.5.right, bf16[256,512]{1,0:T(8,128)(2,1)S(1)} %bitcast.15, f32[1024,512]{1,0:T(8,128)S(1)} %get-tuple-element.38.pre, f32[256,512]{1,0:T(8,128)S(1)} %get-tuple-element.39.node_pre, ...), custom_call_target="tpu_custom_call" | custom-call | flops 2415919104 | bytes 8140800 | tf_op jit(solution)/shard_map/coarse/pallas_call | solution.py:209
  (30 shorter events, 0.1 us)
Async XLA Ops:
  0.6 7.1 %copy-start = (bf16[1536,512]{1,0:T(8,128)(2,1)S(1)}, bf16[1536,512]{1,0:T(8,128)(2,1)}, u32[]{:S(2)}) copy-start(bf16[1536,512]{1,0:T(8,128)(2,1)} %w_in_hbm.1) | copy-start | bytes 4718596
  0.6 7.1 %copy-start.1 = (bf16[512,512]{1,0:T(8,128)(2,1)S(1)}, bf16[512,512]{1,0:T(8,128)(2,1)}, u32[]{:S(2)}) copy-start(bf16[512,512]{1,0:T(8,128)(2,1)} %nodes.5) | copy-start | bytes 1572868
  0.7 7.1 %copy-start.8 = (s32[1024]{0:T(1024)S(1)}, s32[1024]{0:T(1024)}, u32[]{:S(2)}) copy-start(s32[1024]{0:T(1024)} %param.24) | copy-start | bytes 12292
  0.7 7.1 %copy-start.9 = (s32[1024]{0:T(1024)S(1)}, s32[1024]{0:T(1024)}, u32[]{:S(2)}) copy-start(s32[1024]{0:T(1024)} %param.25) | copy-start | bytes 12292
  2.2 7.5 %collective-permute-start = (bf16[96,512]{1,0:T(8,128)(2,1)S(1)}, bf16[96,512]{1,0:T(8,128)(2,1)S(1)}, u32[]{:S(2)}, u32[]{:S(2)}) collective-permute-start(bf16[96,512]{1,0:T(8,128)(2,1)S(1)} %get-tuple-element.24), channel_id=1, source_target_pairs={{32,64},{64,32},{96,128},{128,96},{160,192},{192,160},{224,256},{2... | collective-permute-start | bytes 294920 | tf_op jit(solution)/shard_map/ppermute | solution.py:252
  2.9 6.8 %collective-permute-start.1 = (bf16[96,512]{1,0:T(8,128)(2,1)S(1)}, bf16[96,512]{1,0:T(8,128)(2,1)S(1)}, u32[]{:S(2)}, u32[]{:S(2)}) collective-permute-start(bf16[96,512]{1,0:T(8,128)(2,1)S(1)} %get-tuple-element.25), channel_id=1, source_target_pairs={{0,32},{32,0},{64,96},{96,64},{128,160},{160,128},{192,224},{224,1... | collective-permute-start | bytes 294920 | tf_op jit(solution)/shard_map/ppermute | solution.py:253
  9.7 9.2 %collective-permute-start.2 = (bf16[96,512]{1,0:T(8,128)(2,1)S(1)}, bf16[96,512]{1,0:T(8,128)(2,1)S(1)}, u32[]{:S(2)}, u32[]{:S(2)}) collective-permute-start(bf16[96,512]{1,0:T(8,128)(2,1)S(1)} %pad_maximum_fusion), channel_id=1, source_target_pairs={{0,1},{1,0},{2,3},{3,2},{4,5},{5,4},{6,7},{7,6},{8,9},{9,8},{10,11... | collective-permute-start | bytes 294920 | tf_op jit(solution)/shard_map/ppermute | solution.py:259
  13.2 10.0 %copy-start.4 = (bf16[512,512]{1,0:T(8,128)(2,1)S(1)}, bf16[512,512]{1,0:T(8,128)(2,1)}, u32[]{:S(2)}) copy-start(bf16[512,512]{1,0:T(8,128)(2,1)} %w_out.1) | copy-start | bytes 1572868
  13.2 10.0 %copy-start.5 = (bf16[512,512]{1,0:T(8,128)(2,1)S(1)}, bf16[512,512]{1,0:T(8,128)(2,1)}, u32[]{:S(2)}) copy-start(bf16[512,512]{1,0:T(8,128)(2,1)} %w_node_out.1) | copy-start | bytes 1572868
  13.2 10.0 %copy-start.10 = (f32[512]{0:T(512)S(1)}, f32[512]{0:T(512)}, u32[]{:S(2)}) copy-start(f32[512]{0:T(512)} %param.32) | copy-start | bytes 6148
  13.2 10.0 %copy-start.11 = (f32[512]{0:T(512)S(1)}, f32[512]{0:T(512)}, u32[]{:S(2)}) copy-start(f32[512]{0:T(512)} %param.35) | copy-start | bytes 6148
  13.2 10.0 %copy-start.12 = (s32[512]{0:T(512)S(1)}, s32[512]{0:T(512)}, u32[]{:S(2)}) copy-start(s32[512]{0:T(512)} %param.27) | copy-start | bytes 6148
  13.2 10.0 %collective-permute-start.3 = (bf16[96,512]{1,0:T(8,128)(2,1)S(1)}, bf16[96,512]{1,0:T(8,128)(2,1)S(1)}, u32[]{:S(2)}, u32[]{:S(2)}) collective-permute-start(bf16[96,512]{1,0:T(8,128)(2,1)S(1)} %pad_maximum_fusion.1), channel_id=1, source_target_pairs={{1,2},{2,1},{3,4},{4,3},{5,6},{6,5},{7,8},{8,7},{9,10},{10,9},{11,... | collective-permute-start | bytes 294920 | tf_op jit(solution)/shard_map/ppermute | solution.py:260
  23.2 42.9 %copy-start.2 = (s32[1024]{0:T(1024)S(1)}, s32[1024]{0:T(1024)}, u32[]{:S(2)}) copy-start(s32[1024]{0:T(1024)} %param.28) | copy-start | bytes 12292
  23.2 42.9 %copy-start.3 = (s32[1024]{0:T(1024)S(1)}, s32[1024]{0:T(1024)}, u32[]{:S(2)}) copy-start(s32[1024]{0:T(1024)} %param.29) | copy-start | bytes 12292
  60.2 11.0 %collective-permute-start.5 = (bf16[256,512]{1,0:T(8,128)(2,1)S(1)}, bf16[256,512]{1,0:T(8,128)(2,1)S(1)}, u32[]{:S(2)}, u32[]{:S(2)}) collective-permute-start(bf16[256,512]{1,0:T(8,128)(2,1)S(1)} %bitcast.12), channel_id=1, source_target_pairs={{1,0},{2,1},{3,2},{4,3},{5,4},{6,5},{7,6},{8,7},{9,8},{10,9},{11,1... | collective-permute-start | bytes 786440 | tf_op jit(solution)/shard_map/ppermute | solution.py:280
  63.3 14.1 %collective-permute-start.4 = (bf16[256,512]{1,0:T(8,128)(2,1)S(1)}, bf16[256,512]{1,0:T(8,128)(2,1)S(1)}, u32[]{:S(2)}, u32[]{:S(2)}) collective-permute-start(bf16[256,512]{1,0:T(8,128)(2,1)S(1)} %bitcast.13), channel_id=1, source_target_pairs={{0,1},{1,2},{2,3},{3,4},{4,5},{5,6},{6,7},{7,8},{8,9},{9,10},{10,1... | collective-permute-start | bytes 786440 | tf_op jit(solution)/shard_map/ppermute | solution.py:280
  66.1 11.3 %copy-start.6 = (bf16[512,512]{1,0:T(8,128)(2,1)S(1)}, bf16[512,512]{1,0:T(8,128)(2,1)}, u32[]{:S(2)}) copy-start(bf16[512,512]{1,0:T(8,128)(2,1)} %w_cout.1) | copy-start | bytes 1572868
  66.1 11.3 %copy-start.7 = (bf16[512,512]{1,0:T(8,128)(2,1)S(1)}, bf16[512,512]{1,0:T(8,128)(2,1)}, u32[]{:S(2)}) copy-start(bf16[512,512]{1,0:T(8,128)(2,1)} %w_nout.1) | copy-start | bytes 1572868
  66.1 11.3 %copy-start.13 = (f32[512]{0:T(512)S(1)}, f32[512]{0:T(512)}, u32[]{:S(2)}) copy-start(f32[512]{0:T(512)} %param.40) | copy-start | bytes 6148
  66.1 11.3 %copy-start.14 = (f32[512]{0:T(512)S(1)}, f32[512]{0:T(512)}, u32[]{:S(2)}) copy-start(f32[512]{0:T(512)} %param.43) | copy-start | bytes 6148

commit v4 on v3

--- a/solution.py
+++ b/solution.py
@@ -106,9 +106,9 @@
 
 
 def after_halo_kernel(
-    far, near, side_a, side_b, pre, node_pre, nodes, edges, src, dst, parents,
+    far, near, side_a, side_b, pre, node_pre, nodes, src, dst, parents,
     w_source, w_out, gain, w_summed, w_node_out, node_gain,
-    edges_hbm, level_one, pooled, edges_out, sems,
+    message_out, level_one, pooled,
 ):
     received = jnp.concatenate(
         [
@@ -130,15 +130,13 @@
     slot = jnp.where(slot < 0, -1, k * 32 + (slot & 31))
     part = pre[...] + dot(pick(as_column(slot), 256), halo)
     message = mlp_tail(part, w_out[...], gain[...])
-    edges_out[...] = (edges[...].astype(F32) + message).astype(BF16)
-    (sent,) = fetch(sems, (edges_out, edges_hbm))
+    message_out[...] = message
     summed = dot(spread(as_row(dst[...]), 512), message.astype(BF16)).astype(BF16)
     part = node_pre[...] + dot(summed, w_summed[...])
     level = nodes[...].astype(F32) + mlp_tail(part, w_node_out[...], node_gain[...])
     level = level.astype(BF16)
     level_one[...] = level
     pooled[...] = dot(spread(as_row(parents[...]), COARSE), level).astype(BF16)
-    sent.wait()
 
 
 def share_kernel(parts, out):
@@ -151,13 +149,15 @@
 
 
 def own_kernel(
-    zero, csrc, cdst, level_one, w_cin, w_cin_hbm, w_nin_hbm, w_up_hbm, w_up_out_hbm,
-    pre, node_pre, up_pre, w_source, w_summed, w_lifted, w_up_out, w_nin, w_up, sems,
+    zero, csrc, cdst, level_one, edges, message, w_cin, w_nin_hbm, w_up_hbm,
+    pre, node_pre, up_pre, w_summed, edges_hbm, w_nin, w_up, edges_out, sems,
 ):
     got = fetch(
-        sems, (w_nin_hbm.at[0:512], w_nin), (w_up_hbm.at[0:512], w_up), (w_cin_hbm.at[0:512], w_source),
-        (w_nin_hbm.at[512:1024], w_summed), (w_up_hbm.at[512:1024], w_lifted), (w_up_out_hbm, w_up_out),
-    )
+        sems, (w_nin_hbm.at[0:512], w_nin), (w_up_hbm.at[0:512], w_up), (w_nin_hbm.at[512:1024], w_summed)
+    )
+    edges_out[...] = (edges[...].astype(F32) + message[...]).astype(BF16)
+    sent = pltpu.make_async_copy(edges_out, edges_hbm, sems.at[3])
+    sent.start()
     zero = zero[...]
     side_src = dot(zero, w_cin[0:512, :]).astype(BF16)
     side_dst = dot(zero, w_cin[512:1024, :]).astype(BF16)
@@ -167,19 +167,34 @@
     node_pre[...] = dot(zero, w_nin[...])
     got[1].wait()
     up_pre[...] = dot(level_one[...], w_up[...])
-    for copy in got[2:]:
+    got[2].wait()
+    sent.wait()
+
+
+def first_is_right():
+    odd_x, odd_y = odd_place()
+    return odd_x == odd_y
+
+
+def side_rows(side, right, csrc, w_source):
+    side_src = dot(side[...], w_source[...]).astype(BF16)
+    base = jnp.where(right, 2 * COARSE, 0)
+    return dot(pick(as_column(csrc[...] - base), COARSE), side_src)
+
+
+def first_kernel(side, pre, csrc, w_cin, w_up_hbm, w_up_out_hbm, both, w_lifted, w_up_out, sems):
+    got = fetch(sems, (w_up_hbm.at[512:1024], w_lifted), (w_up_out_hbm, w_up_out))
+    both[...] = pre[...] + side_rows(side, first_is_right(), csrc, w_cin.at[0:512])
+    for copy in got:
         copy.wait()
 
 
 def coarse_kernel(
-    left, right, zero, pre, node_pre, up_pre, csrc, cdst, parents, level_one,
-    w_source, w_cout, w_summed, w_nout, coarse_gain, w_lifted, w_up_out, up_gain,
+    side, zero, pre, node_pre, up_pre, csrc, cdst, parents, level_one,
+    w_cin, w_cout, w_summed, w_nout, coarse_gain, w_lifted, w_up_out, up_gain,
     out_hbm, out, sems,
 ):
-    sides = dot(jnp.concatenate([left[...], right[...]], 0), w_source[...]).astype(BF16)
-    src = csrc[...]
-    src = jnp.where(src < COARSE, src, jnp.where(src < 2 * COARSE, -1, src - COARSE))
-    part = pre[...] + dot(pick(as_column(src), 2 * COARSE), sides)
+    part = pre[...] + side_rows(side, jnp.logical_not(first_is_right()), csrc, w_cin.at[0:512])
     message = layer_norm(dot(silu(part).astype(BF16), w_cout[...]))
     summed = dot(spread(as_row(cdst[...]), COARSE), message.astype(BF16)).astype(BF16)
     part = node_pre[...] + dot(summed, w_summed[...])
@@ -219,11 +234,6 @@
     return result if len(result) > 1 else result[0]
 
 
-def steps(count):
-    up = [(k, k + 1) for k in range(count - 1)]
-    return up, [(b, a) for a, b in up]
-
-
 def trades(count):
     even = [(k, k ^ 1) for k in range(count)]
     return even, [(k, ((k - 1) ^ 1) + 1) for k in range(1, count - 1)]
@@ -264,11 +274,11 @@
         fine_nodes, hold(gathered), hbm=(fine_edges, w_edge_in, w_node_in), held=(0, 1, 2, 3, 4),
         scratch=[block, block], copies=6, flops=2 * 3 * 512**3, name="edges",
     )
-    edges_out, level_one, pooled = call(
-        after_halo_kernel, [((1024, 512), BF16), square, ((COARSE, 512), BF16)],
-        far, near, side_a, side_b, hold(pre), hold(node_pre), fine_nodes, hold(edges), src, dst, owner,
+    message, level_one, pooled = call(
+        after_halo_kernel, [((1024, 512), F32), square, ((COARSE, 512), BF16)],
+        far, near, side_a, side_b, hold(pre), hold(node_pre), fine_nodes, src, dst, owner,
         hold(w_source), w_edge_out, edge_gain, hold(w_summed), w_node_out, node_gain,
-        hbm_outs=(0,), scratch=[pltpu.VMEM((1024, 512), BF16)], copies=1, flops=2 * 8 * 512**3, name="after_halo",
+        held=(0,), flops=2 * 8 * 512**3, name="after_halo",
     )
     parts = lax.all_to_all(pooled, "gx", 0, 0, tiled=True)
     shares = call(
@@ -276,18 +286,26 @@
         flops=COARSE * 512, name="share",
     )
     zero = lax.all_to_all(shares, "gx", 0, 0, tiled=True).reshape(COARSE, 512)
-    up_y, down_y = steps(count_y)
-    left, right = lax.ppermute(zero, "gy", up_y), lax.ppermute(zero, "gy", down_y)
-    pre, node_pre, up_pre, w_source, w_summed, w_lifted, w_last = call(
-        own_kernel, [((1024, 512), F32), ((COARSE, 512), F32), ((512, 512), F32)] + [square] * 4,
-        zero, csrc, cdst, level_one, w_cedge_in, hbm=(w_cedge_in, w_cnode_in, w_up_in, w_up_out),
-        held=range(7), scratch=[block, block], copies=6, flops=2 * 5 * 512**3, name="own_column",
+    sideways = [
+        (i * count_y + j, i * count_y + to) for i in range(count_x) for j, to in (odd_y if i % 2 else even_y)
+    ]
+    first = lax.ppermute(zero, ("gx", "gy"), sideways)
+    pre, node_pre, up_pre, w_summed, edges_out = call(
+        own_kernel, [((1024, 512), F32), ((COARSE, 512), F32), ((512, 512), F32), square, ((1024, 512), BF16)],
+        zero, csrc, cdst, level_one, hold(edges), hold(message), w_cedge_in, hbm=(w_cnode_in, w_up_in),
+        held=range(4), hbm_outs=(4,), scratch=[block, block, pltpu.VMEM((1024, 512), BF16)], copies=4, flops=2 * 5 * 512**3, name="own_column",
+    )
+    first, pre = lax.optimization_barrier((first, pre))
+    second = lax.ppermute(first, "gx", even_x)
+    pre, w_lifted, w_last = call(
+        first_kernel, [((1024, 512), F32), square, square], first, hold(pre), csrc, w_cedge_in,
+        hbm=(w_up_in, w_up_out), held=range(3), copies=2, flops=2 * 2 * 512**3, name="first_side",
     )
     fine_out = call(
         coarse_kernel, [square],
-        left, right, zero, hold(pre), hold(node_pre), hold(up_pre), csrc, cdst, owner, level_one,
-        hold(w_source), w_cedge_out, hold(w_summed), w_cnode_out, coarse_gain, hold(w_lifted), hold(w_last), up_gain,
-        hbm_outs=(0,), scratch=[block], copies=1, flops=2 * 9 * 512**3, name="coarse",
+        second, zero, hold(pre), hold(node_pre), hold(up_pre), csrc, cdst, owner, level_one,
+        w_cedge_in, w_cedge_out, hold(w_summed), w_cnode_out, coarse_gain, hold(w_lifted), hold(w_last), up_gain,
+        hbm_outs=(0,), scratch=[block], copies=1, flops=2 * 8 * 512**3, name="coarse",
     )
     return fine_out, edges_out
 

time: 83.1 us -> 78.9 us (0.949)
  the two profiles are of different devices: /device:TPU:256 before, /device:TPU:199 now
where the time goes in v4:
time: 78.9 us; the launch traced here: 78.5 us
  blocking collectives  34.7 us (44%)
  Pallas kernels  18.6 us (24%)
  starting transfers between devices  18.6 us (24%)
  waiting for transfers between devices  5.38 us (7%)
  between operations  1.13 us (1%)
    all_to_all x1, blocking collectives, per_device(): parts = lax.all_to_all(pooled, 'gx', 0, 0, tiled=True)  20.3 us
    pallas_call x8, Pallas kernels, call(): pl.pallas_call(kernel, out_shape=shapes, in_specs=[vmem] * len(args) + [f...  18.6 us
    all_to_all x1, blocking collectives, per_device(): zero = lax.all_to_all(shares, 'gx', 0, 0, tiled=True).reshape(COARSE, 512)  14.4 us
    ppermute x1, starting transfers between devices, per_device(): lax.ppermute(jnp.concatenate([far[0:32], before, near[0:32]], 0), 'gy', o...  5.13 us
    ppermute x1, waiting for transfers between devices, per_device(): first = lax.ppermute(zero, ('gx', 'gy'), sideways)  4.31 us
    ppermute x1, starting transfers between devices, per_device(): far = lax.ppermute(far, 'gx', odd_x)  3.77 us
    ppermute x1, starting transfers between devices, per_device(): first = lax.ppermute(zero, ('gx', 'gy'), sideways)  3.47 us
    ppermute x1, starting transfers between devices, per_device(): second = lax.ppermute(first, 'gx', even_x)  2.23 us
  transfers between devices with their start and end apart: 6, of which 3 were waited for; matrix products, arithmetic and copies ran while one was open for 0% of the time, Pallas kernels for 10%

profile of v4, /device:TPU:199, one launch (start us, length us, event | category | flops | bytes accessed | tf_op | source)
XLA Modules:
  0.0 78.5 jit_solution(17049423613941946947)
XLA Ops:
  0.6 0.0 copy-start.1
  0.7 1.5 %outgoing.1 = (bf16[96,512]{1,0:T(8,128)(2,1)S(1)}, bf16[32,512]{1,0:T(8,128)(2,1)S(1)}, bf16[32,512]{1,0:T(8,128)(2,1)S(1)}, bf16[96,512]{1,0:T(8,128)(2,1)S(1)}) custom-call(bf16[512,512]{1,0:T(8,128)(2,1)} %nodes.5, s32[8,32]{1,0:T(8,128)} %bitcast.31), custom_call_target="tpu_custom_call" | custom-call | flops 13421772800 | bytes 525312 | tf_op jit(solution)/shard_map/outgoing/pallas_call | solution.py:224
  2.2 3.8 %collective-permute-start = (bf16[96,512]{1,0:T(8,128)(2,1)S(1)}, bf16[96,512]{1,0:T(8,128)(2,1)S(1)}, u32[]{:S(2)}, u32[]{:S(2)}) collective-permute-start(bf16[96,512]{1,0:T(8,128)(2,1)S(1)} %get-tuple-element.27), channel_id=1, source_target_pairs={{32,64},{64,32},{96,128},{128,96},{160,192},{192,160},{224,256},{2... | collective-permute-start | bytes 294920 | tf_op jit(solution)/shard_map/ppermute | solution.py:262
  6.0 1.9 %collective-permute-start.1 = (bf16[96,512]{1,0:T(8,128)(2,1)S(1)}, bf16[96,512]{1,0:T(8,128)(2,1)S(1)}, u32[]{:S(2)}, u32[]{:S(2)}) collective-permute-start(bf16[96,512]{1,0:T(8,128)(2,1)S(1)} %get-tuple-element.28), channel_id=1, source_target_pairs={{0,32},{32,0},{64,96},{96,64},{128,160},{160,128},{192,224},{224,1... | collective-permute-start | bytes 294920 | tf_op jit(solution)/shard_map/ppermute | solution.py:263
  7.9 1.9 %tables.1.gathered = f32[1024,512]{1,0:T(8,128)S(1)} custom-call(bf16[512,512]{1,0:T(8,128)(2,1)S(1)} %copy-done.2, s32[8,128]{1,0:T(8,128)S(1)} %bitcast.25, s32[8,128]{1,0:T(8,128)S(1)} %bitcast.27, bf16[1536,512]{1,0:T(8,128)(2,1)S(1)} %copy-done.1), custom_call_target="tpu_custom_call" | custom-call | flops 1610612736 | bytes 2105344 | tf_op jit(solution)/shard_map/tables/pallas_call | solution.py:224
  9.9 5.1 %collective-permute-start.3 = (bf16[96,512]{1,0:T(8,128)(2,1)S(1)}, bf16[96,512]{1,0:T(8,128)(2,1)S(1)}, u32[]{:S(2)}, u32[]{:S(2)}) collective-permute-start(bf16[96,512]{1,0:T(8,128)(2,1)S(1)} %pad_maximum_fusion.1), channel_id=1, source_target_pairs={{1,2},{2,1},{3,4},{4,3},{5,6},{6,5},{7,8},{8,7},{9,10},{10,9},{11,... | collective-permute-start | bytes 294920 | tf_op jit(solution)/shard_map/ppermute | solution.py:270
  15.1 0.0 copy-start.7
  15.1 0.0 copy-start.10
  15.1 0.0 copy-start.11
  15.1 2.1 %collective-permute-start.2 = (bf16[96,512]{1,0:T(8,128)(2,1)S(1)}, bf16[96,512]{1,0:T(8,128)(2,1)S(1)}, u32[]{:S(2)}, u32[]{:S(2)}) collective-permute-start(bf16[96,512]{1,0:T(8,128)(2,1)S(1)} %pad_maximum_fusion), channel_id=1, source_target_pairs={{0,1},{1,0},{2,3},{3,2},{4,5},{5,4},{6,7},{7,6},{8,9},{9,8},{10,11... | collective-permute-start | bytes 294920 | tf_op jit(solution)/shard_map/ppermute | solution.py:269
  17.2 2.4 %edges.1 = (f32[1024,512]{1,0:T(8,128)S(1)}, f32[512,512]{1,0:T(8,128)S(1)}, bf16[1024,512]{1,0:T(8,128)(2,1)S(1)}, bf16[512,512]{1,0:T(8,128)(2,1)S(1)}, bf16[512,512]{1,0:T(8,128)(2,1)S(1)}) custom-call(bf16[512,512]{1,0:T(8,128)(2,1)S(1)} %copy-done.2, f32[1024,512]{1,0:T(8,128)S(1)} %tables.1.gathered, bf16[1024,512]{1,0:T(8,128)(2,1)} %edges_hbm.1, ...), custom_call_target="tpu_custom_call" | custom-call | flops 805306368 | bytes 6291456 | tf_op jit(solution)/shard_map/edges/pallas_call | solution.py:224
  19.6 1.0 %collective-permute-done.2.side_a = bf16[96,512]{1,0:T(8,128)(2,1)S(1)} collective-permute-done((bf16[96,512]{1,0:T(8,128)(2,1)S(1)}, bf16[96,512]{1,0:T(8,128)(2,1)S(1)}, u32[]{:S(2)}, u32[]{:S(2)}) %collective-permute-start.2) | collective-permute-done | bytes 98336 | tf_op jit(solution)/shard_map/ppermute | solution.py:269
  20.7 0.0 copy-start.5
  20.7 3.6 %after_halo.1 = (f32[1024,512]{1,0:T(8,128)S(1)}, bf16[512,512]{1,0:T(8,128)(2,1)S(1)}, bf16[256,512]{1,0:T(8,128)(2,1)S(1)}) custom-call(bf16[96,512]{1,0:T(8,128)(2,1)S(1)} %collective-permute-done.far, bf16[96,512]{1,0:T(8,128)(2,1)S(1)} %collective-permute-done.1.near, bf16[96,512]{1,0:T(8,128)(2,1)S(1)} %collective-permute-done.2.side_a, ...), custom_call_target="tpu_custom_call" | custom-call | flops 2147483648 | bytes 6174720 | tf_op jit(solution)/shard_map/after_halo/pallas_call | solution.py:224
  24.3 20.3 %all_to_all.14.parts = bf16[16,16,512]{2,1,0:T(8,128)(2,1)S(1)} all-to-all(bf16[16,16,512]{2,1,0:T(8,128)(2,1)S(1)} %bitcast.15), channel_id=1, replica_groups=mesh['gx'=16,'gy'=32] {'gx'}, dimensions={0} | all-to-all | bytes 524288 | tf_op jit(solution)/shard_map/all_to_all | solution.py:283
  44.6 0.2 share.1
  44.8 14.4 %all_to_all.15 = bf16[16,16,512]{2,1,0:T(8,128)(2,1)S(1)} all-to-all(bf16[16,16,512]{2,1,0:T(8,128)(2,1)S(1)} %share.1), channel_id=1, replica_groups=mesh['gx'=16,'gy'=32] {'gx'}, dimensions={0} | all-to-all | bytes 524288 | tf_op jit(solution)/shard_map/all_to_all | solution.py:288
  59.2 3.5 %collective-permute-start.4 = (bf16[256,512]{1,0:T(8,128)(2,1)S(1)}, bf16[256,512]{1,0:T(8,128)(2,1)S(1)}, u32[]{:S(2)}, u32[]{:S(2)}) collective-permute-start(bf16[256,512]{1,0:T(8,128)(2,1)S(1)} %bitcast.12), channel_id=1, source_target_pairs={{0,1},{1,0},{2,3},{3,2},{4,5},{5,4},{6,7},{7,6},{8,9},{9,8},{10,11... | collective-permute-start | bytes 786440 | tf_op jit(solution)/shard_map/ppermute | solution.py:292
  62.7 2.6 %own_column.1 = (f32[1024,512]{1,0:T(8,128)S(1)}, f32[256,512]{1,0:T(8,128)S(1)}, f32[512,512]{1,0:T(8,128)S(1)}, bf16[512,512]{1,0:T(8,128)(2,1)S(1)}, bf16[1024,512]{1,0:T(8,128)(2,1)}) custom-call(bf16[256,512]{1,0:T(8,128)(2,1)S(1)} %bitcast.13, s32[8,128]{1,0:T(8,128)S(1)} %bitcast.16, s32[8,128]{1,0:T(8,128)S(1)} %bitcast.19, ...), custom_call_target="tpu_custom_call" | custom-call | flops 1342177280 | bytes 7086080 | tf_op jit(solution)/shard_map/own_column/pallas_call | solution.py:224
  65.3 4.3 %collective-permute-done.4.side = bf16[256,512]{1,0:T(8,128)(2,1)S(1)} collective-permute-done((bf16[256,512]{1,0:T(8,128)(2,1)S(1)}, bf16[256,512]{1,0:T(8,128)(2,1)S(1)}, u32[]{:S(2)}, u32[]{:S(2)}) %collective-permute-start.4) | collective-permute-done | bytes 262176 | tf_op jit(solution)/shard_map/ppermute | solution.py:292
  69.7 2.2 %collective-permute-start.5 = (bf16[256,512]{1,0:T(8,128)(2,1)S(1)}, bf16[256,512]{1,0:T(8,128)(2,1)S(1)}, u32[]{:S(2)}, u32[]{:S(2)}) collective-permute-start(bf16[256,512]{1,0:T(8,128)(2,1)S(1)} %collective-permute-done.4.side), channel_id=1, source_target_pairs={{0,32},{32,0},{64,96},{96,64},{128,160},{160,128},{192,224},{224,1... | collective-permute-start | bytes 786440 | tf_op jit(solution)/shard_map/ppermute | solution.py:299
  71.9 1.2 %first_side.1 = (f32[1024,512]{1,0:T(8,128)S(1)}, bf16[512,512]{1,0:T(8,128)(2,1)S(1)}, bf16[512,512]{1,0:T(8,128)(2,1)S(1)}) custom-call(bf16[256,512]{1,0:T(8,128)(2,1)S(1)} %collective-permute-done.4.side, f32[1024,512]{1,0:T(8,128)S(1)} %get-tuple-element.44.pre, s32[8,128]{1,0:T(8,128)S(1)} %bitcast.17, bf16[1024,512]{1,0:T(8,128)(2,1)S(1)} %copy-done, ...), custom_call_target="tpu_custom_call" | custom-call | flops 536870912 | bytes 4984832 | tf_op jit(solution)/shard_map/first_side/pallas_call | solution.py:224
  73.1 0.1 collective-permute-done.5.side
  73.2 5.1 %coarse.1 = bf16[512,512]{1,0:T(8,128)(2,1)} custom-call(bf16[256,512]{1,0:T(8,128)(2,1)S(1)} %collective-permute-done.5.side, bf16[256,512]{1,0:T(8,128)(2,1)S(1)} %bitcast.14, f32[1024,512]{1,0:T(8,128)S(1)} %get-tuple-element.45.pre, f32[256,512]{1,0:T(8,128)S(1)} %get-tuple-element.46.node_pre, f32[512,512]{1,0:T(8,128)S(1)} %get-tuple-element.47.up_pre, ...), custom_call_target="tpu_custom_call" | custom-call | flops 2147483648 | bytes 8402944 | tf_op jit(solution)/shard_map/coarse/pallas_call | solution.py:224
  (33 shorter events, 0.1 us)
Async XLA Ops:
  0.6 7.3 %copy-start.1 = (bf16[1536,512]{1,0:T(8,128)(2,1)S(1)}, bf16[1536,512]{1,0:T(8,128)(2,1)}, u32[]{:S(2)}) copy-start(bf16[1536,512]{1,0:T(8,128)(2,1)} %w_in_hbm.1) | copy-start | bytes 4718596
  0.6 7.3 %copy-start.2 = (bf16[512,512]{1,0:T(8,128)(2,1)S(1)}, bf16[512,512]{1,0:T(8,128)(2,1)}, u32[]{:S(2)}) copy-start(bf16[512,512]{1,0:T(8,128)(2,1)} %nodes.5) | copy-start | bytes 1572868
  0.7 7.3 %copy-start.12 = (s32[1024]{0:T(1024)S(1)}, s32[1024]{0:T(1024)}, u32[]{:S(2)}) copy-start(s32[1024]{0:T(1024)} %param.24) | copy-start | bytes 12292
  0.7 7.3 %copy-start.13 = (s32[1024]{0:T(1024)S(1)}, s32[1024]{0:T(1024)}, u32[]{:S(2)}) copy-start(s32[1024]{0:T(1024)} %param.25) | copy-start | bytes 12292
  2.2 7.7 %collective-permute-start = (bf16[96,512]{1,0:T(8,128)(2,1)S(1)}, bf16[96,512]{1,0:T(8,128)(2,1)S(1)}, u32[]{:S(2)}, u32[]{:S(2)}) collective-permute-start(bf16[96,512]{1,0:T(8,128)(2,1)S(1)} %get-tuple-element.27), channel_id=1, source_target_pairs={{32,64},{64,32},{96,128},{128,96},{160,192},{192,160},{224,256},{2... | collective-permute-start | bytes 294920 | tf_op jit(solution)/shard_map/ppermute | solution.py:262
  6.0 3.9 %collective-permute-start.1 = (bf16[96,512]{1,0:T(8,128)(2,1)S(1)}, bf16[96,512]{1,0:T(8,128)(2,1)S(1)}, u32[]{:S(2)}, u32[]{:S(2)}) collective-permute-start(bf16[96,512]{1,0:T(8,128)(2,1)S(1)} %get-tuple-element.28), channel_id=1, source_target_pairs={{0,32},{32,0},{64,96},{96,64},{128,160},{160,128},{192,224},{224,1... | collective-permute-start | bytes 294920 | tf_op jit(solution)/shard_map/ppermute | solution.py:263
  9.9 9.7 %collective-permute-start.3 = (bf16[96,512]{1,0:T(8,128)(2,1)S(1)}, bf16[96,512]{1,0:T(8,128)(2,1)S(1)}, u32[]{:S(2)}, u32[]{:S(2)}) collective-permute-start(bf16[96,512]{1,0:T(8,128)(2,1)S(1)} %pad_maximum_fusion.1), channel_id=1, source_target_pairs={{1,2},{2,1},{3,4},{4,3},{5,6},{6,5},{7,8},{8,7},{9,10},{10,9},{11,... | collective-permute-start | bytes 294920 | tf_op jit(solution)/shard_map/ppermute | solution.py:270
  15.1 5.6 %copy-start.7 = (s32[512]{0:T(512)S(1)}, s32[512]{0:T(512)}, u32[]{:S(2)}) copy-start(s32[512]{0:T(512)} %param.27) | copy-start | bytes 6148
  15.1 5.5 %copy-start.10 = (bf16[512,512]{1,0:T(8,128)(2,1)S(1)}, bf16[512,512]{1,0:T(8,128)(2,1)}, u32[]{:S(2)}) copy-start(bf16[512,512]{1,0:T(8,128)(2,1)} %w_out.1) | copy-start | bytes 1572868
  15.1 5.5 %copy-start.11 = (bf16[512,512]{1,0:T(8,128)(2,1)S(1)}, bf16[512,512]{1,0:T(8,128)(2,1)}, u32[]{:S(2)}) copy-start(bf16[512,512]{1,0:T(8,128)(2,1)} %w_node_out.1) | copy-start | bytes 1572868
  15.1 5.5 %copy-start.14 = (f32[512]{0:T(512)S(1)}, f32[512]{0:T(512)}, u32[]{:S(2)}) copy-start(f32[512]{0:T(512)} %param.32) | copy-start | bytes 6148
  15.1 5.5 %copy-start.15 = (f32[512]{0:T(512)S(1)}, f32[512]{0:T(512)}, u32[]{:S(2)}) copy-start(f32[512]{0:T(512)} %param.35) | copy-start | bytes 6148
  15.1 5.5 %collective-permute-start.2 = (bf16[96,512]{1,0:T(8,128)(2,1)S(1)}, bf16[96,512]{1,0:T(8,128)(2,1)S(1)}, u32[]{:S(2)}, u32[]{:S(2)}) collective-permute-start(bf16[96,512]{1,0:T(8,128)(2,1)S(1)} %pad_maximum_fusion), channel_id=1, source_target_pairs={{0,1},{1,0},{2,3},{3,2},{4,5},{5,4},{6,7},{7,6},{8,9},{9,8},{10,11... | collective-permute-start | bytes 294920 | tf_op jit(solution)/shard_map/ppermute | solution.py:269
  20.7 42.0 %copy-start.5 = (s32[1024]{0:T(1024)S(1)}, s32[1024]{0:T(1024)}, u32[]{:S(2)}) copy-start(s32[1024]{0:T(1024)} %param.28) | copy-start | bytes 12292
  20.7 42.0 %copy-start.6 = (s32[1024]{0:T(1024)S(1)}, s32[1024]{0:T(1024)}, u32[]{:S(2)}) copy-start(s32[1024]{0:T(1024)} %param.29) | copy-start | bytes 12292
  24.3 38.4 %copy-start = (bf16[1024,512]{1,0:T(8,128)(2,1)S(1)}, bf16[1024,512]{1,0:T(8,128)(2,1)}, u32[]{:S(2)}) copy-start(bf16[1024,512]{1,0:T(8,128)(2,1)} %w_cin.5) | copy-start | bytes 3145732
  59.2 10.4 %collective-permute-start.4 = (bf16[256,512]{1,0:T(8,128)(2,1)S(1)}, bf16[256,512]{1,0:T(8,128)(2,1)S(1)}, u32[]{:S(2)}, u32[]{:S(2)}) collective-permute-start(bf16[256,512]{1,0:T(8,128)(2,1)S(1)} %bitcast.12), channel_id=1, source_target_pairs={{0,1},{1,0},{2,3},{3,2},{4,5},{5,4},{6,7},{7,6},{8,9},{9,8},{10,11... | collective-permute-start | bytes 786440 | tf_op jit(solution)/shard_map/ppermute | solution.py:292
  69.6 3.6 %copy-start.3 = (bf16[512,512]{1,0:T(8,128)(2,1)S(1)}, bf16[512,512]{1,0:T(8,128)(2,1)}, u32[]{:S(2)}) copy-start(bf16[512,512]{1,0:T(8,128)(2,1)} %w_cout.1) | copy-start | bytes 1572868
  69.6 3.6 %copy-start.4 = (bf16[512,512]{1,0:T(8,128)(2,1)S(1)}, bf16[512,512]{1,0:T(8,128)(2,1)}, u32[]{:S(2)}) copy-start(bf16[512,512]{1,0:T(8,128)(2,1)} %w_nout.1) | copy-start | bytes 1572868
  69.6 3.6 %copy-start.8 = (f32[512]{0:T(512)S(1)}, f32[512]{0:T(512)}, u32[]{:S(2)}) copy-start(f32[512]{0:T(512)} %param.40) | copy-start | bytes 6148
  69.6 3.6 %copy-start.9 = (f32[512]{0:T(512)S(1)}, f32[512]{0:T(512)}, u32[]{:S(2)}) copy-start(f32[512]{0:T(512)} %param.43) | copy-start | bytes 6148
  69.7 3.6 %collective-permute-start.5 = (bf16[256,512]{1,0:T(8,128)(2,1)S(1)}, bf16[256,512]{1,0:T(8,128)(2,1)S(1)}, u32[]{:S(2)}, u32[]{:S(2)}) collective-permute-start(bf16[256,512]{1,0:T(8,128)(2,1)S(1)} %collective-permute-done.4.side), channel_id=1, source_target_pairs={{0,32},{32,0},{64,96},{96,64},{128,160},{160,128},{192,224},{224,1... | collective-permute-start | bytes 786440 | tf_op jit(solution)/shard_map/ppermute | solution.py:299

commit v5 on v4

--- a/solution.py
+++ b/solution.py
@@ -78,22 +78,40 @@
     near[...] = picked[160:256, :]
 
 
-def tables_kernel(nodes, src, dst, w_in, gathered):
+def tables_kernel(nodes, src, dst, w_in, gathered, dst_spread):
     nodes = nodes[...]
     src_proj = dot(nodes, w_in[512:1024, :]).astype(BF16)
     dst_proj = dot(nodes, w_in[1024:1536, :]).astype(BF16)
     part = dot(pick(as_column(src[...]), 512), src_proj)
     gathered[...] = part + dot(pick(as_column(dst[...]), 512), dst_proj)
+    dst_spread[...] = spread(as_row(dst[...]), 512)
+
+
+def halo_slots(src):
+    odd_x, odd_y = odd_place()
+    slot = src - 512
+    k = slot >> 5
+    turn_x = jnp.where(k < 3, k + 5, jnp.where(k > 4, k - 5, k))
+    k = jnp.where(odd_x, turn_x, k)
+    turn_y = jnp.where(
+        (k == 0) | (k == 5), k + 2, jnp.where((k == 2) | (k == 7), k - 2, jnp.where(k == 3, 4, jnp.where(k == 4, 3, k)))
+    )
+    k = jnp.where(odd_y, turn_y, k)
+    slot = jnp.where(slot < 0, -1, k * 32 + (slot & 31))
+    return slot
 
 
 def edges_kernel(
-    nodes, gathered, edges_hbm, w_in_hbm, w_node_hbm, pre, node_pre, edges, w_source, w_summed, w_in, w_node, sems
+    nodes, gathered, src, parents, edges_hbm, w_in_hbm, w_node_hbm,
+    pre, node_pre, edges, w_source, w_summed, halo_pick, owner_spread, w_in, w_node, sems,
 ):
     got = fetch(
         sems, (w_node_hbm.at[0:512], w_node), (w_in_hbm.at[0:512], w_in),
         (edges_hbm.at[0:512], edges.at[0:512]), (edges_hbm.at[512:1024], edges.at[512:1024]),
         (w_in_hbm.at[512:1024], w_source), (w_node_hbm.at[512:1024], w_summed),
     )
+    halo_pick[...] = pick(as_column(halo_slots(src[...])), 256)
+    owner_spread[...] = spread(as_row(parents[...]), COARSE)
     got[0].wait()
     node_pre[...] = dot(nodes[...], w_node[...])
     got[1].wait()
@@ -106,7 +124,7 @@
 
 
 def after_halo_kernel(
-    far, near, side_a, side_b, pre, node_pre, nodes, src, dst, parents,
+    far, near, side_a, side_b, pre, node_pre, nodes, halo_pick, dst_spread, owner_spread,
     w_source, w_out, gain, w_summed, w_node_out, node_gain,
     message_out, level_one, pooled,
 ):
@@ -118,25 +136,15 @@
         0,
     )
     halo = dot(received, w_source[...]).astype(BF16)
-    odd_x, odd_y = odd_place()
-    slot = src[...] - 512
-    k = slot >> 5
-    turn_x = jnp.where(k < 3, k + 5, jnp.where(k > 4, k - 5, k))
-    k = jnp.where(odd_x, turn_x, k)
-    turn_y = jnp.where(
-        (k == 0) | (k == 5), k + 2, jnp.where((k == 2) | (k == 7), k - 2, jnp.where(k == 3, 4, jnp.where(k == 4, 3, k)))
-    )
-    k = jnp.where(odd_y, turn_y, k)
-    slot = jnp.where(slot < 0, -1, k * 32 + (slot & 31))
-    part = pre[...] + dot(pick(as_column(slot), 256), halo)
+    part = pre[...] + dot(halo_pick[...], halo)
     message = mlp_tail(part, w_out[...], gain[...])
     message_out[...] = message
-    summed = dot(spread(as_row(dst[...]), 512), message.astype(BF16)).astype(BF16)
+    summed = dot(dst_spread[...], message.astype(BF16)).astype(BF16)
     part = node_pre[...] + dot(summed, w_summed[...])
     level = nodes[...].astype(F32) + mlp_tail(part, w_node_out[...], node_gain[...])
     level = level.astype(BF16)
     level_one[...] = level
-    pooled[...] = dot(spread(as_row(parents[...]), COARSE), level).astype(BF16)
+    pooled[...] = dot(owner_spread[...], level).astype(BF16)
 
 
 def share_kernel(parts, out):
@@ -149,25 +157,28 @@
 
 
 def own_kernel(
-    zero, csrc, cdst, level_one, edges, message, w_cin, w_nin_hbm, w_up_hbm,
-    pre, node_pre, up_pre, w_summed, edges_hbm, w_nin, w_up, edges_out, sems,
-):
-    got = fetch(
-        sems, (w_nin_hbm.at[0:512], w_nin), (w_up_hbm.at[0:512], w_up), (w_nin_hbm.at[512:1024], w_summed)
-    )
+    zero, csrc, cdst, parents, level_one, edges, message, w_cin, w_nin_hbm, w_up_hbm,
+    pre, node_pre, up_pre, edges_hbm, first_pick, second_pick, dst_spread, owner_pick,
+    w_nin, w_up, edges_out, sems,
+):
+    got = fetch(sems, (w_nin_hbm.at[0:512], w_nin), (w_up_hbm.at[0:512], w_up))
     edges_out[...] = (edges[...].astype(F32) + message[...]).astype(BF16)
-    sent = pltpu.make_async_copy(edges_out, edges_hbm, sems.at[3])
+    sent = pltpu.make_async_copy(edges_out, edges_hbm, sems.at[2])
     sent.start()
     zero = zero[...]
     side_src = dot(zero, w_cin[0:512, :]).astype(BF16)
     side_dst = dot(zero, w_cin[512:1024, :]).astype(BF16)
     part = dot(pick(as_column(csrc[...]), COARSE, COARSE), side_src)
     pre[...] = part + dot(pick(as_column(cdst[...]), COARSE), side_dst)
+    right = first_is_right()
+    first_pick[...] = side_pick(right, csrc[...])
+    second_pick[...] = side_pick(jnp.logical_not(right), csrc[...])
+    dst_spread[...] = spread(as_row(cdst[...]), COARSE)
+    owner_pick[...] = pick(as_column(parents[...]), COARSE)
     got[0].wait()
     node_pre[...] = dot(zero, w_nin[...])
     got[1].wait()
     up_pre[...] = dot(level_one[...], w_up[...])
-    got[2].wait()
     sent.wait()
 
 
@@ -176,31 +187,33 @@
     return odd_x == odd_y
 
 
-def side_rows(side, right, csrc, w_source):
-    side_src = dot(side[...], w_source[...]).astype(BF16)
-    base = jnp.where(right, 2 * COARSE, 0)
-    return dot(pick(as_column(csrc[...] - base), COARSE), side_src)
-
-
-def first_kernel(side, pre, csrc, w_cin, w_up_hbm, w_up_out_hbm, both, w_lifted, w_up_out, sems):
+def side_pick(right, csrc):
+    return pick(as_column(csrc - jnp.where(right, 2 * COARSE, 0)), COARSE)
+
+
+def first_kernel(side, pre, first_pick, w_cin, w_nin_hbm, both, w_summed, sems):
+    (got,) = fetch(sems, (w_nin_hbm.at[512:1024], w_summed))
+    side_src = dot(side[...], w_cin[0:512, :]).astype(BF16)
+    both[...] = pre[...] + dot(first_pick[...], side_src)
+    got.wait()
+
+
+def coarse_kernel(
+    side, zero, pre, node_pre, up_pre, second_pick, dst_spread, owner_pick, level_one,
+    w_cin, w_cout, w_summed, w_nout, coarse_gain, up_gain, w_up_hbm, w_up_out_hbm,
+    out_hbm, out, w_lifted, w_up_out, sems,
+):
     got = fetch(sems, (w_up_hbm.at[512:1024], w_lifted), (w_up_out_hbm, w_up_out))
-    both[...] = pre[...] + side_rows(side, first_is_right(), csrc, w_cin.at[0:512])
-    for copy in got:
-        copy.wait()
-
-
-def coarse_kernel(
-    side, zero, pre, node_pre, up_pre, csrc, cdst, parents, level_one,
-    w_cin, w_cout, w_summed, w_nout, coarse_gain, w_lifted, w_up_out, up_gain,
-    out_hbm, out, sems,
-):
-    part = pre[...] + side_rows(side, jnp.logical_not(first_is_right()), csrc, w_cin.at[0:512])
+    side_src = dot(side[...], w_cin[0:512, :]).astype(BF16)
+    part = pre[...] + dot(second_pick[...], side_src)
     message = layer_norm(dot(silu(part).astype(BF16), w_cout[...]))
-    summed = dot(spread(as_row(cdst[...]), COARSE), message.astype(BF16)).astype(BF16)
+    summed = dot(dst_spread[...], message.astype(BF16)).astype(BF16)
     part = node_pre[...] + dot(summed, w_summed[...])
     one = (zero[...].astype(F32) + mlp_tail(part, w_nout[...], coarse_gain[...])).astype(BF16)
-    lifted = dot(pick(as_column(parents[...]), COARSE), one).astype(BF16)
+    lifted = dot(owner_pick[...], one).astype(BF16)
+    got[0].wait()
     part = up_pre[...] + dot(lifted, w_lifted[...])
+    got[1].wait()
     tail = mlp_tail(part, w_up_out[...], up_gain[...])
     out[...] = (level_one[...].astype(F32) + tail).astype(BF16)
     (sent,) = fetch(sems, (out, out_hbm))
@@ -261,22 +274,25 @@
     even_y, odd_y = trades(count_y)
     far = lax.ppermute(far, "gx", odd_x)
     near = lax.ppermute(near, "gx", even_x)
-    gathered = call(
-        tables_kernel, [((1024, 512), F32)], fine_nodes, src, dst, w_edge_in, held=(0,),
+    gathered, dst_spread = call(
+        tables_kernel, [((1024, 512), F32), ((512, 1024), BF16)], fine_nodes, src, dst, w_edge_in, held=(0, 1),
         flops=2 * 6 * 512**3, name="tables",
     )
     far, near, gathered = lax.optimization_barrier((far, near, gathered))
     side_a = lax.ppermute(jnp.concatenate([far[64:96], after, near[64:96]], 0), "gy", even_y)
     side_b = lax.ppermute(jnp.concatenate([far[0:32], before, near[0:32]], 0), "gy", odd_y)
     square = ((512, 512), BF16)
-    pre, node_pre, edges, w_source, w_summed = call(
-        edges_kernel, [((1024, 512), F32), ((512, 512), F32), ((1024, 512), BF16), square, square],
-        fine_nodes, hold(gathered), hbm=(fine_edges, w_edge_in, w_node_in), held=(0, 1, 2, 3, 4),
+    pre, node_pre, edges, w_source, w_summed, halo_pick, owner_spread = call(
+        edges_kernel,
+        [((1024, 512), F32), ((512, 512), F32), ((1024, 512), BF16), square, square]
+        + [((1024, 256), BF16), ((COARSE, 512), BF16)],
+        fine_nodes, hold(gathered), src, owner, hbm=(fine_edges, w_edge_in, w_node_in), held=range(7),
         scratch=[block, block], copies=6, flops=2 * 3 * 512**3, name="edges",
     )
     message, level_one, pooled = call(
         after_halo_kernel, [((1024, 512), F32), square, ((COARSE, 512), BF16)],
-        far, near, side_a, side_b, hold(pre), hold(node_pre), fine_nodes, src, dst, owner,
+        far, near, side_a, side_b, hold(pre), hold(node_pre), fine_nodes,
+        hold(halo_pick), hold(dst_spread), hold(owner_spread),
         hold(w_source), w_edge_out, edge_gain, hold(w_summed), w_node_out, node_gain,
         held=(0,), flops=2 * 8 * 512**3, name="after_halo",
     )
@@ -290,22 +306,25 @@
         (i * count_y + j, i * count_y + to) for i in range(count_x) for j, to in (odd_y if i % 2 else even_y)
     ]
     first = lax.ppermute(zero, ("gx", "gy"), sideways)
-    pre, node_pre, up_pre, w_summed, edges_out = call(
-        own_kernel, [((1024, 512), F32), ((COARSE, 512), F32), ((512, 512), F32), square, ((1024, 512), BF16)],
-        zero, csrc, cdst, level_one, hold(edges), hold(message), w_cedge_in, hbm=(w_cnode_in, w_up_in),
-        held=range(4), hbm_outs=(4,), scratch=[block, block, pltpu.VMEM((1024, 512), BF16)], copies=4, flops=2 * 5 * 512**3, name="own_column",
+    picks = [((1024, COARSE), BF16)] * 2 + [((COARSE, 1024), BF16), ((512, COARSE), BF16)]
+    pre, node_pre, up_pre, edges_out, first_pick, second_pick, dst_spread, owner_pick = call(
+        own_kernel,
+        [((1024, 512), F32), ((COARSE, 512), F32), ((512, 512), F32), ((1024, 512), BF16)] + picks,
+        zero, csrc, cdst, owner, level_one, hold(edges), hold(message), w_cedge_in, hbm=(w_cnode_in, w_up_in),
+        held=(0, 1, 2, 4, 5, 6, 7), hbm_outs=(3,), scratch=[block, block, pltpu.VMEM((1024, 512), BF16)], copies=3, flops=2 * 5 * 512**3, name="own_column",
     )
     first, pre = lax.optimization_barrier((first, pre))
     second = lax.ppermute(first, "gx", even_x)
-    pre, w_lifted, w_last = call(
-        first_kernel, [((1024, 512), F32), square, square], first, hold(pre), csrc, w_cedge_in,
-        hbm=(w_up_in, w_up_out), held=range(3), copies=2, flops=2 * 2 * 512**3, name="first_side",
+    pre, w_summed = call(
+        first_kernel, [((1024, 512), F32), square], first, hold(pre), hold(first_pick), w_cedge_in,
+        hbm=(w_cnode_in,), held=(0, 1), copies=1, flops=2 * 2 * 512**3, name="first_side",
     )
     fine_out = call(
         coarse_kernel, [square],
-        second, zero, hold(pre), hold(node_pre), hold(up_pre), csrc, cdst, owner, level_one,
-        w_cedge_in, w_cedge_out, hold(w_summed), w_cnode_out, coarse_gain, hold(w_lifted), hold(w_last), up_gain,
-        hbm_outs=(0,), scratch=[block], copies=1, flops=2 * 8 * 512**3, name="coarse",
+        second, zero, hold(pre), hold(node_pre), hold(up_pre), hold(second_pick), hold(dst_spread), hold(owner_pick),
+        level_one, w_cedge_in, w_cedge_out, hold(w_summed), w_cnode_out, coarse_gain, up_gain,
+        hbm=(w_up_in, w_up_out), hbm_outs=(0,), scratch=[block] * 3, copies=2,
+        flops=2 * 8 * 512**3, name="coarse",
     )
     return fine_out, edges_out
 

time: 78.9 us -> 78.2 us (level)
  transfers between devices with their start and end apart: 6 -> 6, of which waited for: 3 -> 3; matrix products, arithmetic and copies ran while one was open for 0% -> 0% of each run, Pallas kernels for 10% -> 12%
where the time goes in v5:
time: 78.2 us; the launch traced here: 77.8 us
  blocking collectives  34.4 us (44%)
  Pallas kernels  19.2 us (25%)
  starting transfers between devices  18.3 us (23%)
  waiting for transfers between devices  4.64 us (6%)
  between operations  1.14 us (1%)
    all_to_all x1, blocking collectives, per_device(): parts = lax.all_to_all(pooled, 'gx', 0, 0, tiled=True)  20 us
    pallas_call x8, Pallas kernels, call(): pl.pallas_call(kernel, out_shape=shapes, in_specs=[vmem] * len(args) + [f...  19.2 us
    all_to_all x1, blocking collectives, per_device(): zero = lax.all_to_all(shares, 'gx', 0, 0, tiled=True).reshape(COARSE, 512)  14.4 us
    ppermute x1, starting transfers between devices, per_device(): lax.ppermute(jnp.concatenate([far[0:32], before, near[0:32]], 0), 'gy', o...  5.13 us
    ppermute x1, starting transfers between devices, per_device(): far = lax.ppermute(far, 'gx', odd_x)  3.77 us
    ppermute x1, waiting for transfers between devices, per_device(): first = lax.ppermute(zero, ('gx', 'gy'), sideways)  3.68 us
    ppermute x1, starting transfers between devices, per_device(): first = lax.ppermute(zero, ('gx', 'gy'), sideways)  3.46 us
    ppermute x1, starting transfers between devices, per_device(): second = lax.ppermute(first, 'gx', even_x)  2.09 us
  transfers between devices with their start and end apart: 6, of which 3 were waited for; matrix products, arithmetic and copies ran while one was open for 0% of the time, Pallas kernels for 12%

profile of v5, /device:TPU:199, one launch (start us, length us, event | category | flops | bytes accessed | tf_op | source)
XLA Modules:
  0.0 77.8 jit_solution(1182022620178666293)
XLA Ops:
  0.7 1.5 %outgoing.1 = (bf16[96,512]{1,0:T(8,128)(2,1)S(1)}, bf16[32,512]{1,0:T(8,128)(2,1)S(1)}, bf16[32,512]{1,0:T(8,128)(2,1)S(1)}, bf16[96,512]{1,0:T(8,128)(2,1)S(1)}) custom-call(bf16[512,512]{1,0:T(8,128)(2,1)} %nodes.5, s32[8,32]{1,0:T(8,128)} %bitcast.27), custom_call_target="tpu_custom_call" | custom-call | flops 13421772800 | bytes 525312 | tf_op jit(solution)/shard_map/outgoing/pallas_call | solution.py:237
  2.2 3.8 %collective-permute-start = (bf16[96,512]{1,0:T(8,128)(2,1)S(1)}, bf16[96,512]{1,0:T(8,128)(2,1)S(1)}, u32[]{:S(2)}, u32[]{:S(2)}) collective-permute-start(bf16[96,512]{1,0:T(8,128)(2,1)S(1)} %get-tuple-element.33), channel_id=1, source_target_pairs={{32,64},{64,32},{96,128},{128,96},{160,192},{192,160},{224,256},{2... | collective-permute-start | bytes 294920 | tf_op jit(solution)/shard_map/ppermute | solution.py:275
  6.0 1.9 %collective-permute-start.1 = (bf16[96,512]{1,0:T(8,128)(2,1)S(1)}, bf16[96,512]{1,0:T(8,128)(2,1)S(1)}, u32[]{:S(2)}, u32[]{:S(2)}) collective-permute-start(bf16[96,512]{1,0:T(8,128)(2,1)S(1)} %get-tuple-element.34), channel_id=1, source_target_pairs={{0,32},{32,0},{64,96},{96,64},{128,160},{160,128},{192,224},{224,1... | collective-permute-start | bytes 294920 | tf_op jit(solution)/shard_map/ppermute | solution.py:276
  7.9 0.0 copy-start.7
  8.0 2.3 %tables.1 = (f32[1024,512]{1,0:T(8,128)S(1)}, bf16[512,1024]{1,0:T(8,128)(2,1)S(1)}) custom-call(bf16[512,512]{1,0:T(8,128)(2,1)S(1)} %copy-done.1, s32[8,128]{1,0:T(8,128)S(1)} %bitcast.18, s32[8,128]{1,0:T(8,128)S(1)} %bitcast.26, bf16[1536,512]{1,0:T(8,128)(2,1)S(1)} %copy-done.2), custom_call_target="tpu_custom_call" | custom-call | flops 1610612736 | bytes 2105344 | tf_op jit(solution)/shard_map/tables/pallas_call | solution.py:237
  10.3 5.1 %collective-permute-start.3 = (bf16[96,512]{1,0:T(8,128)(2,1)S(1)}, bf16[96,512]{1,0:T(8,128)(2,1)S(1)}, u32[]{:S(2)}, u32[]{:S(2)}) collective-permute-start(bf16[96,512]{1,0:T(8,128)(2,1)S(1)} %pad_maximum_fusion.1), channel_id=1, source_target_pairs={{1,2},{2,1},{3,4},{4,3},{5,6},{6,5},{7,8},{8,7},{9,10},{10,9},{11,... | collective-permute-start | bytes 294920 | tf_op jit(solution)/shard_map/ppermute | solution.py:283
  15.4 1.9 %collective-permute-start.2 = (bf16[96,512]{1,0:T(8,128)(2,1)S(1)}, bf16[96,512]{1,0:T(8,128)(2,1)S(1)}, u32[]{:S(2)}, u32[]{:S(2)}) collective-permute-start(bf16[96,512]{1,0:T(8,128)(2,1)S(1)} %pad_maximum_fusion), channel_id=1, source_target_pairs={{0,1},{1,0},{2,3},{3,2},{4,5},{5,4},{6,7},{7,6},{8,9},{9,8},{10,11... | collective-permute-start | bytes 294920 | tf_op jit(solution)/shard_map/ppermute | solution.py:282
  17.4 0.0 copy-start.11
  17.4 0.0 copy-start.12
  17.4 2.5 %edges.1 = (f32[1024,512]{1,0:T(8,128)S(1)}, f32[512,512]{1,0:T(8,128)S(1)}, bf16[1024,512]{1,0:T(8,128)(2,1)S(1)}, bf16[512,512]{1,0:T(8,128)(2,1)S(1)}, bf16[5...) custom-call(bf16[512,512]{1,0:T(8,128)(2,1)S(1)} %copy-done.1, ...), custom_call_target="tpu_custom_call" | custom-call | flops 805306368 | bytes 6297600 | tf_op jit(solution)/shard_map/edges/pallas_call | solution.py:237
  20.0 0.8 %collective-permute-done.2.side_a = bf16[96,512]{1,0:T(8,128)(2,1)S(1)} collective-permute-done((bf16[96,512]{1,0:T(8,128)(2,1)S(1)}, bf16[96,512]{1,0:T(8,128)(2,1)S(1)}, u32[]{:S(2)}, u32[]{:S(2)}) %collective-permute-start.2) | collective-permute-done | bytes 98336 | tf_op jit(solution)/shard_map/ppermute | solution.py:282
  20.8 0.0 copy-start.10
  20.8 3.4 %after_halo.1 = (f32[1024,512]{1,0:T(8,128)S(1)}, bf16[512,512]{1,0:T(8,128)(2,1)S(1)}, bf16[256,512]{1,0:T(8,128)(2,1)S(1)}) custom-call(bf16[96,512]{1,0:T(8,128)(2,1)S(1)} %collective-permute-done.far, bf16[96,512]{1,0:T(8,128)(2,1)S(1)} %collective-permute-done.1.near, bf16[96,512]{1,0:T(8,128)(2,1)S(1)} %collective-permute-done.2.side_a, ...), custom_call_target="tpu_custom_call" | custom-call | flops 2147483648 | bytes 7999488 | tf_op jit(solution)/shard_map/after_halo/pallas_call | solution.py:237
  24.3 20.0 %all_to_all.14.parts = bf16[16,16,512]{2,1,0:T(8,128)(2,1)S(1)} all-to-all(bf16[16,16,512]{2,1,0:T(8,128)(2,1)S(1)} %bitcast.15), channel_id=1, replica_groups=mesh['gx'=16,'gy'=32] {'gx'}, dimensions={0} | all-to-all | bytes 524288 | tf_op jit(solution)/shard_map/all_to_all | solution.py:299
  44.2 0.2 share.1
  44.4 14.4 %all_to_all.15 = bf16[16,16,512]{2,1,0:T(8,128)(2,1)S(1)} all-to-all(bf16[16,16,512]{2,1,0:T(8,128)(2,1)S(1)} %share.1), channel_id=1, replica_groups=mesh['gx'=16,'gy'=32] {'gx'}, dimensions={0} | all-to-all | bytes 524288 | tf_op jit(solution)/shard_map/all_to_all | solution.py:304
  58.8 3.5 %collective-permute-start.4 = (bf16[256,512]{1,0:T(8,128)(2,1)S(1)}, bf16[256,512]{1,0:T(8,128)(2,1)S(1)}, u32[]{:S(2)}, u32[]{:S(2)}) collective-permute-start(bf16[256,512]{1,0:T(8,128)(2,1)S(1)} %bitcast.12), channel_id=1, source_target_pairs={{0,1},{1,0},{2,3},{3,2},{4,5},{5,4},{6,7},{7,6},{8,9},{9,8},{10,11... | collective-permute-start | bytes 786440 | tf_op jit(solution)/shard_map/ppermute | solution.py:308
  62.3 3.2 %own_column.1 = (f32[1024,512]{1,0:T(8,128)S(1)}, f32[256,512]{1,0:T(8,128)S(1)}, f32[512,512]{1,0:T(8,128)S(1)}, bf16[1024,512]{1,0:T(8,128)(2,1)}, bf16[1024,2...) custom-call(bf16[256,512]{1,0:T(8,128)(2,1)S(1)} %bitcast.13, ...), custom_call_target="tpu_custom_call" | custom-call | flops 1342177280 | bytes 7088128 | tf_op jit(solution)/shard_map/own_column/pallas_call | solution.py:237
  65.6 3.7 %collective-permute-done.4.side = bf16[256,512]{1,0:T(8,128)(2,1)S(1)} collective-permute-done((bf16[256,512]{1,0:T(8,128)(2,1)S(1)}, bf16[256,512]{1,0:T(8,128)(2,1)S(1)}, u32[]{:S(2)}, u32[]{:S(2)}) %collective-permute-start.4) | collective-permute-done | bytes 262176 | tf_op jit(solution)/shard_map/ppermute | solution.py:308
  69.3 2.1 %collective-permute-start.5 = (bf16[256,512]{1,0:T(8,128)(2,1)S(1)}, bf16[256,512]{1,0:T(8,128)(2,1)S(1)}, u32[]{:S(2)}, u32[]{:S(2)}) collective-permute-start(bf16[256,512]{1,0:T(8,128)(2,1)S(1)} %collective-permute-done.4.side), channel_id=1, source_target_pairs={{0,32},{32,0},{64,96},{96,64},{128,160},{160,128},{192,224},{224,1... | collective-permute-start | bytes 786440 | tf_op jit(solution)/shard_map/ppermute | solution.py:317
  71.4 1.1 %first_side.1 = (f32[1024,512]{1,0:T(8,128)S(1)}, bf16[512,512]{1,0:T(8,128)(2,1)S(1)}) custom-call(bf16[256,512]{1,0:T(8,128)(2,1)S(1)} %collective-permute-done.4.side, f32[1024,512]{1,0:T(8,128)S(1)} %get-tuple-element.54.pre, bf16[1024,256]{1,0:T(8,128)(2,1)S(1)} %get-tuple-element.55.first_pick, bf16[1024,512]{1,0:T(8,128)(2,1)S(1)} %copy-done, ...), custom_call_target="tpu_custom_call" | custom-call | flops 536870912 | bytes 4980736 | tf_op jit(solution)/shard_map/first_side/pallas_call | solution.py:237
  72.6 0.1 collective-permute-done.5.side
  72.7 0.0 copy-done.6
  72.7 4.9 %coarse.1 = bf16[512,512]{1,0:T(8,128)(2,1)} custom-call(bf16[256,512]{1,0:T(8,128)(2,1)S(1)} %collective-permute-done.5.side, bf16[256,512]{1,0:T(8,128)(2,1)S(1)} %bitcast.14, f32[1024,512]{1,0:T(8,128)S(1)} %get-tuple-element.56.pre, f32[256,512]{1,0:T(8,128)S(1)} %get-tuple-element.57.node_pre, f32[512,512]{1,0:T(8,128)S(1)} %get-tuple-element.58.up_pre, ...), custom_call_target="tpu_custom_call" | custom-call | flops 2147483648 | bytes 10227712 | tf_op jit(solution)/shard_map/coarse/pallas_call | solution.py:237
  (33 shorter events, 0.1 us)
Async XLA Ops:
  0.6 7.3 %copy-start.1 = (bf16[512,512]{1,0:T(8,128)(2,1)S(1)}, bf16[512,512]{1,0:T(8,128)(2,1)}, u32[]{:S(2)}) copy-start(bf16[512,512]{1,0:T(8,128)(2,1)} %nodes.5) | copy-start | bytes 1572868
  0.6 7.3 %copy-start.2 = (bf16[1536,512]{1,0:T(8,128)(2,1)S(1)}, bf16[1536,512]{1,0:T(8,128)(2,1)}, u32[]{:S(2)}) copy-start(bf16[1536,512]{1,0:T(8,128)(2,1)} %w_in_hbm.1) | copy-start | bytes 4718596
  0.7 7.3 %copy-start.8 = (s32[1024]{0:T(1024)S(1)}, s32[1024]{0:T(1024)}, u32[]{:S(2)}) copy-start(s32[1024]{0:T(1024)} %param.24) | copy-start | bytes 12292
  0.7 7.3 %copy-start.15 = (s32[1024]{0:T(1024)S(1)}, s32[1024]{0:T(1024)}, u32[]{:S(2)}) copy-start(s32[1024]{0:T(1024)} %param.25) | copy-start | bytes 12292
  2.2 8.0 %collective-permute-start = (bf16[96,512]{1,0:T(8,128)(2,1)S(1)}, bf16[96,512]{1,0:T(8,128)(2,1)S(1)}, u32[]{:S(2)}, u32[]{:S(2)}) collective-permute-start(bf16[96,512]{1,0:T(8,128)(2,1)S(1)} %get-tuple-element.33), channel_id=1, source_target_pairs={{32,64},{64,32},{96,128},{128,96},{160,192},{192,160},{224,256},{2... | collective-permute-start | bytes 294920 | tf_op jit(solution)/shard_map/ppermute | solution.py:275
  6.0 4.3 %collective-permute-start.1 = (bf16[96,512]{1,0:T(8,128)(2,1)S(1)}, bf16[96,512]{1,0:T(8,128)(2,1)S(1)}, u32[]{:S(2)}, u32[]{:S(2)}) collective-permute-start(bf16[96,512]{1,0:T(8,128)(2,1)S(1)} %get-tuple-element.34), channel_id=1, source_target_pairs={{0,32},{32,0},{64,96},{96,64},{128,160},{160,128},{192,224},{224,1... | collective-permute-start | bytes 294920 | tf_op jit(solution)/shard_map/ppermute | solution.py:276
  7.9 9.4 %copy-start.7 = (s32[512]{0:T(512)S(1)}, s32[512]{0:T(512)}, u32[]{:S(2)}) copy-start(s32[512]{0:T(512)} %param.27) | copy-start | bytes 6148
  10.3 9.7 %collective-permute-start.3 = (bf16[96,512]{1,0:T(8,128)(2,1)S(1)}, bf16[96,512]{1,0:T(8,128)(2,1)S(1)}, u32[]{:S(2)}, u32[]{:S(2)}) collective-permute-start(bf16[96,512]{1,0:T(8,128)(2,1)S(1)} %pad_maximum_fusion.1), channel_id=1, source_target_pairs={{1,2},{2,1},{3,4},{4,3},{5,6},{6,5},{7,8},{8,7},{9,10},{10,9},{11,... | collective-permute-start | bytes 294920 | tf_op jit(solution)/shard_map/ppermute | solution.py:283
  15.4 5.4 %collective-permute-start.2 = (bf16[96,512]{1,0:T(8,128)(2,1)S(1)}, bf16[96,512]{1,0:T(8,128)(2,1)S(1)}, u32[]{:S(2)}, u32[]{:S(2)}) collective-permute-start(bf16[96,512]{1,0:T(8,128)(2,1)S(1)} %pad_maximum_fusion), channel_id=1, source_target_pairs={{0,1},{1,0},{2,3},{3,2},{4,5},{5,4},{6,7},{7,6},{8,9},{9,8},{10,11... | collective-permute-start | bytes 294920 | tf_op jit(solution)/shard_map/ppermute | solution.py:282
  17.4 3.4 %copy-start.3 = (bf16[512,512]{1,0:T(8,128)(2,1)S(1)}, bf16[512,512]{1,0:T(8,128)(2,1)}, u32[]{:S(2)}) copy-start(bf16[512,512]{1,0:T(8,128)(2,1)} %w_out.1) | copy-start | bytes 1572868
  17.4 3.4 %copy-start.4 = (bf16[512,512]{1,0:T(8,128)(2,1)S(1)}, bf16[512,512]{1,0:T(8,128)(2,1)}, u32[]{:S(2)}) copy-start(bf16[512,512]{1,0:T(8,128)(2,1)} %w_node_out.1) | copy-start | bytes 1572868
  17.4 3.4 %copy-start.11 = (f32[512]{0:T(512)S(1)}, f32[512]{0:T(512)}, u32[]{:S(2)}) copy-start(f32[512]{0:T(512)} %param.32) | copy-start | bytes 6148
  17.4 3.4 %copy-start.12 = (f32[512]{0:T(512)S(1)}, f32[512]{0:T(512)}, u32[]{:S(2)}) copy-start(f32[512]{0:T(512)} %param.35) | copy-start | bytes 6148
  20.8 41.5 %copy-start.9 = (s32[1024]{0:T(1024)S(1)}, s32[1024]{0:T(1024)}, u32[]{:S(2)}) copy-start(s32[1024]{0:T(1024)} %param.28) | copy-start | bytes 12292
  20.8 41.5 %copy-start.10 = (s32[1024]{0:T(1024)S(1)}, s32[1024]{0:T(1024)}, u32[]{:S(2)}) copy-start(s32[1024]{0:T(1024)} %param.29) | copy-start | bytes 12292
  24.2 38.1 %copy-start = (bf16[1024,512]{1,0:T(8,128)(2,1)S(1)}, bf16[1024,512]{1,0:T(8,128)(2,1)}, u32[]{:S(2)}) copy-start(bf16[1024,512]{1,0:T(8,128)(2,1)} %w_cin.5) | copy-start | bytes 3145732
  58.8 10.4 %collective-permute-start.4 = (bf16[256,512]{1,0:T(8,128)(2,1)S(1)}, bf16[256,512]{1,0:T(8,128)(2,1)S(1)}, u32[]{:S(2)}, u32[]{:S(2)}) collective-permute-start(bf16[256,512]{1,0:T(8,128)(2,1)S(1)} %bitcast.12), channel_id=1, source_target_pairs={{0,1},{1,0},{2,3},{3,2},{4,5},{5,4},{6,7},{7,6},{8,9},{9,8},{10,11... | collective-permute-start | bytes 786440 | tf_op jit(solution)/shard_map/ppermute | solution.py:308
  69.3 3.4 %collective-permute-start.5 = (bf16[256,512]{1,0:T(8,128)(2,1)S(1)}, bf16[256,512]{1,0:T(8,128)(2,1)S(1)}, u32[]{:S(2)}, u32[]{:S(2)}) collective-permute-start(bf16[256,512]{1,0:T(8,128)(2,1)S(1)} %collective-permute-done.4.side), channel_id=1, source_target_pairs={{0,32},{32,0},{64,96},{96,64},{128,160},{160,128},{192,224},{224,1... | collective-permute-start | bytes 786440 | tf_op jit(solution)/shard_map/ppermute | solution.py:317
  71.4 1.3 %copy-start.5 = (bf16[512,512]{1,0:T(8,128)(2,1)S(1)}, bf16[512,512]{1,0:T(8,128)(2,1)}, u32[]{:S(2)}) copy-start(bf16[512,512]{1,0:T(8,128)(2,1)} %w_cout.1) | copy-start | bytes 1572868
  71.4 1.4 %copy-start.6 = (bf16[512,512]{1,0:T(8,128)(2,1)S(1)}, bf16[512,512]{1,0:T(8,128)(2,1)}, u32[]{:S(2)}) copy-start(bf16[512,512]{1,0:T(8,128)(2,1)} %w_nout.1) | copy-start | bytes 1572868
  71.4 1.3 %copy-start.13 = (f32[512]{0:T(512)S(1)}, f32[512]{0:T(512)}, u32[]{:S(2)}) copy-start(f32[512]{0:T(512)} %param.40) | copy-start | bytes 6148
  71.4 1.3 %copy-start.14 = (f32[512]{0:T(512)S(1)}, f32[512]{0:T(512)}, u32[]{:S(2)}) copy-start(f32[512]{0:T(512)} %param.43) | copy-start | bytes 6148

commit v6 on v5

--- a/solution.py
+++ b/solution.py
@@ -78,13 +78,12 @@
     near[...] = picked[160:256, :]
 
 
-def tables_kernel(nodes, src, dst, w_in, gathered, dst_spread):
+def tables_kernel(nodes, src, dst, w_in, gathered):
     nodes = nodes[...]
     src_proj = dot(nodes, w_in[512:1024, :]).astype(BF16)
     dst_proj = dot(nodes, w_in[1024:1536, :]).astype(BF16)
     part = dot(pick(as_column(src[...]), 512), src_proj)
     gathered[...] = part + dot(pick(as_column(dst[...]), 512), dst_proj)
-    dst_spread[...] = spread(as_row(dst[...]), 512)
 
 
 def halo_slots(src):
@@ -102,14 +101,15 @@
 
 
 def edges_kernel(
-    nodes, gathered, src, parents, edges_hbm, w_in_hbm, w_node_hbm,
-    pre, node_pre, edges, w_source, w_summed, halo_pick, owner_spread, w_in, w_node, sems,
+    nodes, gathered, src, dst, parents, edges_hbm, w_in_hbm, w_node_hbm,
+    pre, node_pre, edges, w_source, w_summed, halo_pick, owner_spread, dst_spread, w_in, w_node, sems,
 ):
     got = fetch(
         sems, (w_node_hbm.at[0:512], w_node), (w_in_hbm.at[0:512], w_in),
         (edges_hbm.at[0:512], edges.at[0:512]), (edges_hbm.at[512:1024], edges.at[512:1024]),
         (w_in_hbm.at[512:1024], w_source), (w_node_hbm.at[512:1024], w_summed),
     )
+    dst_spread[...] = spread(as_row(dst[...]), 512)
     halo_pick[...] = pick(as_column(halo_slots(src[...])), 256)
     owner_spread[...] = spread(as_row(parents[...]), COARSE)
     got[0].wait()
@@ -157,13 +157,16 @@
 
 
 def own_kernel(
-    zero, csrc, cdst, parents, level_one, edges, message, w_cin, w_nin_hbm, w_up_hbm,
-    pre, node_pre, up_pre, edges_hbm, first_pick, second_pick, dst_spread, owner_pick,
+    zero, csrc, cdst, parents, level_one, edges, message, w_cin, w_nin_hbm, w_up_hbm, w_up_out_hbm,
+    pre, node_pre, up_pre, edges_hbm, first_pick, second_pick, dst_spread, owner_pick, w_summed, w_lifted, w_up_out,
     w_nin, w_up, edges_out, sems,
 ):
-    got = fetch(sems, (w_nin_hbm.at[0:512], w_nin), (w_up_hbm.at[0:512], w_up))
+    got = fetch(
+        sems, (w_nin_hbm.at[0:512], w_nin), (w_up_hbm.at[0:512], w_up), (w_nin_hbm.at[512:1024], w_summed),
+        (w_up_hbm.at[512:1024], w_lifted), (w_up_out_hbm, w_up_out),
+    )
     edges_out[...] = (edges[...].astype(F32) + message[...]).astype(BF16)
-    sent = pltpu.make_async_copy(edges_out, edges_hbm, sems.at[2])
+    sent = pltpu.make_async_copy(edges_out, edges_hbm, sems.at[5])
     sent.start()
     zero = zero[...]
     side_src = dot(zero, w_cin[0:512, :]).astype(BF16)
@@ -179,6 +182,8 @@
     node_pre[...] = dot(zero, w_nin[...])
     got[1].wait()
     up_pre[...] = dot(level_one[...], w_up[...])
+    for copy in got[2:]:
+        copy.wait()
     sent.wait()
 
 
@@ -191,19 +196,16 @@
     return pick(as_column(csrc - jnp.where(right, 2 * COARSE, 0)), COARSE)
 
 
-def first_kernel(side, pre, first_pick, w_cin, w_nin_hbm, both, w_summed, sems):
-    (got,) = fetch(sems, (w_nin_hbm.at[512:1024], w_summed))
+def first_kernel(side, pre, first_pick, w_cin, both):
     side_src = dot(side[...], w_cin[0:512, :]).astype(BF16)
     both[...] = pre[...] + dot(first_pick[...], side_src)
-    got.wait()
 
 
 def coarse_kernel(
     side, zero, pre, node_pre, up_pre, second_pick, dst_spread, owner_pick, level_one,
-    w_cin, w_cout, w_summed, w_nout, coarse_gain, up_gain, w_up_hbm, w_up_out_hbm,
-    out_hbm, out, w_lifted, w_up_out, sems,
-):
-    got = fetch(sems, (w_up_hbm.at[512:1024], w_lifted), (w_up_out_hbm, w_up_out))
+    w_cin, w_cout, w_summed, w_nout, coarse_gain, w_lifted, w_up_out, up_gain,
+    out_hbm, out, sems,
+):
     side_src = dot(side[...], w_cin[0:512, :]).astype(BF16)
     part = pre[...] + dot(second_pick[...], side_src)
     message = layer_norm(dot(silu(part).astype(BF16), w_cout[...]))
@@ -211,9 +213,7 @@
     part = node_pre[...] + dot(summed, w_summed[...])
     one = (zero[...].astype(F32) + mlp_tail(part, w_nout[...], coarse_gain[...])).astype(BF16)
     lifted = dot(owner_pick[...], one).astype(BF16)
-    got[0].wait()
     part = up_pre[...] + dot(lifted, w_lifted[...])
-    got[1].wait()
     tail = mlp_tail(part, w_up_out[...], up_gain[...])
     out[...] = (level_one[...].astype(F32) + tail).astype(BF16)
     (sent,) = fetch(sems, (out, out_hbm))
@@ -274,25 +274,25 @@
     even_y, odd_y = trades(count_y)
     far = lax.ppermute(far, "gx", odd_x)
     near = lax.ppermute(near, "gx", even_x)
-    gathered, dst_spread = call(
-        tables_kernel, [((1024, 512), F32), ((512, 1024), BF16)], fine_nodes, src, dst, w_edge_in, held=(0, 1),
+    gathered = call(
+        tables_kernel, [((1024, 512), F32)], fine_nodes, src, dst, w_edge_in, held=(0,),
         flops=2 * 6 * 512**3, name="tables",
     )
     far, near, gathered = lax.optimization_barrier((far, near, gathered))
     side_a = lax.ppermute(jnp.concatenate([far[64:96], after, near[64:96]], 0), "gy", even_y)
     side_b = lax.ppermute(jnp.concatenate([far[0:32], before, near[0:32]], 0), "gy", odd_y)
     square = ((512, 512), BF16)
-    pre, node_pre, edges, w_source, w_summed, halo_pick, owner_spread = call(
+    pre, node_pre, edges, w_source, w_summed, halo_pick, owner_spread, edge_spread = call(
         edges_kernel,
         [((1024, 512), F32), ((512, 512), F32), ((1024, 512), BF16), square, square]
-        + [((1024, 256), BF16), ((COARSE, 512), BF16)],
-        fine_nodes, hold(gathered), src, owner, hbm=(fine_edges, w_edge_in, w_node_in), held=range(7),
+        + [((1024, 256), BF16), ((COARSE, 512), BF16), ((512, 1024), BF16)],
+        fine_nodes, hold(gathered), src, dst, owner, hbm=(fine_edges, w_edge_in, w_node_in), held=range(8),
         scratch=[block, block], copies=6, flops=2 * 3 * 512**3, name="edges",
     )
     message, level_one, pooled = call(
         after_halo_kernel, [((1024, 512), F32), square, ((COARSE, 512), BF16)],
         far, near, side_a, side_b, hold(pre), hold(node_pre), fine_nodes,
-        hold(halo_pick), hold(dst_spread), hold(owner_spread),
+        hold(halo_pick), hold(edge_spread), hold(owner_spread),
         hold(w_source), w_edge_out, edge_gain, hold(w_summed), w_node_out, node_gain,
         held=(0,), flops=2 * 8 * 512**3, name="after_halo",
     )
@@ -307,24 +307,24 @@
     ]
     first = lax.ppermute(zero, ("gx", "gy"), sideways)
     picks = [((1024, COARSE), BF16)] * 2 + [((COARSE, 1024), BF16), ((512, COARSE), BF16)]
-    pre, node_pre, up_pre, edges_out, first_pick, second_pick, dst_spread, owner_pick = call(
+    pre, node_pre, up_pre, edges_out, first_pick, second_pick, dst_spread, owner_pick, *late = call(
         own_kernel,
-        [((1024, 512), F32), ((COARSE, 512), F32), ((512, 512), F32), ((1024, 512), BF16)] + picks,
-        zero, csrc, cdst, owner, level_one, hold(edges), hold(message), w_cedge_in, hbm=(w_cnode_in, w_up_in),
-        held=(0, 1, 2, 4, 5, 6, 7), hbm_outs=(3,), scratch=[block, block, pltpu.VMEM((1024, 512), BF16)], copies=3, flops=2 * 5 * 512**3, name="own_column",
+        [((1024, 512), F32), ((COARSE, 512), F32), ((512, 512), F32), ((1024, 512), BF16)] + picks + [square] * 3,
+        zero, csrc, cdst, owner, level_one, hold(edges), hold(message), w_cedge_in, hbm=(w_cnode_in, w_up_in, w_up_out),
+        held=(0, 1, 2, *range(4, 11)), hbm_outs=(3,), scratch=[block, block, pltpu.VMEM((1024, 512), BF16)], copies=6, flops=2 * 5 * 512**3, name="own_column",
     )
     first, pre = lax.optimization_barrier((first, pre))
     second = lax.ppermute(first, "gx", even_x)
-    pre, w_summed = call(
-        first_kernel, [((1024, 512), F32), square], first, hold(pre), hold(first_pick), w_cedge_in,
-        hbm=(w_cnode_in,), held=(0, 1), copies=1, flops=2 * 2 * 512**3, name="first_side",
-    )
+    pre = call(
+        first_kernel, [((1024, 512), F32)], first, hold(pre), hold(first_pick), w_cedge_in, held=(0,),
+        flops=2 * 2 * 512**3, name="first_side",
+    )
+    w_summed, w_lifted, w_last = (hold(weight) for weight in late)
     fine_out = call(
         coarse_kernel, [square],
         second, zero, hold(pre), hold(node_pre), hold(up_pre), hold(second_pick), hold(dst_spread), hold(owner_pick),
-        level_one, w_cedge_in, w_cedge_out, hold(w_summed), w_cnode_out, coarse_gain, up_gain,
-        hbm=(w_up_in, w_up_out), hbm_outs=(0,), scratch=[block] * 3, copies=2,
-        flops=2 * 8 * 512**3, name="coarse",
+        level_one, w_cedge_in, w_cedge_out, w_summed, w_cnode_out, coarse_gain, w_lifted, w_last, up_gain,
+        hbm_outs=(0,), scratch=[block], copies=1, flops=2 * 8 * 512**3, name="coarse",
     )
     return fine_out, edges_out
 

time: 78.2 us -> 77.9 us (level)
  transfers between devices with their start and end apart: 6 -> 6, of which waited for: 3 -> 3; matrix products, arithmetic and copies ran while one was open for 0% -> 0% of each run, Pallas kernels for 12% -> 11%
where the time goes in v6:
time: 77.9 us; the launch traced here: 77.5 us
  blocking collectives  34.7 us (45%)
  Pallas kernels  18.5 us (24%)
  starting transfers between devices  18.3 us (23%)
  waiting for transfers between devices  4.81 us (6%)
  between operations  1.15 us (1%)
    all_to_all x1, blocking collectives, per_device(): parts = lax.all_to_all(pooled, 'gx', 0, 0, tiled=True)  20.3 us
    pallas_call x8, Pallas kernels, call(): pl.pallas_call(kernel, out_shape=shapes, in_specs=[vmem] * len(args) + [f...  18.5 us
    all_to_all x1, blocking collectives, per_device(): zero = lax.all_to_all(shares, 'gx', 0, 0, tiled=True).reshape(COARSE, 512)  14.4 us
    ppermute x1, starting transfers between devices, per_device(): lax.ppermute(jnp.concatenate([far[0:32], before, near[0:32]], 0), 'gy', o...  5.13 us
    ppermute x1, starting transfers between devices, per_device(): far = lax.ppermute(far, 'gx', odd_x)  3.77 us
    ppermute x1, waiting for transfers between devices, per_device(): first = lax.ppermute(zero, ('gx', 'gy'), sideways)  3.61 us
    ppermute x1, starting transfers between devices, per_device(): first = lax.ppermute(zero, ('gx', 'gy'), sideways)  3.48 us
    ppermute x1, starting transfers between devices, per_device(): second = lax.ppermute(first, 'gx', even_x)  2.09 us
  transfers between devices with their start and end apart: 6, of which 3 were waited for; matrix products, arithmetic and copies ran while one was open for 0% of the time, Pallas kernels for 11%

profile of v6, /device:TPU:199, one launch (start us, length us, event | category | flops | bytes accessed | tf_op | source)
XLA Modules:
  0.0 77.5 jit_solution(12618041442097434014)
XLA Ops:
  0.7 1.5 %outgoing.1 = (bf16[96,512]{1,0:T(8,128)(2,1)S(1)}, bf16[32,512]{1,0:T(8,128)(2,1)S(1)}, bf16[32,512]{1,0:T(8,128)(2,1)S(1)}, bf16[96,512]{1,0:T(8,128)(2,1)S(1)}) custom-call(bf16[512,512]{1,0:T(8,128)(2,1)} %nodes.5, s32[8,32]{1,0:T(8,128)} %bitcast.28), custom_call_target="tpu_custom_call" | custom-call | flops 13421772800 | bytes 525312 | tf_op jit(solution)/shard_map/outgoing/pallas_call | solution.py:237
  2.2 3.8 %collective-permute-start = (bf16[96,512]{1,0:T(8,128)(2,1)S(1)}, bf16[96,512]{1,0:T(8,128)(2,1)S(1)}, u32[]{:S(2)}, u32[]{:S(2)}) collective-permute-start(bf16[96,512]{1,0:T(8,128)(2,1)S(1)} %get-tuple-element.33), channel_id=1, source_target_pairs={{32,64},{64,32},{96,128},{128,96},{160,192},{192,160},{224,256},{2... | collective-permute-start | bytes 294920 | tf_op jit(solution)/shard_map/ppermute | solution.py:275
  6.0 1.9 %collective-permute-start.1 = (bf16[96,512]{1,0:T(8,128)(2,1)S(1)}, bf16[96,512]{1,0:T(8,128)(2,1)S(1)}, u32[]{:S(2)}, u32[]{:S(2)}) collective-permute-start(bf16[96,512]{1,0:T(8,128)(2,1)S(1)} %get-tuple-element.34), channel_id=1, source_target_pairs={{0,32},{32,0},{64,96},{96,64},{128,160},{160,128},{192,224},{224,1... | collective-permute-start | bytes 294920 | tf_op jit(solution)/shard_map/ppermute | solution.py:276
  7.9 0.0 copy-start.7
  8.0 1.9 %tables.1.gathered = f32[1024,512]{1,0:T(8,128)S(1)} custom-call(bf16[512,512]{1,0:T(8,128)(2,1)S(1)} %copy-done.1, s32[8,128]{1,0:T(8,128)S(1)} %bitcast.20, s32[8,128]{1,0:T(8,128)S(1)} %bitcast.22, bf16[1536,512]{1,0:T(8,128)(2,1)S(1)} %copy-done.2), custom_call_target="tpu_custom_call" | custom-call | flops 1610612736 | bytes 2105344 | tf_op jit(solution)/shard_map/tables/pallas_call | solution.py:237
  9.9 5.1 %collective-permute-start.3 = (bf16[96,512]{1,0:T(8,128)(2,1)S(1)}, bf16[96,512]{1,0:T(8,128)(2,1)S(1)}, u32[]{:S(2)}, u32[]{:S(2)}) collective-permute-start(bf16[96,512]{1,0:T(8,128)(2,1)S(1)} %pad_maximum_fusion.1), channel_id=1, source_target_pairs={{1,2},{2,1},{3,4},{4,3},{5,6},{6,5},{7,8},{8,7},{9,10},{10,9},{11,... | collective-permute-start | bytes 294920 | tf_op jit(solution)/shard_map/ppermute | solution.py:283
  15.1 1.9 %collective-permute-start.2 = (bf16[96,512]{1,0:T(8,128)(2,1)S(1)}, bf16[96,512]{1,0:T(8,128)(2,1)S(1)}, u32[]{:S(2)}, u32[]{:S(2)}) collective-permute-start(bf16[96,512]{1,0:T(8,128)(2,1)S(1)} %pad_maximum_fusion), channel_id=1, source_target_pairs={{0,1},{1,0},{2,3},{3,2},{4,5},{5,4},{6,7},{7,6},{8,9},{9,8},{10,11... | collective-permute-start | bytes 294920 | tf_op jit(solution)/shard_map/ppermute | solution.py:282
  17.0 0.0 copy-start.12
  17.1 0.0 copy-start.13
  17.1 2.7 %edges.1 = (f32[1024,512]{1,0:T(8,128)S(1)}, f32[512,512]{1,0:T(8,128)S(1)}, bf16[1024,512]{1,0:T(8,128)(2,1)S(1)}, bf16[512,512]{1,0:T(8,128)(2,1)S(1)}, bf16[5...) custom-call(bf16[512,512]{1,0:T(8,128)(2,1)S(1)} %copy-done.1, ...), custom_call_target="tpu_custom_call" | custom-call | flops 805306368 | bytes 6301696 | tf_op jit(solution)/shard_map/edges/pallas_call | solution.py:237
  19.8 0.6 collective-permute-done.2.side_a
  20.5 0.0 copy-start.9
  20.5 3.4 %after_halo.1 = (f32[1024,512]{1,0:T(8,128)S(1)}, bf16[512,512]{1,0:T(8,128)(2,1)S(1)}, bf16[256,512]{1,0:T(8,128)(2,1)S(1)}) custom-call(bf16[96,512]{1,0:T(8,128)(2,1)S(1)} %collective-permute-done.far, bf16[96,512]{1,0:T(8,128)(2,1)S(1)} %collective-permute-done.1.near, bf16[96,512]{1,0:T(8,128)(2,1)S(1)} %collective-permute-done.2.side_a, ...), custom_call_target="tpu_custom_call" | custom-call | flops 2147483648 | bytes 7999488 | tf_op jit(solution)/shard_map/after_halo/pallas_call | solution.py:237
  23.9 0.0 copy-start
  23.9 20.3 %all_to_all.14.parts = bf16[16,16,512]{2,1,0:T(8,128)(2,1)S(1)} all-to-all(bf16[16,16,512]{2,1,0:T(8,128)(2,1)S(1)} %bitcast.15), channel_id=1, replica_groups=mesh['gx'=16,'gy'=32] {'gx'}, dimensions={0} | all-to-all | bytes 524288 | tf_op jit(solution)/shard_map/all_to_all | solution.py:299
  44.2 0.2 share.1
  44.4 14.4 %all_to_all.15 = bf16[16,16,512]{2,1,0:T(8,128)(2,1)S(1)} all-to-all(bf16[16,16,512]{2,1,0:T(8,128)(2,1)S(1)} %share.1), channel_id=1, replica_groups=mesh['gx'=16,'gy'=32] {'gx'}, dimensions={0} | all-to-all | bytes 524288 | tf_op jit(solution)/shard_map/all_to_all | solution.py:304
  58.8 3.5 %collective-permute-start.4 = (bf16[256,512]{1,0:T(8,128)(2,1)S(1)}, bf16[256,512]{1,0:T(8,128)(2,1)S(1)}, u32[]{:S(2)}, u32[]{:S(2)}) collective-permute-start(bf16[256,512]{1,0:T(8,128)(2,1)S(1)} %bitcast.12), channel_id=1, source_target_pairs={{0,1},{1,0},{2,3},{3,2},{4,5},{5,4},{6,7},{7,6},{8,9},{9,8},{10,11... | collective-permute-start | bytes 786440 | tf_op jit(solution)/shard_map/ppermute | solution.py:308
  62.4 3.3 %own_column.1 = (f32[1024,512]{1,0:T(8,128)S(1)}, f32[256,512]{1,0:T(8,128)S(1)}, f32[512,512]{1,0:T(8,128)S(1)}, bf16[1024,512]{1,0:T(8,128)(2,1)}, bf16[1024,2...) custom-call(bf16[256,512]{1,0:T(8,128)(2,1)S(1)} %bitcast.13, ...), custom_call_target="tpu_custom_call" | custom-call | flops 1342177280 | bytes 7612416 | tf_op jit(solution)/shard_map/own_column/pallas_call | solution.py:237
  65.7 3.6 %collective-permute-done.4.side = bf16[256,512]{1,0:T(8,128)(2,1)S(1)} collective-permute-done((bf16[256,512]{1,0:T(8,128)(2,1)S(1)}, bf16[256,512]{1,0:T(8,128)(2,1)S(1)}, u32[]{:S(2)}, u32[]{:S(2)}) %collective-permute-start.4) | collective-permute-done | bytes 262176 | tf_op jit(solution)/shard_map/ppermute | solution.py:308
  69.3 2.1 %collective-permute-start.5 = (bf16[256,512]{1,0:T(8,128)(2,1)S(1)}, bf16[256,512]{1,0:T(8,128)(2,1)S(1)}, u32[]{:S(2)}, u32[]{:S(2)}) collective-permute-start(bf16[256,512]{1,0:T(8,128)(2,1)S(1)} %collective-permute-done.4.side), channel_id=1, source_target_pairs={{0,32},{32,0},{64,96},{96,64},{128,160},{160,128},{192,224},{224,1... | collective-permute-start | bytes 786440 | tf_op jit(solution)/shard_map/ppermute | solution.py:317
  71.4 0.7 first_side.1.pre
  72.1 0.6 collective-permute-done.5.side
  72.7 4.7 %coarse.1 = bf16[512,512]{1,0:T(8,128)(2,1)} custom-call(bf16[256,512]{1,0:T(8,128)(2,1)S(1)} %collective-permute-done.5.side, bf16[256,512]{1,0:T(8,128)(2,1)S(1)} %bitcast.14, f32[1024,512]{1,0:T(8,128)S(1)} %first_side.1.pre, f32[256,512]{1,0:T(8,128)S(1)} %get-tuple-element.55.node_pre, f32[512,512]{1,0:T(8,128)S(1)} %get-tuple-element.56.up_pre, ...), custom_call_target="tpu_custom_call" | custom-call | flops 2147483648 | bytes 9703424 | tf_op jit(solution)/shard_map/coarse/pallas_call | solution.py:237
  (33 shorter events, 0.1 us)
Async XLA Ops:
  0.6 7.3 %copy-start.1 = (bf16[512,512]{1,0:T(8,128)(2,1)S(1)}, bf16[512,512]{1,0:T(8,128)(2,1)}, u32[]{:S(2)}) copy-start(bf16[512,512]{1,0:T(8,128)(2,1)} %nodes.5) | copy-start | bytes 1572868
  0.6 7.3 %copy-start.2 = (bf16[1536,512]{1,0:T(8,128)(2,1)S(1)}, bf16[1536,512]{1,0:T(8,128)(2,1)}, u32[]{:S(2)}) copy-start(bf16[1536,512]{1,0:T(8,128)(2,1)} %w_in_hbm.1) | copy-start | bytes 4718596
  0.7 7.3 %copy-start.10 = (s32[1024]{0:T(1024)S(1)}, s32[1024]{0:T(1024)}, u32[]{:S(2)}) copy-start(s32[1024]{0:T(1024)} %param.24) | copy-start | bytes 12292
  0.7 7.3 %copy-start.11 = (s32[1024]{0:T(1024)S(1)}, s32[1024]{0:T(1024)}, u32[]{:S(2)}) copy-start(s32[1024]{0:T(1024)} %param.25) | copy-start | bytes 12292
  2.2 7.7 %collective-permute-start = (bf16[96,512]{1,0:T(8,128)(2,1)S(1)}, bf16[96,512]{1,0:T(8,128)(2,1)S(1)}, u32[]{:S(2)}, u32[]{:S(2)}) collective-permute-start(bf16[96,512]{1,0:T(8,128)(2,1)S(1)} %get-tuple-element.33), channel_id=1, source_target_pairs={{32,64},{64,32},{96,128},{128,96},{160,192},{192,160},{224,256},{2... | collective-permute-start | bytes 294920 | tf_op jit(solution)/shard_map/ppermute | solution.py:275
  6.0 3.9 %collective-permute-start.1 = (bf16[96,512]{1,0:T(8,128)(2,1)S(1)}, bf16[96,512]{1,0:T(8,128)(2,1)S(1)}, u32[]{:S(2)}, u32[]{:S(2)}) collective-permute-start(bf16[96,512]{1,0:T(8,128)(2,1)S(1)} %get-tuple-element.34), channel_id=1, source_target_pairs={{0,32},{32,0},{64,96},{96,64},{128,160},{160,128},{192,224},{224,1... | collective-permute-start | bytes 294920 | tf_op jit(solution)/shard_map/ppermute | solution.py:276
  7.9 9.1 %copy-start.7 = (s32[512]{0:T(512)S(1)}, s32[512]{0:T(512)}, u32[]{:S(2)}) copy-start(s32[512]{0:T(512)} %param.27) | copy-start | bytes 6148
  9.9 9.9 %collective-permute-start.3 = (bf16[96,512]{1,0:T(8,128)(2,1)S(1)}, bf16[96,512]{1,0:T(8,128)(2,1)S(1)}, u32[]{:S(2)}, u32[]{:S(2)}) collective-permute-start(bf16[96,512]{1,0:T(8,128)(2,1)S(1)} %pad_maximum_fusion.1), channel_id=1, source_target_pairs={{1,2},{2,1},{3,4},{4,3},{5,6},{6,5},{7,8},{8,7},{9,10},{10,9},{11,... | collective-permute-start | bytes 294920 | tf_op jit(solution)/shard_map/ppermute | solution.py:283
  15.1 5.4 %collective-permute-start.2 = (bf16[96,512]{1,0:T(8,128)(2,1)S(1)}, bf16[96,512]{1,0:T(8,128)(2,1)S(1)}, u32[]{:S(2)}, u32[]{:S(2)}) collective-permute-start(bf16[96,512]{1,0:T(8,128)(2,1)S(1)} %pad_maximum_fusion), channel_id=1, source_target_pairs={{0,1},{1,0},{2,3},{3,2},{4,5},{5,4},{6,7},{7,6},{8,9},{9,8},{10,11... | collective-permute-start | bytes 294920 | tf_op jit(solution)/shard_map/ppermute | solution.py:282
  17.0 3.4 %copy-start.3 = (bf16[512,512]{1,0:T(8,128)(2,1)S(1)}, bf16[512,512]{1,0:T(8,128)(2,1)}, u32[]{:S(2)}) copy-start(bf16[512,512]{1,0:T(8,128)(2,1)} %w_out.1) | copy-start | bytes 1572868
  17.0 3.4 %copy-start.4 = (bf16[512,512]{1,0:T(8,128)(2,1)S(1)}, bf16[512,512]{1,0:T(8,128)(2,1)}, u32[]{:S(2)}) copy-start(bf16[512,512]{1,0:T(8,128)(2,1)} %w_node_out.1) | copy-start | bytes 1572868
  17.0 3.4 %copy-start.12 = (f32[512]{0:T(512)S(1)}, f32[512]{0:T(512)}, u32[]{:S(2)}) copy-start(f32[512]{0:T(512)} %param.32) | copy-start | bytes 6148
  17.1 3.4 %copy-start.13 = (f32[512]{0:T(512)S(1)}, f32[512]{0:T(512)}, u32[]{:S(2)}) copy-start(f32[512]{0:T(512)} %param.35) | copy-start | bytes 6148
  20.5 41.9 %copy-start.8 = (s32[1024]{0:T(1024)S(1)}, s32[1024]{0:T(1024)}, u32[]{:S(2)}) copy-start(s32[1024]{0:T(1024)} %param.28) | copy-start | bytes 12292
  20.5 41.9 %copy-start.9 = (s32[1024]{0:T(1024)S(1)}, s32[1024]{0:T(1024)}, u32[]{:S(2)}) copy-start(s32[1024]{0:T(1024)} %param.29) | copy-start | bytes 12292
  23.9 38.4 %copy-start = (bf16[1024,512]{1,0:T(8,128)(2,1)S(1)}, bf16[1024,512]{1,0:T(8,128)(2,1)}, u32[]{:S(2)}) copy-start(bf16[1024,512]{1,0:T(8,128)(2,1)} %w_cin.5) | copy-start | bytes 3145732
  58.8 10.4 %collective-permute-start.4 = (bf16[256,512]{1,0:T(8,128)(2,1)S(1)}, bf16[256,512]{1,0:T(8,128)(2,1)S(1)}, u32[]{:S(2)}, u32[]{:S(2)}) collective-permute-start(bf16[256,512]{1,0:T(8,128)(2,1)S(1)} %bitcast.12), channel_id=1, source_target_pairs={{0,1},{1,0},{2,3},{3,2},{4,5},{5,4},{6,7},{7,6},{8,9},{9,8},{10,11... | collective-permute-start | bytes 786440 | tf_op jit(solution)/shard_map/ppermute | solution.py:308
  69.3 3.4 %collective-permute-start.5 = (bf16[256,512]{1,0:T(8,128)(2,1)S(1)}, bf16[256,512]{1,0:T(8,128)(2,1)S(1)}, u32[]{:S(2)}, u32[]{:S(2)}) collective-permute-start(bf16[256,512]{1,0:T(8,128)(2,1)S(1)} %collective-permute-done.4.side), channel_id=1, source_target_pairs={{0,32},{32,0},{64,96},{96,64},{128,160},{160,128},{192,224},{224,1... | collective-permute-start | bytes 786440 | tf_op jit(solution)/shard_map/ppermute | solution.py:317
  71.4 1.3 %copy-start.5 = (bf16[512,512]{1,0:T(8,128)(2,1)S(1)}, bf16[512,512]{1,0:T(8,128)(2,1)}, u32[]{:S(2)}) copy-start(bf16[512,512]{1,0:T(8,128)(2,1)} %w_cout.1) | copy-start | bytes 1572868
  71.4 1.3 %copy-start.6 = (bf16[512,512]{1,0:T(8,128)(2,1)S(1)}, bf16[512,512]{1,0:T(8,128)(2,1)}, u32[]{:S(2)}) copy-start(bf16[512,512]{1,0:T(8,128)(2,1)} %w_nout.1) | copy-start | bytes 1572868
  71.4 1.3 %copy-start.14 = (f32[512]{0:T(512)S(1)}, f32[512]{0:T(512)}, u32[]{:S(2)}) copy-start(f32[512]{0:T(512)} %param.40) | copy-start | bytes 6148
  71.4 1.3 %copy-start.15 = (f32[512]{0:T(512)S(1)}, f32[512]{0:T(512)}, u32[]{:S(2)}) copy-start(f32[512]{0:T(512)} %param.43) | copy-start | bytes 6148
